TPU v7x, 32 devices: a whole 2x2x4 slice. The times are simulated.
32 devices in a mesh: tok: 8 (over z, core), ten: 4 (over y, x).
Axes of the slice: x: 2, y: 2, z: 4, core: 2. Of those that a mesh axis runs over, the one named last changes fastest.
Arguments:
- counts: int32 [1024, 128256], P('ten', 'tok'), may hold values from 0 to 31
- u_factor: float32 [64, 1024], P('tok', 'ten'), may hold values from -2.5 to 2.5
- u_accum: float32 [64, 1024], P('tok', 'ten'), may hold values from 8016 to 513024
- v_factor: float32 [64, 128256], P('ten', 'tok'), may hold values from -2.5 to 2.5
- v_accum: float32 [64, 128256], P('ten', 'tok'), may hold values from 64 to 4096
Outputs:
- u_next: float32 [64, 1024], P('tok', 'ten')
- u_accum_next: float32 [64, 1024], P('tok', 'ten')
- v_next: float32 [64, 128256], P('ten', 'tok')
- v_accum_next: float32 [64, 128256], P('ten', 'tok')
All inputs are finite; a program needn't handle non-finite values.
Results may differ from a plain program's by a relative error of at most 0.0076.
Values may be sent and summed in bfloat16 or wider, within the bound.
No kernel may reach another device: no remote copies, remote signals or barrier semaphores. Data moves between devices by JAX's collectives and lax.ppermute only.
A program may use at most 64 MiB of HBM per device.

v0:
```python
import jax
import jax.numpy as jnp
from jax import lax
from jax.sharding import PartitionSpec as P

weight_scale = 0.5
step_rate = 0.3


def residual(low_tile, v_tile, counts):
    logits = lax.dot_general(
        low_tile, v_tile, (((0,), (0,)), ((), ())), preferred_element_type=jnp.float32
    )
    weighted = weight_scale * counts.astype(jnp.float32)
    return (weighted - (1.0 + weighted) * jax.nn.sigmoid(logits)).astype(jnp.bfloat16)


def gather_tenant(low_rows):
    return lax.all_gather(low_rows, "tok", axis=0, tiled=True)


def shards(counts, u_factor, u_accum, v_factor, v_accum):
    v_tile = lax.all_gather(v_factor.astype(jnp.bfloat16), "ten", axis=0, tiled=True)
    u_tile = gather_tenant(u_factor.astype(jnp.bfloat16))
    resid = residual(u_tile, v_tile, counts)
    grad_u = lax.psum_scatter(
        lax.dot_general(
            v_tile, resid, (((1,), (1,)), ((), ())), preferred_element_type=jnp.float32
        ),
        "tok",
        scatter_dimension=0,
        tiled=True,
    )
    u_accum_next = u_accum + grad_u * grad_u
    u_next = u_factor + step_rate * grad_u / jnp.sqrt(u_accum_next)
    u_fresh = gather_tenant(u_next.astype(jnp.bfloat16))
    resid_fresh = residual(u_fresh, v_tile, counts)
    grad_v = lax.psum_scatter(
        jnp.dot(u_fresh, resid_fresh, preferred_element_type=jnp.float32),
        "ten",
        scatter_dimension=0,
        tiled=True,
    )
    v_accum_next = v_accum + grad_v * grad_v
    v_next = v_factor + step_rate * grad_v / jnp.sqrt(v_accum_next)
    return (u_next, u_accum_next, v_next, v_accum_next)


def solution(mesh):
    return jax.shard_map(
        shards,
        mesh=mesh,
        in_specs=(
            P("ten", "tok"),
            P("tok", "ten"),
            P("tok", "ten"),
            P("ten", "tok"),
            P("ten", "tok"),
        ),
        out_specs=(P("tok", "ten"), P("tok", "ten"), P("ten", "tok"), P("ten", "tok")),
        check_vma=False,
    )
```

profile of v0, /device:TPU:0, one launch (start us, length us, event | category | flops | bytes accessed | tf_op | source)
XLA Modules:
  0.0 178.9 jit_solution(14522150623463380587)
XLA Ops:
  7.2 0.0 all-gather.2.cloned.1.call-start
  7.2 2.1 %convert_element_type.21 = bf16[16,16032]{1,0:T(8,128)(2,1)} convert(f32[16,16032]{1,0:T(8,128)} %param.8) | non-fusion elementwise | flops 256512 | bytes 1539072 | tf_op jit(solution)/shard_map/convert_element_type | solution.py:23
  9.3 0.0 all-gather.2.cloned.1.call-update
  9.3 0.0 reduce-scatter.3.cloned.1.call-start
  9.3 0.7 convert_element_type.20
  10.0 15.7 %all_gather.9 = bf16[64,256]{1,0:T(8,128)(2,1)S(1)} all-gather(bf16[8,256]{1,0:T(8,128)(2,1)S(1)} %convert_element_type.20), channel_id=1, replica_groups=mesh['tok'=8,'ten'=4] {'tok'}, dimensions={0}, use_global_device_ids=true | all-gather | bytes 36864 | tf_op jit(solution)/shard_map/all_gather | solution.py:19
  25.7 0.0 copy-start.2
  25.7 0.0 copy-start.3
  25.7 22.5 %all-gather.2.cloned.1.call-done = bf16[64,16032]{1,0:T(8,128)(2,1)} async-done(((bf16[16,16032]{1,0:T(8,128)(2,1)}), bf16[64,16032]{1,0:T(8,128)(2,1)}) %all-gather.2.cloned.1.call-update) | async-done | bytes 2052112 | tf_op jit(solution)/shard_map/all_gather | solution.py:23
  48.2 14.0 %convolution_bitcast_fusion = f32[64,256]{1,0:T(8,128)} fusion(bf16[64,16032]{1,0:T(8,128)(2,1)} %all-gather.2.cloned.1.call-done, bf16[64,256]{1,0:T(8,128)(2,1)S(1)} %all_gather.9, s32[256,16032]{0,1:T(8,128)} %param.5), kind=kOutput, calls=%fused_computation.16 | convolution fusion | flops 1087610880 | bytes 18567168 | tf_op jit(solution)/shard_map/dot_general | solution.py:27
  62.2 0.0 reduce-scatter.3.cloned.1.call-update
  62.2 0.0 reduce-scatter.5.cloned.1.call-start
  62.3 30.1 %reduce-scatter.3.cloned.1.call-done = f32[8,256]{1,0:T(8,128)} async-done(((f32[64,256]{1,0:T(8,128)}), f32[8,256]{1,0:T(8,128)}) %reduce-scatter.3.cloned.1.call-update) | async-done | bytes 8208 | tf_op jit(solution)/shard_map/reduce_scatter | solution.py:26
  92.4 0.0 copy-done.2
  92.4 0.0 copy-done.3
  92.4 1.3 fusion.17
  93.7 14.0 %all_gather.11 = bf16[64,256]{1,0:T(8,128)(2,1)S(1)} all-gather(bf16[8,256]{1,0:T(8,128)(2,1)S(1)} %get-tuple-element.6), channel_id=1, replica_groups=mesh['tok'=8,'ten'=4] {'tok'}, dimensions={0}, use_global_device_ids=true | all-gather | bytes 36864 | tf_op jit(solution)/shard_map/all_gather | solution.py:19
  107.7 0.0 copy-start
  107.7 0.0 copy-start.1
  107.7 11.4 %fusion.12 = f32[64,16032]{1,0:T(8,128)} fusion(bf16[64,256]{1,0:T(8,128)(2,1)S(1)} %all_gather.11, bf16[64,16032]{1,0:T(8,128)(2,1)} %all-gather.2.cloned.1.call-done, s32[256,16032]{0,1:T(8,128)} %param.5), kind=kOutput, calls=%fused_computation.15 | convolution fusion | flops 1087610880 | bytes 22605824 | tf_op jit(solution)/shard_map/dot_general | solution.py:39
  119.1 0.0 reduce-scatter.5.cloned.1.call-update
  119.1 50.5 %reduce-scatter.5.cloned.1.call-done = f32[16,16032]{1,0:T(8,128)} async-done(((f32[64,16032]{1,0:T(8,128)}), f32[16,16032]{1,0:T(8,128)}) %reduce-scatter.5.cloned.1.call-update) | async-done | bytes 1026064 | tf_op jit(solution)/shard_map/reduce_scatter | solution.py:38
  169.6 0.0 copy-done
  169.6 0.0 copy-done.1
  169.6 2.7 %multiply_add_fusion = (f32[16,16032]{1,0:T(8,128)}, f32[16,16032]{1,0:T(8,128)}) fusion(f32[16,16032]{1,0:T(8,128)S(1)} %copy-done, f32[16,16032]{1,0:T(8,128)} %reduce-scatter.5.cloned.1.call-done, f32[16,16032]{1,0:T(8,128)S(1)} %copy-done.1), kind=kLoop, calls=%fused_computation.17 | loop fusion | flops 1282560 | bytes 5130240 | tf_op jit(solution)/shard_map/add | solution.py:45
Async XLA Ops:
  7.2 41.0 %all-gather.2.cloned.1.call-start = ((), (), s32[]{:S(2)}) async-start(), calls=%async_computation.2 | async-start | bytes 2580480 | tf_op jit(solution)/shard_map/all_gather | solution.py:23
  9.3 83.1 %reduce-scatter.3.cloned.1.call-start = ((), (), s32[]{:S(2)}) async-start(), calls=%async_computation.3 | async-start | bytes 73728 | tf_op jit(solution)/shard_map/reduce_scatter | solution.py:26
  25.7 66.7 %copy-start.2 = (f32[8,256]{1,0:T(8,128)S(1)}, f32[8,256]{1,0:T(8,128)}, u32[]{:S(2)}) copy-start(f32[8,256]{1,0:T(8,128)} %param.6) | copy-start | bytes 24580
  25.7 66.7 %copy-start.3 = (f32[8,256]{1,0:T(8,128)S(1)}, f32[8,256]{1,0:T(8,128)}, u32[]{:S(2)}) copy-start(f32[8,256]{1,0:T(8,128)} %param.7) | copy-start | bytes 24580
  62.2 107.4 %reduce-scatter.5.cloned.1.call-start = ((), (), s32[]{:S(2)}) async-start(), calls=%async_computation.4 | async-start | bytes 5160960 | tf_op jit(solution)/shard_map/reduce_scatter | solution.py:38
  107.7 61.9 %copy-start = (f32[16,16032]{1,0:T(8,128)S(1)}, f32[16,16032]{1,0:T(8,128)}, u32[]{:S(2)}) copy-start(f32[16,16032]{1,0:T(8,128)} %param.8) | copy-start | bytes 3078148
  107.7 61.9 %copy-start.1 = (f32[16,16032]{1,0:T(8,128)S(1)}, f32[16,16032]{1,0:T(8,128)}, u32[]{:S(2)}) copy-start(f32[16,16032]{1,0:T(8,128)} %param.9) | copy-start | bytes 3078148
Sparse Core Ops, SparseCore 0:
  10.4 37.7 all-gather.1
  62.3 30.0 reduce-scatter.2
  119.3 50.2 reduce-scatter.4
where the time goes:
time: 179 us
  waiting for transfers between devices  103 us (58%)
  blocking collectives  29.7 us (17%)
  matrix products  25.4 us (14%)
  between operations  13.8 us (8%)
  other arithmetic  6.78 us (4%)
    reduce_scatter x1, waiting for transfers between devices, shards(): lax.psum_scatter(jnp.dot(u_fresh, resid_fresh, preferred_element_type=jnp...  50.5 us
    reduce_scatter x1, waiting for transfers between devices, shards(): lax.psum_scatter(lax.dot_general(v_tile, resid, (((1,), (1,)), ((), ())),...  30.1 us
    all_gather x2, blocking collectives, gather_tenant(): return lax.all_gather(low_rows, 'tok', axis=0, tiled=True)  29.7 us
    all_gather x1, waiting for transfers between devices, shards(): lax.all_gather(v_factor.astype(jnp.bfloat16), 'ten', axis=0, tiled=True)  22.5 us
    dot_general x1, matrix products, shards(): lax.dot_general(v_tile, resid, (((1,), (1,)), ((), ())), preferred_elemen...  14 us
    dot_general x1, matrix products, shards(): jnp.dot(u_fresh, resid_fresh, preferred_element_type=jnp.float32)  11.4 us
  transfers between devices with their start and end apart: 3, of which 3 were waited for; matrix products, arithmetic and copies ran while one was open for 0% of the time, Pallas kernels for 0%

commit v1 on v0

--- a/solution.py
+++ b/solution.py
@@ -1,10 +1,19 @@
 import jax
 import jax.numpy as jnp
 from jax import lax
+from jax.experimental import pallas as pl
+from jax.experimental.pallas import tpu as pltpu
 from jax.sharding import PartitionSpec as P
 
 weight_scale = 0.5
 step_rate = 0.3
+LANES = 128
+CHUNK = 6144
+INNER = 1024
+VMEM_LIMIT = 30 * 2**20
+
+whole = pl.BlockSpec(memory_space=pltpu.VMEM)
+scalars = pl.BlockSpec(memory_space=pltpu.SMEM)
 
 
 def residual(low_tile, v_tile, counts):
@@ -19,7 +28,7 @@
     return lax.all_gather(low_rows, "tok", axis=0, tiled=True)
 
 
-def shards(counts, u_factor, u_accum, v_factor, v_accum):
+def shards_any(counts, u_factor, u_accum, v_factor, v_accum):
     v_tile = lax.all_gather(v_factor.astype(jnp.bfloat16), "ten", axis=0, tiled=True)
     u_tile = gather_tenant(u_factor.astype(jnp.bfloat16))
     resid = residual(u_tile, v_tile, counts)
@@ -46,17 +55,275 @@
     return (u_next, u_accum_next, v_next, v_accum_next)
 
 
+def swap(a, axis, bit, size):
+    return lax.ppermute(a, axis, [(i, i ^ bit) for i in range(size)])
+
+
+def call(kernel, out_shape, operands, in_specs, flops=0, moved=0, **options):
+    return pl.pallas_call(
+        kernel,
+        out_shape=out_shape,
+        in_specs=in_specs,
+        compiler_params=pltpu.CompilerParams(vmem_limit_bytes=VMEM_LIMIT),
+        cost_estimate=pl.CostEstimate(
+            flops=flops, bytes_accessed=moved, transcendentals=0
+        ),
+        **options,
+    )(*operands)
+
+
+def order_tenant(place, gathered):
+    def kernel(place_ref, all_ref, factor_ref, accum_ref, half_ref):
+        for j in range(4):
+            for h in range(2):
+                source = (2 * (place_ref[1] ^ j) + h) ^ place_ref[0]
+                rows = pl.ds(16 * j + 8 * h, 8)
+                factor_ref[rows, :] = all_ref[source, :8, :]
+                accum_ref[rows, :] = all_ref[source, 8:, :]
+        half_ref[...] = (factor_ref[...].astype(jnp.bfloat16).astype(jnp.float32) * 0.5).astype(
+            jnp.bfloat16
+        )
+
+    width = gathered.shape[2]
+    return call(
+        kernel,
+        (
+            jax.ShapeDtypeStruct((64, width), jnp.float32),
+            jax.ShapeDtypeStruct((64, width), jnp.float32),
+            jax.ShapeDtypeStruct((64, width), jnp.bfloat16),
+        ),
+        (place, gathered),
+        [scalars, whole],
+        out_specs=(whole, whole, whole),
+    )
+
+
+def update_tenant(place, mine, other, factor, accum):
+    def kernel(place_ref, a_ref, b_ref, factor_ref, accum_ref, low_ref, half_ref, next_ref, sums_ref, full_ref, tot_ref):
+        grad = a_ref[...] + b_ref[...]
+        total = accum_ref[...] + grad * grad
+        fresh = factor_ref[...] + step_rate * grad * lax.rsqrt(total)
+        full_ref[...] = fresh
+        tot_ref[...] = total
+        low = fresh.astype(jnp.bfloat16)
+        low_ref[...] = low
+        half_ref[...] = (low.astype(jnp.float32) * 0.5).astype(jnp.bfloat16)
+        row = ((place_ref[0] // 2) ^ place_ref[1]) * 16 + (place_ref[0] % 2) * 8
+        rows = pl.ds(pl.multiple_of(row, 8), 8)
+        next_ref[...] = full_ref[rows, :]
+        sums_ref[...] = tot_ref[rows, :]
+
+    width = mine.shape[1]
+    return call(
+        kernel,
+        (
+            jax.ShapeDtypeStruct((64, width), jnp.bfloat16),
+            jax.ShapeDtypeStruct((64, width), jnp.bfloat16),
+            jax.ShapeDtypeStruct((8, width), jnp.float32),
+            jax.ShapeDtypeStruct((8, width), jnp.float32),
+        ),
+        (place, mine, other, factor, accum),
+        [scalars, whole, whole, whole, whole],
+        out_specs=(whole,) * 4,
+        scratch_shapes=[pltpu.VMEM((64, width), jnp.float32)] * 2,
+    )
+
+
+def pieces(start, size, tokens):
+    found = []
+    half = size // 2
+    for side in range(2):
+        for at in range(side * half, (side + 1) * half, INNER):
+            length = min(INNER, (side + 1) * half - at)
+            valid = max(0, min(length, tokens - start - at))
+            found.append((side, at, length, valid))
+    return found
+
+
+def fresh_residual(half_low, v, counts_ref, row, valid):
+    logits = lax.dot_general(
+        v, half_low, (((0,), (0,)), ((), ())), preferred_element_type=jnp.float32
+    )[:valid]
+    bend = jnp.tanh(logits)
+    lift = counts_ref[row : row + valid, :].astype(jnp.float32) * 0.25 + 0.5
+    resid = (lift - lift * bend - 1.0).astype(jnp.bfloat16)
+    if valid < v.shape[1]:
+        pad = jnp.zeros((v.shape[1] - valid, resid.shape[1]), jnp.bfloat16)
+        resid = jnp.concatenate([resid, pad], axis=0)
+    return resid
+
+
+def tenant_grad(start, size, half_low, blocks, counts, total):
+    tokens, width = counts.shape
+
+    def kernel(half_ref, own, x, y, d0, d1, counts_ref, *rest):
+        out_ref = rest[-1]
+        half = size // 2
+        grad = rest[0][...] if len(rest) == 2 else jnp.zeros(out_ref.shape, jnp.float32)
+        for side, at, length, valid in pieces(start, size, tokens):
+            if valid == 0:
+                continue
+            diag = (d0, d1)[side][:, at - side * half : at - side * half + length]
+            v = jnp.concatenate([r[:, at : at + length] for r in (own, x, y)] + [diag], axis=0)
+            resid = fresh_residual(half_ref[...], v, counts_ref, start + at, valid)
+            grad += jnp.dot(v, resid, preferred_element_type=jnp.float32)
+        out_ref[...] = grad
+
+    extra = () if total is None else (total,)
+    return call(
+        kernel,
+        jax.ShapeDtypeStruct((64, width), jnp.float32),
+        (half_low, *blocks, counts) + extra,
+        [whole] * (7 + len(extra)),
+        flops=4 * 64 * width * size,
+        moved=4 * width * size,
+        out_specs=whole,
+    )
+
+
+def token_grad(start, size, low, half_low, blocks, counts):
+    tokens, width = counts.shape
+    half = size // 2
+
+    def kernel(low_ref, half_ref, own, x, y, d0, d1, counts_ref, mine, sx, kx, sy, ky):
+        for side, at, length, valid in pieces(start, size, tokens):
+            lo = at - side * half
+            diag = (d0, d1)[side][:, lo : lo + length]
+            v = jnp.concatenate([r[:, at : at + length] for r in (own, x, y)] + [diag], axis=0)
+            if valid == 0:
+                grad = jnp.zeros((64, length), jnp.float32)
+            else:
+                resid = fresh_residual(half_ref[...], v, counts_ref, start + at, valid)
+                grad = lax.dot_general(
+                    low_ref[...], resid, (((1,), (1,)), ((), ())), preferred_element_type=jnp.float32
+                )
+            mine[:, at : at + length] = grad[:16]
+            send, keep = ((sx, kx), (sy, ky))[side]
+            first, kept = ((16, 32), (32, 16))[side]
+            here = slice(lo, lo + length)
+            send[:16, here] = grad[first : first + 16].astype(jnp.bfloat16)
+            send[16:, here] = grad[48:].astype(jnp.bfloat16)
+            keep[:, here] = grad[kept : kept + 16]
+
+    return call(
+        kernel,
+        (
+            jax.ShapeDtypeStruct((16, size), jnp.float32),
+            jax.ShapeDtypeStruct((32, half), jnp.bfloat16),
+            jax.ShapeDtypeStruct((16, half), jnp.float32),
+            jax.ShapeDtypeStruct((32, half), jnp.bfloat16),
+            jax.ShapeDtypeStruct((16, half), jnp.float32),
+        ),
+        (low, half_low, *blocks, counts),
+        [whole] * 8,
+        flops=4 * 64 * width * size,
+        moved=4 * width * size,
+        out_specs=(whole,) * 5,
+    )
+
+
+def update_token(index, size, mine, parts, factor, accum, before):
+    rows, tokens = factor.shape
+    half = size // 2
+    start = index * CHUNK
+
+    def kernel(mine_ref, rx, ry, qy, qx, factor_ref, accum_ref, *rest):
+        next_ref, sums_ref = rest[-2:]
+        for side, (wide, thin) in enumerate(((rx, ry), (qy, qx))):
+            at = side * half
+            valid = min(half, tokens - start - at)
+            here = slice(start + at, start + at + valid)
+            grad = (
+                mine_ref[:, at : at + valid]
+                + wide[:16, :valid].astype(jnp.float32)
+                + thin[:, :valid].astype(jnp.float32)
+            )
+            total = accum_ref[:, here] + grad * grad
+            sums_ref[:, at : at + valid] = total
+            next_ref[:, at : at + valid] = factor_ref[:, here] + step_rate * grad * lax.rsqrt(total)
+
+    block = pl.BlockSpec((rows, CHUNK), lambda i: (0, index))
+    extra = () if before is None else tuple(before)
+    return call(
+        kernel,
+        (jax.ShapeDtypeStruct(factor.shape, jnp.float32),) * 2,
+        (mine, *parts, factor, accum) + extra,
+        [whole] * 7 + [pl.BlockSpec(memory_space=pl.ANY)] * len(extra),
+        moved=16 * rows * size,
+        grid=(1,),
+        out_specs=(block, block),
+        input_output_aliases={7: 0, 8: 1} if extra else {},
+    )
+
+
+def shards(counts, u_factor, u_accum, v_factor, v_accum):
+    tokens = v_factor.shape[1]
+    by_token = counts.T
+    place = jnp.stack([lax.axis_index("tok"), lax.axis_index("ten")]).astype(jnp.int32)
+    ten = lambda a, bit: swap(a, "ten", bit, 4)
+    tok = lambda a, bit: swap(a, "tok", bit, 8)
+
+    chunks = []
+    for index, start in enumerate(range(0, tokens, CHUNK)):
+        size = min(CHUNK, -(-(tokens - start) // (2 * LANES)) * 2 * LANES)
+        chunks.append((index, start, size))
+
+    with jax.named_scope("gather_tokens"):
+        held = []
+        for index, start, size in chunks:
+            own = v_factor[:, start : start + size].astype(jnp.bfloat16)
+            own = jnp.pad(own, ((0, 0), (0, size - own.shape[1])))
+            x, y = ten(own, 1), ten(own, 2)
+            held.append((own, x, y, ten(x[:, : size // 2], 2), ten(y[:, size // 2 :], 1)))
+
+    with jax.named_scope("gather_tenants"):
+        stack = jnp.concatenate([u_factor, u_accum], axis=0)[None]
+        for bit in (1, 2, 4):
+            stack = jnp.concatenate([stack, tok(stack, bit)], axis=0)
+        factor, accum, half_low = order_tenant(place, stack)
+
+    with jax.named_scope("tenant_grad"):
+        grad = None
+        for (index, start, size), blocks in zip(chunks, held):
+            grad = tenant_grad(start, size, half_low, blocks, by_token, grad)
+        for bit in (1, 2):
+            grad = grad + tok(grad, bit)
+        low, half_low, u_next, u_accum_next = update_tenant(place, grad, tok(grad, 4), factor, accum)
+
+    with jax.named_scope("token_grad"):
+        outs = None
+        for (index, start, size), blocks in reversed(list(zip(chunks, held))):
+            mine, sx, kx, sy, ky = token_grad(start, size, low, half_low, blocks, by_token)
+            rx, qy = ten(sx, 1), ten(sy, 2)
+            ry = ten((kx + rx[16:].astype(jnp.float32)).astype(jnp.bfloat16), 2)
+            qx = ten((ky + qy[16:].astype(jnp.float32)).astype(jnp.bfloat16), 1)
+            outs = update_token(index, size, mine, (rx, ry, qy, qx), v_factor, v_accum, outs)
+    return (u_next, u_accum_next, *outs)
+
+
 def solution(mesh):
-    return jax.shard_map(
-        shards,
-        mesh=mesh,
-        in_specs=(
-            P("ten", "tok"),
-            P("tok", "ten"),
-            P("tok", "ten"),
-            P("ten", "tok"),
-            P("ten", "tok"),
-        ),
-        out_specs=(P("tok", "ten"), P("tok", "ten"), P("ten", "tok"), P("ten", "tok")),
-        check_vma=False,
-    )
+    def program(counts, u_factor, u_accum, v_factor, v_accum):
+        rank, tenants = u_factor.shape
+        tokens = v_factor.shape[1] // mesh.shape["tok"]
+        suits = (
+            mesh.shape["ten"] == 4
+            and mesh.shape["tok"] == 8
+            and rank == 64
+            and tenants == 4 * 256
+            and tokens % 16 == 0
+        )
+        return jax.shard_map(
+            shards if suits else shards_any,
+            mesh=mesh,
+            in_specs=(
+                P("ten", "tok"),
+                P("tok", "ten"),
+                P("tok", "ten"),
+                P("ten", "tok"),
+                P("ten", "tok"),
+            ),
+            out_specs=(P("tok", "ten"), P("tok", "ten"), P("ten", "tok"), P("ten", "tok")),
+            check_vma=False,
+        )(counts, u_factor, u_accum, v_factor, v_accum)
+
+    return program

time: 179 us -> 82.4 us (0.46)
  waiting for transfers between devices: 103 us -> 18.1 us
  starting transfers between devices: 0.12 us -> 33.5 us
  blocking collectives: 29.7 us -> 0 us
  matrix products: 25.4 us -> 0 us
  Pallas kernels: 0 us -> 16 us
  between operations: 13.8 us -> 0.9 us
  local copies, waits for them, and re-layouts: 0.01 us -> 11.4 us
  other arithmetic: 6.78 us -> 2.24 us
    reduce_scatter x2 -> x0, waiting for transfers between devices: 80.6 us -> none  [the longest x1 50.5 us: shards(): lax.psum_scatter(jnp.dot(u_fresh, resid_fresh, preferred_element_type=jnp...]
    ppermute x0 -> x30, starting transfers between devices: none -> 33.5 us  [swap(): return lax.ppermute(a, axis, [(i, i ^ bit) for i in range(size)])]
    all_gather x2 -> x0, blocking collectives: 29.7 us -> none  [gather_tenant(): return lax.all_gather(low_rows, 'tok', axis=0, tiled=True)]
    dot_general x2 -> x0, matrix products: 25.4 us -> none  [the longest x1 14 us: shards(): lax.dot_general(v_tile, resid, (((1,), (1,)), ((), ())), preferred_elemen...]
    all_gather x1 -> x0, waiting for transfers between devices: 22.5 us -> none  [shards(): lax.all_gather(v_factor.astype(jnp.bfloat16), 'ten', axis=0, tiled=True)]
    ppermute x0 -> x30, waiting for transfers between devices: none -> 18.1 us  [swap(): return lax.ppermute(a, axis, [(i, i ^ bit) for i in range(size)])]
    pallas_call x0 -> x11, Pallas kernels: none -> 16 us  [call(): pl.pallas_call(kernel, out_shape=out_shape, in_specs=in_specs, compiler_p...]
    unnamed x8 -> x36, local copies, waits for them, and re-layouts: 0.01 us -> 11.3 us
  transfers between devices with their start and end apart: 3 -> 30, of which waited for: 3 -> 10; matrix products, arithmetic and copies ran while one was open for 0% -> 2% of each run, Pallas kernels for 0% -> 13%
where the time goes in v1:
time: 82.4 us; the launch traced here: 82.1 us
  starting transfers between devices  33.5 us (41%)
  waiting for transfers between devices  18.1 us (22%)
  Pallas kernels  16 us (19%)
  local copies, waits for them, and re-layouts  11.4 us (14%)
  other arithmetic  2.24 us (3%)
  between operations  0.9 us (1%)
    ppermute x30, starting transfers between devices, swap(): return lax.ppermute(a, axis, [(i, i ^ bit) for i in range(size)])  33.5 us
    ppermute x30, waiting for transfers between devices, swap(): return lax.ppermute(a, axis, [(i, i ^ bit) for i in range(size)])  18.1 us
    pallas_call x11, Pallas kernels, call(): pl.pallas_call(kernel, out_shape=out_shape, in_specs=in_specs, compiler_p...  16 us
    unnamed x36, local copies, waits for them, and re-layouts  11.3 us
  transfers between devices with their start and end apart: 30, of which 10 were waited for; matrix products, arithmetic and copies ran while one was open for 2% of the time, Pallas kernels for 13%

profile of v1, /device:TPU:0, one launch (start us, length us, event | category | flops | bytes accessed | tf_op | source)
XLA Modules:
  0.0 82.1 jit_solution(3094767499437526883)
XLA Ops:
  1.8 1.3 %convert.5 = bf16[16,16032]{1,0:T(8,128)(2,1)S(1)} convert(f32[16,16032]{1,0:T(8,128)} %factor_ref.5) | non-fusion elementwise | flops 256512 | bytes 1539072 | tf_op jit(solution)/shard_map/convert.2 | solution.py:315
  3.1 2.6 %collective-permute-start.11 = (bf16[16,6144]{1,0:T(8,128)(2,1)S(1)}, bf16[16,6144]{1,0:T(8,128)(2,1)S(1)}, u32[]{:S(2)}, u32[]{:S(2)}) collective-permute-start(bf16[16,6144]{1,0:T(8,128)(2,1)S(1)} %get-tuple-element.60.own), channel_id=1, source_target_pairs={{0,1},{1,0},{2,3},{3,2},{4,5},{5,4},{6,7},{7,6},{8,9},{9,8},{10,11... | collective-permute-start | bytes 589832 | tf_op jit(solution)/shard_map/gather_tokens/ppermute | solution.py:59
  5.7 1.5 %collective-permute-start.12 = (bf16[16,6144]{1,0:T(8,128)(2,1)S(1)}, bf16[16,6144]{1,0:T(8,128)(2,1)S(1)}, u32[]{:S(2)}, u32[]{:S(2)}) collective-permute-start(bf16[16,6144]{1,0:T(8,128)(2,1)S(1)} %get-tuple-element.60.own), channel_id=1, source_target_pairs={{0,2},{1,3},{2,0},{3,1},{4,6},{5,7},{6,4},{7,5},{8,10},{9,11},{10,... | collective-permute-start | bytes 589832 | tf_op jit(solution)/shard_map/gather_tokens/ppermute | solution.py:59
  7.2 1.6 %collective-permute-start.1 = (f32[2,16,256]{2,1,0:T(8,128)S(1)}, f32[2,16,256]{2,1,0:T(8,128)S(1)}, u32[]{:S(2)}, u32[]{:S(2)}) collective-permute-start(f32[2,16,256]{2,1,0:T(8,128)S(1)} %pad_maximum_fusion.2), channel_id=1, source_target_pairs={{0,8},{4,12},{8,0},{12,4},{16,24},{20,28},{24,16},{28,20},{1,9},{5... | collective-permute-start | bytes 98312 | tf_op jit(solution)/shard_map/gather_tenants/ppermute | solution.py:59
  9.8 1.3 %collective-permute-done.1 = f32[2,16,256]{2,1,0:T(8,128)S(1)} collective-permute-done((f32[2,16,256]{2,1,0:T(8,128)S(1)}, f32[2,16,256]{2,1,0:T(8,128)S(1)}, u32[]{:S(2)}, u32[]{:S(2)}) %collective-permute-start.1) | collective-permute-done | bytes 32800 | tf_op jit(solution)/shard_map/gather_tenants/ppermute | solution.py:59
  11.7 1.5 %collective-permute-start.4 = (bf16[16,3840]{1,0:T(8,128)(2,1)S(1)}, bf16[16,3840]{1,0:T(8,128)(2,1)S(1)}, u32[]{:S(2)}, u32[]{:S(2)}) collective-permute-start(bf16[16,3840]{1,0:T(8,128)(2,1)S(1)} %pad.4.own), channel_id=1, source_target_pairs={{0,2},{1,3},{2,0},{3,1},{4,6},{5,7},{6,4},{7,5},{8,10},{9,11},{10,... | collective-permute-start | bytes 368648 | tf_op jit(solution)/shard_map/gather_tokens/ppermute | solution.py:59
  13.4 2.6 %collective-permute-start.2 = (f32[4,16,256]{2,1,0:T(8,128)S(1)}, f32[4,16,256]{2,1,0:T(8,128)S(1)}, u32[]{:S(2)}, u32[]{:S(2)}) collective-permute-start(f32[4,16,256]{2,1,0:T(8,128)S(1)} %pad_maximum_fusion.1), channel_id=1, source_target_pairs={{0,16},{4,20},{8,24},{12,28},{16,0},{20,4},{24,8},{28,12},{1,17},{... | collective-permute-start | bytes 196616 | tf_op jit(solution)/shard_map/gather_tenants/ppermute | solution.py:59
  16.1 1.5 %collective-permute-done.8.y = bf16[16,6144]{1,0:T(8,128)(2,1)S(1)} collective-permute-done((bf16[16,6144]{1,0:T(8,128)(2,1)S(1)}, bf16[16,6144]{1,0:T(8,128)(2,1)S(1)}, u32[]{:S(2)}, u32[]{:S(2)}) %collective-permute-start.8) | collective-permute-done | bytes 196640 | tf_op jit(solution)/shard_map/gather_tokens/ppermute | solution.py:59
  17.6 1.5 %collective-permute-start.13 = (bf16[16,3072]{1,0:T(8,128)(2,1)S(1)}, bf16[16,3072]{1,0:T(8,128)(2,1)S(1)}, u32[]{:S(2)}, u32[]{:S(2)}) collective-permute-start(bf16[16,3072]{1,0:T(8,128)(2,1)S(1)} %slice.70), channel_id=1, source_target_pairs={{0,2},{1,3},{2,0},{3,1},{4,6},{5,7},{6,4},{7,5},{8,10},{9,11},{10,... | collective-permute-start | bytes 294920 | tf_op jit(solution)/shard_map/gather_tokens/ppermute | solution.py:59
  19.8 1.6 %collective-permute-start.10 = (bf16[16,3072]{1,0:T(8,128)(2,1)S(1)}, bf16[16,3072]{1,0:T(8,128)(2,1)S(1)}, u32[]{:S(2)}, u32[]{:S(2)}) collective-permute-start(bf16[16,3072]{1,0:T(8,128)(2,1)S(1)} %slice.68), channel_id=1, source_target_pairs={{0,1},{1,0},{2,3},{3,2},{4,5},{5,4},{6,7},{7,6},{8,9},{9,8},{10,11... | collective-permute-start | bytes 294920 | tf_op jit(solution)/shard_map/gather_tokens/ppermute | solution.py:59
  22.4 1.6 %collective-permute-start.5 = (bf16[16,1920]{1,0:T(8,128)(2,1)S(1)}, bf16[16,1920]{1,0:T(8,128)(2,1)S(1)}, u32[]{:S(2)}, u32[]{:S(2)}) collective-permute-start(bf16[16,1920]{1,0:T(8,128)(2,1)S(1)} %slice.64), channel_id=1, source_target_pairs={{0,2},{1,3},{2,0},{3,1},{4,6},{5,7},{6,4},{7,5},{8,10},{9,11},{10,... | collective-permute-start | bytes 184328 | tf_op jit(solution)/shard_map/gather_tokens/ppermute | solution.py:59
  24.7 5.7 %copy-done = s32[256,16032]{0,1:T(8,128)S(1)} copy-done((s32[256,16032]{0,1:T(8,128)S(1)}, s32[256,16032]{0,1:T(8,128)}, u32[]{:S(2)}) %copy-start) | copy-done | bytes 16416792
  31.3 2.3 %tenant_grad.4.rest_0_ = f32[64,256]{1,0:T(8,128)S(1)} custom-call(bf16[64,256]{1,0:T(8,128)(2,1)S(1)} %get-tuple-element.32.half_ref, bf16[16,6144]{1,0:T(8,128)(2,1)S(1)} %get-tuple-element.60.own, bf16[16,6144]{1,0:T(8,128)(2,1)S(1)} %collective-permute-done.11.x, bf16[16,6144]{1,0:T(8,128)(2,1)S(1)} %copy-done.5, ...), custom_call_target="tpu_custom_call" | custom-call | flops 402653184 | bytes 6291456 | tf_op jit(solution)/shard_map/tenant_grad/pallas_call | solution.py:63
  33.6 3.3 %copy-done.1 = s32[256,16032]{0,1:T(8,128)S(1)} copy-done((s32[256,16032]{0,1:T(8,128)S(1)}, s32[256,16032]{0,1:T(8,128)}, u32[]{:S(2)}) %copy-start.1) | copy-done | bytes 16416792
  37.0 2.2 %tenant_grad.5.rest_0_ = f32[64,256]{1,0:T(8,128)S(1)} custom-call(bf16[64,256]{1,0:T(8,128)(2,1)S(1)} %get-tuple-element.32.half_ref, bf16[16,6144]{1,0:T(8,128)(2,1)S(1)} %get-tuple-element.61.own, bf16[16,6144]{1,0:T(8,128)(2,1)S(1)} %copy-done.10, bf16[16,6144]{1,0:T(8,128)(2,1)S(1)} %copy-done.8, bf16[16,3072]{1,0:T(8,128)(2,1)S(1)} %collective-permute-done.9.d0, ...), custom_call_target="tpu_custom_call" | custom-call | flops 402653184 | bytes 6291456 | tf_op jit(solution)/shard_map/tenant_grad/pallas_call | solution.py:63
  40.5 1.5 %tenant_grad.6 = f32[64,256]{1,0:T(8,128)S(1)} custom-call(bf16[64,256]{1,0:T(8,128)(2,1)S(1)} %get-tuple-element.32.half_ref, bf16[16,3840]{1,0:T(8,128)(2,1)S(1)} %pad.4.own, bf16[16,3840]{1,0:T(8,128)(2,1)S(1)} %collective-permute-done.3.x, bf16[16,3840]{1,0:T(8,128)(2,1)S(1)} %collective-permute-done.4.y, ...), custom_call_target="tpu_custom_call" | custom-call | flops 251658240 | bytes 3932160 | tf_op jit(solution)/shard_map/tenant_grad/pallas_call | solution.py:63
  42.1 1.2 %collective-permute-done.15 = f32[64,256]{1,0:T(8,128)S(1)} collective-permute-done((f32[64,256]{1,0:T(8,128)S(1)}, f32[64,256]{1,0:T(8,128)S(1)}, u32[]{:S(2)}, u32[]{:S(2)}) %collective-permute-start.15) | collective-permute-done | bytes 65568 | tf_op jit(solution)/shard_map/tenant_grad/ppermute | solution.py:59
  43.3 1.6 %collective-permute-start.16 = (f32[64,256]{1,0:T(8,128)S(1)}, f32[64,256]{1,0:T(8,128)S(1)}, u32[]{:S(2)}, u32[]{:S(2)}) collective-permute-start(f32[64,256]{1,0:T(8,128)S(1)} %add.26), channel_id=1, source_target_pairs={{0,8},{4,12},{8,0},{12,4},{16,24},{20,28},{24,16},{28,20},{1,9},{5... | collective-permute-start | bytes 196616 | tf_op jit(solution)/shard_map/tenant_grad/ppermute | solution.py:59
  45.0 2.7 %collective-permute-done.16 = f32[64,256]{1,0:T(8,128)S(1)} collective-permute-done((f32[64,256]{1,0:T(8,128)S(1)}, f32[64,256]{1,0:T(8,128)S(1)}, u32[]{:S(2)}, u32[]{:S(2)}) %collective-permute-start.16) | collective-permute-done | bytes 65568 | tf_op jit(solution)/shard_map/tenant_grad/ppermute | solution.py:59
  47.7 2.7 %collective-permute-start.17 = (f32[64,256]{1,0:T(8,128)S(1)}, f32[64,256]{1,0:T(8,128)S(1)}, u32[]{:S(2)}, u32[]{:S(2)}) collective-permute-start(f32[64,256]{1,0:T(8,128)S(1)} %add.27.a_ref), channel_id=1, source_target_pairs={{0,16},{4,20},{8,24},{12,28},{16,0},{20,4},{24,8},{28,12},{1,17},{... | collective-permute-start | bytes 196616 | tf_op jit(solution)/shard_map/tenant_grad/ppermute | solution.py:59
  50.3 2.6 %collective-permute-done.17.b_ref = f32[64,256]{1,0:T(8,128)S(1)} collective-permute-done((f32[64,256]{1,0:T(8,128)S(1)}, f32[64,256]{1,0:T(8,128)S(1)}, u32[]{:S(2)}, u32[]{:S(2)}) %collective-permute-start.17) | collective-permute-done | bytes 65568 | tf_op jit(solution)/shard_map/tenant_grad/ppermute | solution.py:59
  54.1 1.4 %token_grad.8 = (f32[16,3840]{1,0:T(8,128)S(1)}, bf16[32,1920]{1,0:T(8,128)(2,1)S(1)}, f32[16,1920]{1,0:T(8,128)S(1)}, bf16[32,1920]{1,0:T(8,128)(2,1)S(1)}, f32[16,1920]{1,0:T(8,128)S(1)}) custom-call(bf16[64,256]{1,0:T(8,128)(2,1)S(1)} %get-tuple-element.37.low_ref, bf16[64,256]{1,0:T(8,128)(2,1)S(1)} %get-tuple-element.38.half_ref, ...), custom_call_target="tpu_custom_call" | custom-call | flops 251658240 | bytes 3932160 | tf_op jit(solution)/shard_map/token_grad/pallas_call | solution.py:63
  56.1 1.5 %collective-permute-start.26 = (bf16[32,1920]{1,0:T(8,128)(2,1)S(1)}, bf16[32,1920]{1,0:T(8,128)(2,1)S(1)}, u32[]{:S(2)}, u32[]{:S(2)}) collective-permute-start(bf16[32,1920]{1,0:T(8,128)(2,1)S(1)} %get-tuple-element.50), channel_id=1, source_target_pairs={{0,1},{1,0},{2,3},{3,2},{4,5},{5,4},{6,7},{7,6},{8,9},{9,8},{10,11... | collective-permute-start | bytes 368648 | tf_op jit(solution)/shard_map/token_grad/ppermute | solution.py:59
  57.5 2.0 %token_grad.7 = (f32[16,6144]{1,0:T(8,128)S(1)}, bf16[32,3072]{1,0:T(8,128)(2,1)S(1)}, f32[16,3072]{1,0:T(8,128)S(1)}, bf16[32,3072]{1,0:T(8,128)(2,1)S(1)}, f32[16,3072]{1,0:T(8,128)S(1)}) custom-call(bf16[64,256]{1,0:T(8,128)(2,1)S(1)} %get-tuple-element.37.low_ref, bf16[64,256]{1,0:T(8,128)(2,1)S(1)} %get-tuple-element.38.half_ref, ...), custom_call_target="tpu_custom_call" | custom-call | flops 402653184 | bytes 6291456 | tf_op jit(solution)/shard_map/token_grad/pallas_call | solution.py:63
  59.6 1.6 %collective-permute-start.24 = (bf16[32,3072]{1,0:T(8,128)(2,1)S(1)}, bf16[32,3072]{1,0:T(8,128)(2,1)S(1)}, u32[]{:S(2)}, u32[]{:S(2)}) collective-permute-start(bf16[32,3072]{1,0:T(8,128)(2,1)S(1)} %get-tuple-element.47), channel_id=1, source_target_pairs={{0,2},{1,3},{2,0},{3,1},{4,6},{5,7},{6,4},{7,5},{8,10},{9,11},{10,... | collective-permute-start | bytes 589832 | tf_op jit(solution)/shard_map/token_grad/ppermute | solution.py:59
  61.7 2.0 %token_grad.6 = (f32[16,6144]{1,0:T(8,128)S(1)}, bf16[32,3072]{1,0:T(8,128)(2,1)S(1)}, f32[16,3072]{1,0:T(8,128)S(1)}, bf16[32,3072]{1,0:T(8,128)(2,1)S(1)}, f32[16,3072]{1,0:T(8,128)S(1)}) custom-call(bf16[64,256]{1,0:T(8,128)(2,1)S(1)} %get-tuple-element.37.low_ref, bf16[64,256]{1,0:T(8,128)(2,1)S(1)} %get-tuple-element.38.half_ref, ...), custom_call_target="tpu_custom_call" | custom-call | flops 402653184 | bytes 6291456 | tf_op jit(solution)/shard_map/token_grad/pallas_call | solution.py:63
  64.3 1.5 %collective-permute-start.18 = (bf16[32,3072]{1,0:T(8,128)(2,1)S(1)}, bf16[32,3072]{1,0:T(8,128)(2,1)S(1)}, u32[]{:S(2)}, u32[]{:S(2)}) collective-permute-start(bf16[32,3072]{1,0:T(8,128)(2,1)S(1)} %get-tuple-element.40), channel_id=1, source_target_pairs={{0,1},{1,0},{2,3},{3,2},{4,5},{5,4},{6,7},{7,6},{8,9},{9,8},{10,11... | collective-permute-start | bytes 589832 | tf_op jit(solution)/shard_map/token_grad/ppermute | solution.py:59
  65.8 1.5 %collective-permute-done.24.qy = bf16[32,3072]{1,0:T(8,128)(2,1)S(1)} collective-permute-done((bf16[32,3072]{1,0:T(8,128)(2,1)S(1)}, bf16[32,3072]{1,0:T(8,128)(2,1)S(1)}, u32[]{:S(2)}, u32[]{:S(2)}) %collective-permute-start.24) | collective-permute-done | bytes 196640 | tf_op jit(solution)/shard_map/token_grad/ppermute | solution.py:59
  67.6 1.3 %collective-permute-done.22.rx = bf16[32,3072]{1,0:T(8,128)(2,1)S(1)} collective-permute-done((bf16[32,3072]{1,0:T(8,128)(2,1)S(1)}, bf16[32,3072]{1,0:T(8,128)(2,1)S(1)}, u32[]{:S(2)}, u32[]{:S(2)}) %collective-permute-start.22) | collective-permute-done | bytes 196640 | tf_op jit(solution)/shard_map/token_grad/ppermute | solution.py:59
  70.6 2.3 %collective-permute-done.18.rx = bf16[32,3072]{1,0:T(8,128)(2,1)S(1)} collective-permute-done((bf16[32,3072]{1,0:T(8,128)(2,1)S(1)}, bf16[32,3072]{1,0:T(8,128)(2,1)S(1)}, u32[]{:S(2)}, u32[]{:S(2)}) %collective-permute-start.18) | collective-permute-done | bytes 196640 | tf_op jit(solution)/shard_map/token_grad/ppermute | solution.py:59
  73.6 1.3 %collective-permute-start.19 = (bf16[16,3072]{1,0:T(8,128)(2,1)S(1)}, bf16[16,3072]{1,0:T(8,128)(2,1)S(1)}, u32[]{:S(2)}, u32[]{:S(2)}) collective-permute-start(bf16[16,3072]{1,0:T(8,128)(2,1)S(1)} %add_convert_fusion.3), channel_id=1, source_target_pairs={{0,2},{1,3},{2,0},{3,1},{4,6},{5,7},{6,4},{7,5},{8,10},{9,11},{10,... | collective-permute-start | bytes 294920 | tf_op jit(solution)/shard_map/token_grad/ppermute | solution.py:59
  75.8 3.4 %collective-permute-done.27.ry = bf16[16,1920]{1,0:T(8,128)(2,1)S(1)} collective-permute-done((bf16[16,1920]{1,0:T(8,128)(2,1)S(1)}, bf16[16,1920]{1,0:T(8,128)(2,1)S(1)}, u32[]{:S(2)}, u32[]{:S(2)}) %collective-permute-start.27) | collective-permute-done | bytes 61472 | tf_op jit(solution)/shard_map/token_grad/ppermute | solution.py:59
  (98 shorter events, 17.2 us)
Async XLA Ops:
  1.3 5.8 %collective-permute-start = (f32[1,16,256]{2,1,0:T(8,128)S(1)}, f32[1,16,256]{2,1,0:T(8,128)S(1)}, u32[]{:S(2)}, u32[]{:S(2)}) collective-permute-start(f32[1,16,256]{2,1,0:T(8,128)S(1)} %maximum_bitcast_fusion), channel_id=1, source_target_pairs={{0,4},{4,0},{8,12},{12,8},{16,20},{20,16},{24,28},{28,24},{1,5},{5... | collective-permute-start | bytes 49160 | tf_op jit(solution)/shard_map/gather_tenants/ppermute | solution.py:59
  3.1 8.5 %collective-permute-start.11 = (bf16[16,6144]{1,0:T(8,128)(2,1)S(1)}, bf16[16,6144]{1,0:T(8,128)(2,1)S(1)}, u32[]{:S(2)}, u32[]{:S(2)}) collective-permute-start(bf16[16,6144]{1,0:T(8,128)(2,1)S(1)} %get-tuple-element.60.own), channel_id=1, source_target_pairs={{0,1},{1,0},{2,3},{3,2},{4,5},{5,4},{6,7},{7,6},{8,9},{9,8},{10,11... | collective-permute-start | bytes 589832 | tf_op jit(solution)/shard_map/gather_tokens/ppermute | solution.py:59
  5.7 7.7 %collective-permute-start.12 = (bf16[16,6144]{1,0:T(8,128)(2,1)S(1)}, bf16[16,6144]{1,0:T(8,128)(2,1)S(1)}, u32[]{:S(2)}, u32[]{:S(2)}) collective-permute-start(bf16[16,6144]{1,0:T(8,128)(2,1)S(1)} %get-tuple-element.60.own), channel_id=1, source_target_pairs={{0,2},{1,3},{2,0},{3,1},{4,6},{5,7},{6,4},{7,5},{8,10},{9,11},{10,... | collective-permute-start | bytes 589832 | tf_op jit(solution)/shard_map/gather_tokens/ppermute | solution.py:59
  7.2 3.9 %collective-permute-start.1 = (f32[2,16,256]{2,1,0:T(8,128)S(1)}, f32[2,16,256]{2,1,0:T(8,128)S(1)}, u32[]{:S(2)}, u32[]{:S(2)}) collective-permute-start(f32[2,16,256]{2,1,0:T(8,128)S(1)} %pad_maximum_fusion.2), channel_id=1, source_target_pairs={{0,8},{4,12},{8,0},{12,4},{16,24},{20,28},{24,16},{28,20},{1,9},{5... | collective-permute-start | bytes 98312 | tf_op jit(solution)/shard_map/gather_tenants/ppermute | solution.py:59
  8.8 8.8 %collective-permute-start.8 = (bf16[16,6144]{1,0:T(8,128)(2,1)S(1)}, bf16[16,6144]{1,0:T(8,128)(2,1)S(1)}, u32[]{:S(2)}, u32[]{:S(2)}) collective-permute-start(bf16[16,6144]{1,0:T(8,128)(2,1)S(1)} %get-tuple-element.61.own), channel_id=1, source_target_pairs={{0,2},{1,3},{2,0},{3,1},{4,6},{5,7},{6,4},{7,5},{8,10},{9,11},{10,... | collective-permute-start | bytes 589832 | tf_op jit(solution)/shard_map/gather_tokens/ppermute | solution.py:59
  9.3 9.9 %collective-permute-start.7 = (bf16[16,6144]{1,0:T(8,128)(2,1)S(1)}, bf16[16,6144]{1,0:T(8,128)(2,1)S(1)}, u32[]{:S(2)}, u32[]{:S(2)}) collective-permute-start(bf16[16,6144]{1,0:T(8,128)(2,1)S(1)} %get-tuple-element.61.own), channel_id=1, source_target_pairs={{0,1},{1,0},{2,3},{3,2},{4,5},{5,4},{6,7},{7,6},{8,9},{9,8},{10,11... | collective-permute-start | bytes 589832 | tf_op jit(solution)/shard_map/gather_tokens/ppermute | solution.py:59
  11.1 10.2 %collective-permute-start.3 = (bf16[16,3840]{1,0:T(8,128)(2,1)S(1)}, bf16[16,3840]{1,0:T(8,128)(2,1)S(1)}, u32[]{:S(2)}, u32[]{:S(2)}) collective-permute-start(bf16[16,3840]{1,0:T(8,128)(2,1)S(1)} %pad.4.own), channel_id=1, source_target_pairs={{0,1},{1,0},{2,3},{3,2},{4,5},{5,4},{6,7},{7,6},{8,9},{9,8},{10,11... | collective-permute-start | bytes 368648 | tf_op jit(solution)/shard_map/gather_tokens/ppermute | solution.py:59
  11.7 10.8 %collective-permute-start.4 = (bf16[16,3840]{1,0:T(8,128)(2,1)S(1)}, bf16[16,3840]{1,0:T(8,128)(2,1)S(1)}, u32[]{:S(2)}, u32[]{:S(2)}) collective-permute-start(bf16[16,3840]{1,0:T(8,128)(2,1)S(1)} %pad.4.own), channel_id=1, source_target_pairs={{0,2},{1,3},{2,0},{3,1},{4,6},{5,7},{6,4},{7,5},{8,10},{9,11},{10,... | collective-permute-start | bytes 368648 | tf_op jit(solution)/shard_map/gather_tokens/ppermute | solution.py:59
  13.4 6.4 %collective-permute-start.2 = (f32[4,16,256]{2,1,0:T(8,128)S(1)}, f32[4,16,256]{2,1,0:T(8,128)S(1)}, u32[]{:S(2)}, u32[]{:S(2)}) collective-permute-start(f32[4,16,256]{2,1,0:T(8,128)S(1)} %pad_maximum_fusion.1), channel_id=1, source_target_pairs={{0,16},{4,20},{8,24},{12,28},{16,0},{20,4},{24,8},{28,12},{1,17},{... | collective-permute-start | bytes 196616 | tf_op jit(solution)/shard_map/gather_tenants/ppermute | solution.py:59
  17.6 6.4 %collective-permute-start.13 = (bf16[16,3072]{1,0:T(8,128)(2,1)S(1)}, bf16[16,3072]{1,0:T(8,128)(2,1)S(1)}, u32[]{:S(2)}, u32[]{:S(2)}) collective-permute-start(bf16[16,3072]{1,0:T(8,128)(2,1)S(1)} %slice.70), channel_id=1, source_target_pairs={{0,2},{1,3},{2,0},{3,1},{4,6},{5,7},{6,4},{7,5},{8,10},{9,11},{10,... | collective-permute-start | bytes 294920 | tf_op jit(solution)/shard_map/gather_tokens/ppermute | solution.py:59
  19.2 5.5 %collective-permute-start.14 = (bf16[16,3072]{1,0:T(8,128)(2,1)S(1)}, bf16[16,3072]{1,0:T(8,128)(2,1)S(1)}, u32[]{:S(2)}, u32[]{:S(2)}) collective-permute-start(bf16[16,3072]{1,0:T(8,128)(2,1)S(1)} %slice.71), channel_id=1, source_target_pairs={{0,1},{1,0},{2,3},{3,2},{4,5},{5,4},{6,7},{7,6},{8,9},{9,8},{10,11... | collective-permute-start | bytes 294920 | tf_op jit(solution)/shard_map/gather_tokens/ppermute | solution.py:59
  19.8 13.8 %collective-permute-start.10 = (bf16[16,3072]{1,0:T(8,128)(2,1)S(1)}, bf16[16,3072]{1,0:T(8,128)(2,1)S(1)}, u32[]{:S(2)}, u32[]{:S(2)}) collective-permute-start(bf16[16,3072]{1,0:T(8,128)(2,1)S(1)} %slice.68), channel_id=1, source_target_pairs={{0,1},{1,0},{2,3},{3,2},{4,5},{5,4},{6,7},{7,6},{8,9},{9,8},{10,11... | collective-permute-start | bytes 294920 | tf_op jit(solution)/shard_map/gather_tokens/ppermute | solution.py:59
  21.3 12.3 %collective-permute-start.9 = (bf16[16,3072]{1,0:T(8,128)(2,1)S(1)}, bf16[16,3072]{1,0:T(8,128)(2,1)S(1)}, u32[]{:S(2)}, u32[]{:S(2)}) collective-permute-start(bf16[16,3072]{1,0:T(8,128)(2,1)S(1)} %slice.67), channel_id=1, source_target_pairs={{0,2},{1,3},{2,0},{3,1},{4,6},{5,7},{6,4},{7,5},{8,10},{9,11},{10,... | collective-permute-start | bytes 294920 | tf_op jit(solution)/shard_map/gather_tokens/ppermute | solution.py:59
  22.4 18.0 %collective-permute-start.5 = (bf16[16,1920]{1,0:T(8,128)(2,1)S(1)}, bf16[16,1920]{1,0:T(8,128)(2,1)S(1)}, u32[]{:S(2)}, u32[]{:S(2)}) collective-permute-start(bf16[16,1920]{1,0:T(8,128)(2,1)S(1)} %slice.64), channel_id=1, source_target_pairs={{0,2},{1,3},{2,0},{3,1},{4,6},{5,7},{6,4},{7,5},{8,10},{9,11},{10,... | collective-permute-start | bytes 184328 | tf_op jit(solution)/shard_map/gather_tokens/ppermute | solution.py:59
  24.0 16.4 %collective-permute-start.6 = (bf16[16,1920]{1,0:T(8,128)(2,1)S(1)}, bf16[16,1920]{1,0:T(8,128)(2,1)S(1)}, u32[]{:S(2)}, u32[]{:S(2)}) collective-permute-start(bf16[16,1920]{1,0:T(8,128)(2,1)S(1)} %slice.65), channel_id=1, source_target_pairs={{0,1},{1,0},{2,3},{3,2},{4,5},{5,4},{6,7},{7,6},{8,9},{9,8},{10,11... | collective-permute-start | bytes 184328 | tf_op jit(solution)/shard_map/gather_tokens/ppermute | solution.py:59
  42.0 1.3 %collective-permute-start.15 = (f32[64,256]{1,0:T(8,128)S(1)}, f32[64,256]{1,0:T(8,128)S(1)}, u32[]{:S(2)}, u32[]{:S(2)}) collective-permute-start(f32[64,256]{1,0:T(8,128)S(1)} %tenant_grad.6), channel_id=1, source_target_pairs={{0,4},{4,0},{8,12},{12,8},{16,20},{20,16},{24,28},{28,24},{1,5},{5... | collective-permute-start | bytes 196616 | tf_op jit(solution)/shard_map/tenant_grad/ppermute | solution.py:59
  43.3 4.3 %collective-permute-start.16 = (f32[64,256]{1,0:T(8,128)S(1)}, f32[64,256]{1,0:T(8,128)S(1)}, u32[]{:S(2)}, u32[]{:S(2)}) collective-permute-start(f32[64,256]{1,0:T(8,128)S(1)} %add.26), channel_id=1, source_target_pairs={{0,8},{4,12},{8,0},{12,4},{16,24},{20,28},{24,16},{28,20},{1,9},{5... | collective-permute-start | bytes 196616 | tf_op jit(solution)/shard_map/tenant_grad/ppermute | solution.py:59
  47.7 5.2 %collective-permute-start.17 = (f32[64,256]{1,0:T(8,128)S(1)}, f32[64,256]{1,0:T(8,128)S(1)}, u32[]{:S(2)}, u32[]{:S(2)}) collective-permute-start(f32[64,256]{1,0:T(8,128)S(1)} %add.27.a_ref), channel_id=1, source_target_pairs={{0,16},{4,20},{8,24},{12,28},{16,0},{20,4},{24,8},{28,12},{1,17},{... | collective-permute-start | bytes 196616 | tf_op jit(solution)/shard_map/tenant_grad/ppermute | solution.py:59
  55.5 8.8 %collective-permute-start.28 = (bf16[32,1920]{1,0:T(8,128)(2,1)S(1)}, bf16[32,1920]{1,0:T(8,128)(2,1)S(1)}, u32[]{:S(2)}, u32[]{:S(2)}) collective-permute-start(bf16[32,1920]{1,0:T(8,128)(2,1)S(1)} %get-tuple-element.52), channel_id=1, source_target_pairs={{0,2},{1,3},{2,0},{3,1},{4,6},{5,7},{6,4},{7,5},{8,10},{9,11},{10,... | collective-permute-start | bytes 368648 | tf_op jit(solution)/shard_map/token_grad/ppermute | solution.py:59
  56.1 23.2 %copy-start.2 = (f32[16,16032]{1,0:T(8,128)S(1)}, f32[16,16032]{1,0:T(8,128)}, u32[]{:S(2)}) copy-start(f32[16,16032]{1,0:T(8,128)} %factor_ref.5) | copy-start | bytes 3078148
  56.1 23.2 %copy-start.3 = (f32[16,16032]{1,0:T(8,128)S(1)}, f32[16,16032]{1,0:T(8,128)}, u32[]{:S(2)}) copy-start(f32[16,16032]{1,0:T(8,128)} %accum_ref.5) | copy-start | bytes 3078148
  56.1 17.5 %collective-permute-start.26 = (bf16[32,1920]{1,0:T(8,128)(2,1)S(1)}, bf16[32,1920]{1,0:T(8,128)(2,1)S(1)}, u32[]{:S(2)}, u32[]{:S(2)}) collective-permute-start(bf16[32,1920]{1,0:T(8,128)(2,1)S(1)} %get-tuple-element.50), channel_id=1, source_target_pairs={{0,1},{1,0},{2,3},{3,2},{4,5},{5,4},{6,7},{7,6},{8,9},{9,8},{10,11... | collective-permute-start | bytes 368648 | tf_op jit(solution)/shard_map/token_grad/ppermute | solution.py:59
  59.6 7.8 %collective-permute-start.24 = (bf16[32,3072]{1,0:T(8,128)(2,1)S(1)}, bf16[32,3072]{1,0:T(8,128)(2,1)S(1)}, u32[]{:S(2)}, u32[]{:S(2)}) collective-permute-start(bf16[32,3072]{1,0:T(8,128)(2,1)S(1)} %get-tuple-element.47), channel_id=1, source_target_pairs={{0,2},{1,3},{2,0},{3,1},{4,6},{5,7},{6,4},{7,5},{8,10},{9,11},{10,... | collective-permute-start | bytes 589832 | tf_op jit(solution)/shard_map/token_grad/ppermute | solution.py:59
  61.2 7.8 %collective-permute-start.22 = (bf16[32,3072]{1,0:T(8,128)(2,1)S(1)}, bf16[32,3072]{1,0:T(8,128)(2,1)S(1)}, u32[]{:S(2)}, u32[]{:S(2)}) collective-permute-start(bf16[32,3072]{1,0:T(8,128)(2,1)S(1)} %get-tuple-element.45), channel_id=1, source_target_pairs={{0,1},{1,0},{2,3},{3,2},{4,5},{5,4},{6,7},{7,6},{8,9},{9,8},{10,11... | collective-permute-start | bytes 589832 | tf_op jit(solution)/shard_map/token_grad/ppermute | solution.py:59
  63.7 5.8 %collective-permute-start.20 = (bf16[32,3072]{1,0:T(8,128)(2,1)S(1)}, bf16[32,3072]{1,0:T(8,128)(2,1)S(1)}, u32[]{:S(2)}, u32[]{:S(2)}) collective-permute-start(bf16[32,3072]{1,0:T(8,128)(2,1)S(1)} %get-tuple-element.42), channel_id=1, source_target_pairs={{0,2},{1,3},{2,0},{3,1},{4,6},{5,7},{6,4},{7,5},{8,10},{9,11},{10,... | collective-permute-start | bytes 589832 | tf_op jit(solution)/shard_map/token_grad/ppermute | solution.py:59
  64.3 8.6 %collective-permute-start.18 = (bf16[32,3072]{1,0:T(8,128)(2,1)S(1)}, bf16[32,3072]{1,0:T(8,128)(2,1)S(1)}, u32[]{:S(2)}, u32[]{:S(2)}) collective-permute-start(bf16[32,3072]{1,0:T(8,128)(2,1)S(1)} %get-tuple-element.40), channel_id=1, source_target_pairs={{0,1},{1,0},{2,3},{3,2},{4,5},{5,4},{6,7},{7,6},{8,9},{9,8},{10,11... | collective-permute-start | bytes 589832 | tf_op jit(solution)/shard_map/token_grad/ppermute | solution.py:59
  67.3 7.6 %collective-permute-start.29 = (bf16[16,1920]{1,0:T(8,128)(2,1)S(1)}, bf16[16,1920]{1,0:T(8,128)(2,1)S(1)}, u32[]{:S(2)}, u32[]{:S(2)}) collective-permute-start(bf16[16,1920]{1,0:T(8,128)(2,1)S(1)} %add_convert_fusion.4), channel_id=1, source_target_pairs={{0,1},{1,0},{2,3},{3,2},{4,5},{5,4},{6,7},{7,6},{8,9},{9,8},{10,11... | collective-permute-start | bytes 184328 | tf_op jit(solution)/shard_map/token_grad/ppermute | solution.py:59
  68.9 11.2 %collective-permute-start.25 = (bf16[16,3072]{1,0:T(8,128)(2,1)S(1)}, bf16[16,3072]{1,0:T(8,128)(2,1)S(1)}, u32[]{:S(2)}, u32[]{:S(2)}) collective-permute-start(bf16[16,3072]{1,0:T(8,128)(2,1)S(1)} %add_convert_fusion), channel_id=1, source_target_pairs={{0,1},{1,0},{2,3},{3,2},{4,5},{5,4},{6,7},{7,6},{8,9},{9,8},{10,11... | collective-permute-start | bytes 294920 | tf_op jit(solution)/shard_map/token_grad/ppermute | solution.py:59
  69.5 10.6 %collective-permute-start.23 = (bf16[16,3072]{1,0:T(8,128)(2,1)S(1)}, bf16[16,3072]{1,0:T(8,128)(2,1)S(1)}, u32[]{:S(2)}, u32[]{:S(2)}) collective-permute-start(bf16[16,3072]{1,0:T(8,128)(2,1)S(1)} %add_convert_fusion.1), channel_id=1, source_target_pairs={{0,2},{1,3},{2,0},{3,1},{4,6},{5,7},{6,4},{7,5},{8,10},{9,11},{10,... | collective-permute-start | bytes 294920 | tf_op jit(solution)/shard_map/token_grad/ppermute | solution.py:59
  72.9 8.2 %collective-permute-start.21 = (bf16[16,3072]{1,0:T(8,128)(2,1)S(1)}, bf16[16,3072]{1,0:T(8,128)(2,1)S(1)}, u32[]{:S(2)}, u32[]{:S(2)}) collective-permute-start(bf16[16,3072]{1,0:T(8,128)(2,1)S(1)} %add_convert_fusion.2), channel_id=1, source_target_pairs={{0,1},{1,0},{2,3},{3,2},{4,5},{5,4},{6,7},{7,6},{8,9},{9,8},{10,11... | collective-permute-start | bytes 294920 | tf_op jit(solution)/shard_map/token_grad/ppermute | solution.py:59
  73.6 7.5 %collective-permute-start.19 = (bf16[16,3072]{1,0:T(8,128)(2,1)S(1)}, bf16[16,3072]{1,0:T(8,128)(2,1)S(1)}, u32[]{:S(2)}, u32[]{:S(2)}) collective-permute-start(bf16[16,3072]{1,0:T(8,128)(2,1)S(1)} %add_convert_fusion.3), channel_id=1, source_target_pairs={{0,2},{1,3},{2,0},{3,1},{4,6},{5,7},{6,4},{7,5},{8,10},{9,11},{10,... | collective-permute-start | bytes 294920 | tf_op jit(solution)/shard_map/token_grad/ppermute | solution.py:59
  74.9 4.3 %collective-permute-start.27 = (bf16[16,1920]{1,0:T(8,128)(2,1)S(1)}, bf16[16,1920]{1,0:T(8,128)(2,1)S(1)}, u32[]{:S(2)}, u32[]{:S(2)}) collective-permute-start(bf16[16,1920]{1,0:T(8,128)(2,1)S(1)} %add_convert_fusion.5), channel_id=1, source_target_pairs={{0,2},{1,3},{2,0},{3,1},{4,6},{5,7},{6,4},{7,5},{8,10},{9,11},{10,... | collective-permute-start | bytes 184328 | tf_op jit(solution)/shard_map/token_grad/ppermute | solution.py:59
  (16 other events, 129.6 us)

commit v2 on v1

v2 whole, which is shorter than its diff:
```python
import jax
import jax.numpy as jnp
from jax import lax
from jax.experimental import pallas as pl
from jax.experimental.pallas import tpu as pltpu
from jax.sharding import PartitionSpec as P

weight_scale = 0.5
step_rate = 0.3
LANES = 128
CHUNK = 5376
INNER = 1024
PASS_COST = 64
HBM_SIDE_LIMIT = 34 * 2**20
VMEM_LIMIT = 12 * 2**20

whole = pl.BlockSpec(memory_space=pltpu.VMEM)
scalars = pl.BlockSpec(memory_space=pltpu.SMEM)


def residual(low_tile, v_tile, counts):
    logits = lax.dot_general(
        low_tile, v_tile, (((0,), (0,)), ((), ())), preferred_element_type=jnp.float32
    )
    weighted = weight_scale * counts.astype(jnp.float32)
    return (weighted - (1.0 + weighted) * jax.nn.sigmoid(logits)).astype(jnp.bfloat16)


def gather_tenant(low_rows):
    return lax.all_gather(low_rows, "tok", axis=0, tiled=True)


def shards_any(counts, u_factor, u_accum, v_factor, v_accum):
    v_tile = lax.all_gather(v_factor.astype(jnp.bfloat16), "ten", axis=0, tiled=True)
    u_tile = gather_tenant(u_factor.astype(jnp.bfloat16))
    resid = residual(u_tile, v_tile, counts)
    grad_u = lax.psum_scatter(
        lax.dot_general(
            v_tile, resid, (((1,), (1,)), ((), ())), preferred_element_type=jnp.float32
        ),
        "tok",
        scatter_dimension=0,
        tiled=True,
    )
    u_accum_next = u_accum + grad_u * grad_u
    u_next = u_factor + step_rate * grad_u / jnp.sqrt(u_accum_next)
    u_fresh = gather_tenant(u_next.astype(jnp.bfloat16))
    resid_fresh = residual(u_fresh, v_tile, counts)
    grad_v = lax.psum_scatter(
        jnp.dot(u_fresh, resid_fresh, preferred_element_type=jnp.float32),
        "ten",
        scatter_dimension=0,
        tiled=True,
    )
    v_accum_next = v_accum + grad_v * grad_v
    v_next = v_factor + step_rate * grad_v / jnp.sqrt(v_accum_next)
    return (u_next, u_accum_next, v_next, v_accum_next)


def swap(a, axis, bit, size):
    return lax.ppermute(a, axis, [(i, i ^ bit) for i in range(size)])


def call(kernel, out_shape, operands, in_specs, moved=0, limit=VMEM_LIMIT, **options):
    return pl.pallas_call(
        kernel,
        out_shape=out_shape,
        in_specs=in_specs,
        compiler_params=pltpu.CompilerParams(vmem_limit_bytes=limit),
        cost_estimate=pl.CostEstimate(
            flops=0, bytes_accessed=moved, transcendentals=0
        ),
        **options,
    )(*operands)


def order_tenant(place, gathered):
    def kernel(place_ref, all_ref, factor_ref, accum_ref, half_ref):
        for j in range(4):
            for h in range(2):
                source = (2 * (place_ref[1] ^ j) + h) ^ place_ref[0]
                rows = pl.ds(16 * j + 8 * h, 8)
                factor_ref[rows, :] = all_ref[source, :8, :]
                accum_ref[rows, :] = all_ref[source, 8:, :]
        half_ref[...] = (factor_ref[...].astype(jnp.bfloat16).astype(jnp.float32) * 0.5).astype(
            jnp.bfloat16
        )

    width = gathered.shape[2]
    return call(
        kernel,
        (
            jax.ShapeDtypeStruct((64, width), jnp.float32),
            jax.ShapeDtypeStruct((64, width), jnp.float32),
            jax.ShapeDtypeStruct((64, width), jnp.bfloat16),
        ),
        (place, gathered),
        [scalars, whole],
        out_specs=(whole, whole, whole),
    )


def pieces(start, size, cuts, tokens):
    found, at = [], start
    while at < start + size:
        stop = min([start + size, at + INNER] + [cut for cut in cuts if cut > at])
        found.append((at, stop - at, max(0, min(stop, tokens) - at)))
        at = stop
    return found


def stage(counts, after):
    tokens, width = counts.shape
    step = -(-tokens // 32) * 8

    def kernel(counts_ref, after_ref, out_ref, sems):
        copies = []
        for i, at in enumerate(range(0, tokens, step)):
            rows = pl.ds(at, min(step, tokens - at))
            copies.append(pltpu.make_async_copy(counts_ref.at[rows, :], out_ref.at[rows, :], sems.at[i]))
        for copy in copies:
            copy.start()
        for copy in copies:
            copy.wait()

    return call(
        kernel,
        jax.ShapeDtypeStruct((tokens, width), jnp.int32),
        (counts, after),
        [pl.BlockSpec(memory_space=pltpu.HBM)] * 2,
        moved=8 * tokens * width,
        limit=HBM_SIDE_LIMIT,
        out_specs=whole,
        scratch_shapes=[pltpu.SemaphoreType.DMA((4,))],
    )


def lifted(part):
    return part.astype(jnp.float32) * 0.25 + 0.5


def fresh_residual(half_low, v, lift):
    valid = lift.shape[0]
    logits = lax.dot_general(
        v, half_low, (((0,), (0,)), ((), ())), preferred_element_type=jnp.float32
    )[:valid]
    bend = jnp.tanh(logits)
    resid = (lift - lift * bend - 1.0).astype(jnp.bfloat16)
    if valid < v.shape[1]:
        pad = jnp.zeros((v.shape[1] - valid, resid.shape[1]), jnp.bfloat16)
        resid = jnp.concatenate([resid, pad], axis=0)
    return resid


def gathered(blocks, at, length):
    own, x, y, d0, d1 = blocks
    middle = d0.shape[1]
    diag = d0[:, at : at + length] if at < middle else d1[:, at - middle : at - middle + length]
    return jnp.concatenate([r[:, at : at + length] for r in (own, x, y)] + [diag], axis=0)


def tenant_grad(half_low, blocks, counts):
    tokens, width = counts.shape
    padded = blocks[0].shape[1]

    def kernel(half_ref, *refs):
        blocks_ref, counts_ref, out_ref = refs[:5], refs[5], refs[6]
        grad = jnp.zeros(out_ref.shape, jnp.float32)
        for at, length, valid in pieces(0, padded, [padded // 2], tokens):
            v = gathered(blocks_ref, at, length)
            resid = fresh_residual(half_ref[...], v, lifted(counts_ref[at : at + valid, :]))
            grad += jnp.dot(v, resid, preferred_element_type=jnp.float32)
        out_ref[...] = grad

    return call(
        kernel,
        jax.ShapeDtypeStruct((64, width), jnp.float32),
        (half_low, *blocks, counts),
        [whole] * 7,
        moved=PASS_COST * padded,
        out_specs=whole,
    )


def token_grad(start, size, low, step, blocks, counts):
    tokens, width = counts.shape
    half = size // 2
    ahead = len(step) if step else 2

    def kernel(*refs):
        blocks_ref, counts_ref = refs[ahead : ahead + 5], refs[ahead + 5]
        mine, sx, kx, sy, ky = refs[ahead + 6 : ahead + 11]
        if step:
            place_ref, a_ref, b_ref, factor_ref, accum_ref = refs[:ahead]
            low_ref, half_ref, next_ref, sums_ref, full_ref, total_ref = refs[ahead + 11 :]
            grad = a_ref[...].astype(jnp.float32) + b_ref[...].astype(jnp.float32)
            total = accum_ref[...] + grad * grad
            fresh = factor_ref[...] + step_rate * grad * lax.rsqrt(total)
            full_ref[...] = fresh
            total_ref[...] = total
            low_u = fresh.astype(jnp.bfloat16)
            half_u = (low_u.astype(jnp.float32) * 0.5).astype(jnp.bfloat16)
            low_ref[...] = low_u
            half_ref[...] = half_u
            row = ((place_ref[0] // 2) ^ place_ref[1]) * 16 + (place_ref[0] % 2) * 8
            mine_rows = pl.ds(pl.multiple_of(row, 8), 8)
            next_ref[...] = full_ref[mine_rows, :]
            sums_ref[...] = total_ref[mine_rows, :]
        else:
            low_u, half_u = refs[0][...], refs[1][...]
        middle = start + half
        for at, length, valid in pieces(start, size, [middle, blocks[0].shape[1] // 2], tokens):
            v = gathered(blocks_ref, at, length)
            resid = fresh_residual(half_u, v, lifted(counts_ref[at : at + valid, :]))
            grad = lax.dot_general(
                low_u, resid, (((1,), (1,)), ((), ())), preferred_element_type=jnp.float32
            )
            mine[:, at - start : at - start + length] = grad[:16]
            side = int(at >= middle)
            send, keep = ((sx, kx), (sy, ky))[side]
            first, kept = ((16, 32), (32, 16))[side]
            lo = at - (start, middle)[side]
            here = slice(lo, lo + length)
            send[:16, here] = grad[first : first + 16].astype(jnp.bfloat16)
            send[16:, here] = grad[48:].astype(jnp.bfloat16)
            keep[:, here] = grad[kept : kept + 16]

    shapes = [
        jax.ShapeDtypeStruct((16, size), jnp.float32),
        jax.ShapeDtypeStruct((32, half), jnp.bfloat16),
        jax.ShapeDtypeStruct((16, half), jnp.float32),
        jax.ShapeDtypeStruct((32, half), jnp.bfloat16),
        jax.ShapeDtypeStruct((16, half), jnp.float32),
    ]
    scratch = []
    if step:
        shapes += [jax.ShapeDtypeStruct((64, width), jnp.bfloat16)] * 2
        shapes += [jax.ShapeDtypeStruct((8, width), jnp.float32)] * 2
        scratch = [pltpu.VMEM((64, width), jnp.float32)] * 2
    front = tuple(step) if step else tuple(low)
    return call(
        kernel,
        tuple(shapes),
        front + (*blocks, counts),
        ([scalars] + [whole] * 10) if step else [whole] * 8,
        moved=PASS_COST * size,
        out_specs=(whole,) * len(shapes),
        scratch_shapes=scratch,
    )


def update_token(index, size, mine, parts, factor, accum, before):
    rows, tokens = factor.shape
    half = size // 2
    start = index * CHUNK

    def kernel(mine_ref, rx, ry, qy, qx, factor_ref, accum_ref, *rest):
        next_ref, sums_ref = rest[-2:]
        for side, (wide, thin) in enumerate(((rx, ry), (qy, qx))):
            at = side * half
            valid = min(half, tokens - start - at)
            here = slice(start + at, start + at + valid)
            grad = (
                mine_ref[:, at : at + valid]
                + wide[:16, :valid].astype(jnp.float32)
                + thin[:, :valid].astype(jnp.float32)
            )
            total = accum_ref[:, here] + grad * grad
            sums_ref[:, at : at + valid] = total
            next_ref[:, at : at + valid] = factor_ref[:, here] + step_rate * grad * lax.rsqrt(total)

    block = pl.BlockSpec((rows, CHUNK), lambda i: (0, index))
    extra = () if before is None else tuple(before)
    return call(
        kernel,
        (jax.ShapeDtypeStruct(factor.shape, jnp.float32),) * 2,
        (mine, *parts, factor, accum) + extra,
        [whole] * 7 + [pl.BlockSpec(memory_space=pl.ANY)] * len(extra),
        moved=16 * rows * size,
        grid=(1,),
        out_specs=(block, block),
        input_output_aliases={7: 0, 8: 1} if extra else {},
    )


def shards(counts, u_factor, u_accum, v_factor, v_accum):
    tokens = v_factor.shape[1]
    by_token = counts.T
    place = jnp.stack([lax.axis_index("tok"), lax.axis_index("ten")]).astype(jnp.int32)
    ten = lambda a, bit: swap(a, "ten", bit, 4)
    tok = lambda a, bit: swap(a, "tok", bit, 8)

    padded = -(-tokens // (2 * LANES)) * 2 * LANES
    chunks = [(i, s, min(CHUNK, padded - s)) for i, s in enumerate(range(0, padded, CHUNK))]

    with jax.named_scope("gather_tokens"):
        own = jnp.pad(v_factor.astype(jnp.bfloat16), ((0, 0), (0, padded - tokens)))
        x, y = ten(own, 1), ten(own, 2)
        d0, d1 = x[:, : padded // 2], y[:, padded // 2 :]
        relayed = (d0, d1)
        blocks = (own, x, y, ten(d0, 2), ten(d1, 1))

    with jax.named_scope("gather_tenants"):
        stack = jnp.concatenate([u_factor, u_accum], axis=0)[None]
        for bit in (1, 2, 4):
            stack = jnp.concatenate([stack, tok(stack, bit)], axis=0)
            if bit == 1:
                staged = stage(by_token, stack)
            elif bit == 2:
                stack, staged, _, _ = lax.optimization_barrier((stack, staged, *relayed))
        factor, accum, half_low = order_tenant(place, stack)

    with jax.named_scope("tenant_grad"):
        grad = tenant_grad(half_low, blocks, staged)
        grad = (grad + tok(grad, 1)).astype(jnp.bfloat16)
        grad = grad.astype(jnp.float32) + tok(grad, 2).astype(jnp.float32)
        grad = grad.astype(jnp.bfloat16)

    with jax.named_scope("token_grad"):
        outs, ahead, low, step = None, None, None, (place, grad, tok(grad, 4), factor, accum)
        for index, start, size in chunks:
            made = token_grad(start, size, low, step, blocks, staged)
            mine, sx, kx, sy, ky = made[:5]
            if step:
                low, u_next, u_accum_next, step = made[5:7], made[7], made[8], None
            rx, qy = ten(sx, 1), ten(sy, 2)
            if ahead is not None:
                kx, ky, _, _ = lax.optimization_barrier((kx, ky, *ahead))
            ahead = (
                (kx + rx[16:].astype(jnp.float32)).astype(jnp.bfloat16),
                (ky + qy[16:].astype(jnp.float32)).astype(jnp.bfloat16),
            )
            ry, qx = ten(ahead[0], 2), ten(ahead[1], 1)
            outs = update_token(index, size, mine, (rx, ry, qy, qx), v_factor, v_accum, outs)
    return (u_next, u_accum_next, *outs)


def solution(mesh):
    def program(counts, u_factor, u_accum, v_factor, v_accum):
        rank, tenants = u_factor.shape
        tokens = v_factor.shape[1] // mesh.shape["tok"]
        suits = (
            mesh.shape["ten"] == 4
            and mesh.shape["tok"] == 8
            and rank == 64
            and tenants == 4 * 256
            and tokens % 16 == 0
            and CHUNK < tokens
        )
        return jax.shard_map(
            shards if suits else shards_any,
            mesh=mesh,
            in_specs=(
                P("ten", "tok"),
                P("tok", "ten"),
                P("tok", "ten"),
                P("ten", "tok"),
                P("ten", "tok"),
            ),
            out_specs=(P("tok", "ten"), P("tok", "ten"), P("ten", "tok"), P("ten", "tok")),
            check_vma=False,
        )(counts, u_factor, u_accum, v_factor, v_accum)

    return program
```

time: 82.4 us -> 66.5 us (0.81)
  local copies, waits for them, and re-layouts: 11.4 us -> 0.08 us
  waiting for transfers between devices: 18.1 us -> 13.3 us
  Pallas kernels: 16 us -> 20.4 us
  starting transfers between devices: 33.5 us -> 29.5 us
    unnamed x36 -> x4, local copies, waits for them, and re-layouts: 11.3 us -> 0.01 us
    ppermute x30 -> x22, waiting for transfers between devices: 18.1 us -> 13.3 us  [swap(): return lax.ppermute(a, axis, [(i, i ^ bit) for i in range(size)])]
    pallas_call x11 -> x9, Pallas kernels: 16 us -> 20.4 us  [call(): pl.pallas_call(kernel, out_shape=out_shape, in_specs=in_specs, compiler_p...]
    ppermute x30 -> x22, starting transfers between devices: 33.5 us -> 29.5 us  [swap(): return lax.ppermute(a, axis, [(i, i ^ bit) for i in range(size)])]
    convert_element_type x6 -> x9, other arithmetic: 0.14 us -> 1.41 us  [the longest x1 1.27 us: shards(): own = jnp.pad(v_factor.astype(jnp.bfloat16), ((0, 0), (0, padded - tokens)))]
    another operation x1 -> x0, other arithmetic: 1.27 us -> none  [program(): jax.shard_map(shards if suits else shards_any, mesh=mesh, in_specs=(P('te...]
  transfers between devices with their start and end apart: 30 -> 22, of which waited for: 10 -> 12; matrix products, arithmetic and copies ran while one was open for 2% -> 1% of each run, Pallas kernels for 13% -> 18%
where the time goes in v2:
time: 66.5 us; the launch traced here: 66.3 us
  starting transfers between devices  29.5 us (44%)
  Pallas kernels  20.4 us (31%)
  waiting for transfers between devices  13.3 us (20%)
  other arithmetic  2.22 us (3%)
  between operations  0.76 us (1%)
    ppermute x22, starting transfers between devices, swap(): return lax.ppermute(a, axis, [(i, i ^ bit) for i in range(size)])  29.5 us
    pallas_call x9, Pallas kernels, call(): pl.pallas_call(kernel, out_shape=out_shape, in_specs=in_specs, compiler_p...  20.4 us
    ppermute x22, waiting for transfers between devices, swap(): return lax.ppermute(a, axis, [(i, i ^ bit) for i in range(size)])  13.3 us
  transfers between devices with their start and end apart: 22, of which 12 were waited for; matrix products, arithmetic and copies ran while one was open for 1% of the time, Pallas kernels for 18%

profile of v2, /device:TPU:0, one launch (start us, length us, event | category | flops | bytes accessed | tf_op | source)
XLA Modules:
  0.0 66.3 jit_solution(9649624410875204612)
XLA Ops:
  0.6 1.3 %convert_element_type.53 = bf16[16,16032]{1,0:T(8,128)(2,1)S(1)} convert(f32[16,16032]{1,0:T(8,128)} %factor_ref.5) | non-fusion elementwise | flops 256512 | bytes 1539072 | tf_op jit(solution)/shard_map/gather_tokens/convert_element_type | solution.py:297
  2.0 3.0 %collective-permute-start.3 = (bf16[16,16128]{1,0:T(8,128)(2,1)S(1)}, bf16[16,16128]{1,0:T(8,128)(2,1)S(1)}, u32[]{:S(2)}, u32[]{:S(2)}) collective-permute-start(bf16[16,16128]{1,0:T(8,128)(2,1)S(1)} %pad.4.refs_0_.refs_5_.refs_2_), channel_id=1, source_target_pairs={{0,2},{1,3},{2,0},{3,1},{4,6},{5,7},{6,4},{7,5},{8,10},{9,11},{10,... | collective-permute-start | bytes 1548296 | tf_op jit(solution)/shard_map/gather_tokens/ppermute | solution.py:61
  5.0 1.5 %collective-permute-start.2 = (bf16[16,16128]{1,0:T(8,128)(2,1)S(1)}, bf16[16,16128]{1,0:T(8,128)(2,1)S(1)}, u32[]{:S(2)}, u32[]{:S(2)}) collective-permute-start(bf16[16,16128]{1,0:T(8,128)(2,1)S(1)} %pad.4.refs_0_.refs_5_.refs_2_), channel_id=1, source_target_pairs={{0,1},{1,0},{2,3},{3,2},{4,5},{5,4},{6,7},{7,6},{8,9},{9,8},{10,11... | collective-permute-start | bytes 1548296 | tf_op jit(solution)/shard_map/gather_tokens/ppermute | solution.py:61
  7.2 1.2 %collective-permute-done = f32[1,16,256]{2,1,0:T(8,128)S(1)} collective-permute-done((f32[1,16,256]{2,1,0:T(8,128)S(1)}, f32[1,16,256]{2,1,0:T(8,128)S(1)}, u32[]{:S(2)}, u32[]{:S(2)}) %collective-permute-start) | collective-permute-done | bytes 16416 | tf_op jit(solution)/shard_map/gather_tenants/ppermute | solution.py:61
  8.4 1.6 %collective-permute-start.1 = (f32[2,16,256]{2,1,0:T(8,128)S(1)}, f32[2,16,256]{2,1,0:T(8,128)S(1)}, u32[]{:S(2)}, u32[]{:S(2)}) collective-permute-start(f32[2,16,256]{2,1,0:T(8,128)S(1)} %pad_maximum_fusion.2.after_ref), channel_id=1, source_target_pairs={{0,8},{4,12},{8,0},{12,4},{16,24},{20,28},{24,16},{28,20},{1,9},{5... | collective-permute-start | bytes 98312 | tf_op jit(solution)/shard_map/gather_tenants/ppermute | solution.py:61
  10.0 5.8 %gather_tenants.2.refs_5_.refs_10_.refs_7_ = s32[16032,256]{1,0:T(8,128)S(1)} custom-call(s32[16032,256]{1,0:T(8,128)} %bitcast.5, f32[2,16,256]{2,1,0:T(8,128)S(1)} %pad_maximum_fusion.2.after_ref), custom_call_target="tpu_custom_call" | custom-call | bytes 32833536 | tf_op jit(solution)/shard_map/gather_tenants/pallas_call | solution.py:65
  15.7 1.0 %collective-permute-done.3.refs_2_.refs_7_.refs_4_ = bf16[16,16128]{1,0:T(8,128)(2,1)S(1)} collective-permute-done((bf16[16,16128]{1,0:T(8,128)(2,1)S(1)}, bf16[16,16128]{1,0:T(8,128)(2,1)S(1)}, u32[]{:S(2)}, u32[]{:S(2)}) %collective-permute-start.3) | collective-permute-done | bytes 516128 | tf_op jit(solution)/shard_map/gather_tokens/ppermute | solution.py:61
  16.8 1.8 %collective-permute-start.6 = (bf16[16,8064]{1,0:T(8,128)(2,1)S(1)}, bf16[16,8064]{1,0:T(8,128)(2,1)S(1)}, u32[]{:S(2)}, u32[]{:S(2)}) collective-permute-start(bf16[16,8064]{1,0:T(8,128)(2,1)S(1)} %slice.33), channel_id=1, source_target_pairs={{0,1},{1,0},{2,3},{3,2},{4,5},{5,4},{6,7},{7,6},{8,9},{9,8},{10,11... | collective-permute-start | bytes 774152 | tf_op jit(solution)/shard_map/gather_tokens/ppermute | solution.py:61
  18.6 1.6 %collective-permute-start.5 = (bf16[16,8064]{1,0:T(8,128)(2,1)S(1)}, bf16[16,8064]{1,0:T(8,128)(2,1)S(1)}, u32[]{:S(2)}, u32[]{:S(2)}) collective-permute-start(bf16[16,8064]{1,0:T(8,128)(2,1)S(1)} %slice.32), channel_id=1, source_target_pairs={{0,2},{1,3},{2,0},{3,1},{4,6},{5,7},{6,4},{7,5},{8,10},{9,11},{10,... | collective-permute-start | bytes 774152 | tf_op jit(solution)/shard_map/gather_tokens/ppermute | solution.py:61
  20.2 2.7 %collective-permute-start.4 = (f32[4,16,256]{2,1,0:T(8,128)S(1)}, f32[4,16,256]{2,1,0:T(8,128)S(1)}, u32[]{:S(2)}, u32[]{:S(2)}) collective-permute-start(f32[4,16,256]{2,1,0:T(8,128)S(1)} %pad_maximum_fusion.1), channel_id=1, source_target_pairs={{0,16},{4,20},{8,24},{12,28},{16,0},{20,4},{24,8},{28,12},{1,17},{... | collective-permute-start | bytes 196616 | tf_op jit(solution)/shard_map/gather_tenants/ppermute | solution.py:61
  22.9 2.5 %collective-permute-done.4 = f32[4,16,256]{2,1,0:T(8,128)S(1)} collective-permute-done((f32[4,16,256]{2,1,0:T(8,128)S(1)}, f32[4,16,256]{2,1,0:T(8,128)S(1)}, u32[]{:S(2)}, u32[]{:S(2)}) %collective-permute-start.4) | collective-permute-done | bytes 65568 | tf_op jit(solution)/shard_map/gather_tenants/ppermute | solution.py:61
  26.0 4.7 %tenant_grad.1 = f32[64,256]{1,0:T(8,128)S(1)} custom-call(bf16[64,256]{1,0:T(8,128)(2,1)S(1)} %get-tuple-element.39.half_ref, bf16[16,16128]{1,0:T(8,128)(2,1)S(1)} %pad.4.refs_0_.refs_5_.refs_2_, bf16[16,16128]{1,0:T(8,128)(2,1)S(1)} %collective-permute-done.2.refs_1_.refs_6_.refs_3_, bf16[16,16128]{1,0:T(8,128)(2,1)S(1)} %collective-permute-done.3.refs_2_.refs_7_.refs_4_, ...), custom_call_target="tpu_custom_call" | custom-call | bytes 1032192 | tf_op jit(solution)/shard_map/tenant_grad/pallas_call | solution.py:65
  30.8 1.2 %collective-permute-done.7 = f32[64,256]{1,0:T(8,128)S(1)} collective-permute-done((f32[64,256]{1,0:T(8,128)S(1)}, f32[64,256]{1,0:T(8,128)S(1)}, u32[]{:S(2)}, u32[]{:S(2)}) %collective-permute-start.7) | collective-permute-done | bytes 65568 | tf_op jit(solution)/shard_map/tenant_grad/ppermute | solution.py:61
  32.1 1.6 %collective-permute-start.8 = (bf16[64,256]{1,0:T(8,128)(2,1)S(1)}, bf16[64,256]{1,0:T(8,128)(2,1)S(1)}, u32[]{:S(2)}, u32[]{:S(2)}) collective-permute-start(bf16[64,256]{1,0:T(8,128)(2,1)S(1)} %add_convert_fusion.7), channel_id=1, source_target_pairs={{0,8},{4,12},{8,0},{12,4},{16,24},{20,28},{24,16},{28,20},{1,9},{5... | collective-permute-start | bytes 98312 | tf_op jit(solution)/shard_map/tenant_grad/ppermute | solution.py:61
  33.7 2.3 %collective-permute-done.8 = bf16[64,256]{1,0:T(8,128)(2,1)S(1)} collective-permute-done((bf16[64,256]{1,0:T(8,128)(2,1)S(1)}, bf16[64,256]{1,0:T(8,128)(2,1)S(1)}, u32[]{:S(2)}, u32[]{:S(2)}) %collective-permute-start.8) | collective-permute-done | bytes 32800 | tf_op jit(solution)/shard_map/tenant_grad/ppermute | solution.py:61
  36.1 2.8 %collective-permute-start.9 = (bf16[64,256]{1,0:T(8,128)(2,1)S(1)}, bf16[64,256]{1,0:T(8,128)(2,1)S(1)}, u32[]{:S(2)}, u32[]{:S(2)}) collective-permute-start(bf16[64,256]{1,0:T(8,128)(2,1)S(1)} %add_convert_fusion.6.refs_1_), channel_id=1, source_target_pairs={{0,16},{4,20},{8,24},{12,28},{16,0},{20,4},{24,8},{28,12},{1,17},{... | collective-permute-start | bytes 98312 | tf_op jit(solution)/shard_map/token_grad/ppermute | solution.py:61
  38.9 2.1 %collective-permute-done.9.refs_2_ = bf16[64,256]{1,0:T(8,128)(2,1)S(1)} collective-permute-done((bf16[64,256]{1,0:T(8,128)(2,1)S(1)}, bf16[64,256]{1,0:T(8,128)(2,1)S(1)}, u32[]{:S(2)}, u32[]{:S(2)}) %collective-permute-start.9) | collective-permute-done | bytes 32800 | tf_op jit(solution)/shard_map/token_grad/ppermute | solution.py:61
  40.9 2.8 %token_grad.6 = (f32[16,5376]{1,0:T(8,128)S(1)}, bf16[32,2688]{1,0:T(8,128)(2,1)S(1)}, f32[16,2688]{1,0:T(8,128)S(1)}, bf16[32,2688]{1,0:T(8,128)(2,1)S(1)}, f32...) custom-call(s32[2]{0:T(128)S(1)} %pad_add_fusion.place_ref.refs_0_, ...), custom_call_target="tpu_custom_call" | custom-call | bytes 344064 | tf_op jit(solution)/shard_map/token_grad/pallas_call | solution.py:65
  44.3 1.1 %collective-permute-start.12 = (bf16[32,2688]{1,0:T(8,128)(2,1)S(1)}, bf16[32,2688]{1,0:T(8,128)(2,1)S(1)}, u32[]{:S(2)}, u32[]{:S(2)}) collective-permute-start(bf16[32,2688]{1,0:T(8,128)(2,1)S(1)} %get-tuple-element.56), channel_id=1, source_target_pairs={{0,2},{1,3},{2,0},{3,1},{4,6},{5,7},{6,4},{7,5},{8,10},{9,11},{10,... | collective-permute-start | bytes 516104 | tf_op jit(solution)/shard_map/token_grad/ppermute | solution.py:61
  45.4 1.8 %token_grad.8 = (f32[16,5376]{1,0:T(8,128)S(1)}, bf16[32,2688]{1,0:T(8,128)(2,1)S(1)}, f32[16,2688]{1,0:T(8,128)S(1)}, bf16[32,2688]{1,0:T(8,128)(2,1)S(1)}, f32[16,2688]{1,0:T(8,128)S(1)}) custom-call(bf16[64,256]{1,0:T(8,128)(2,1)S(1)} %get-tuple-element.45.refs_0_, bf16[64,256]{1,0:T(8,128)(2,1)S(1)} %get-tuple-element.46.refs_1_, ...), custom_call_target="tpu_custom_call" | custom-call | bytes 344064 | tf_op jit(solution)/shard_map/token_grad/pallas_call | solution.py:65
  47.3 1.4 %collective-permute-start.13 = (bf16[32,2688]{1,0:T(8,128)(2,1)S(1)}, bf16[32,2688]{1,0:T(8,128)(2,1)S(1)}, u32[]{:S(2)}, u32[]{:S(2)}) collective-permute-start(bf16[32,2688]{1,0:T(8,128)(2,1)S(1)} %get-tuple-element.58), channel_id=1, source_target_pairs={{0,1},{1,0},{2,3},{3,2},{4,5},{5,4},{6,7},{7,6},{8,9},{9,8},{10,11... | collective-permute-start | bytes 516104 | tf_op jit(solution)/shard_map/token_grad/ppermute | solution.py:61
  48.6 1.1 %collective-permute-start.14 = (bf16[32,2688]{1,0:T(8,128)(2,1)S(1)}, bf16[32,2688]{1,0:T(8,128)(2,1)S(1)}, u32[]{:S(2)}, u32[]{:S(2)}) collective-permute-start(bf16[32,2688]{1,0:T(8,128)(2,1)S(1)} %get-tuple-element.60), channel_id=1, source_target_pairs={{0,2},{1,3},{2,0},{3,1},{4,6},{5,7},{6,4},{7,5},{8,10},{9,11},{10,... | collective-permute-start | bytes 516104 | tf_op jit(solution)/shard_map/token_grad/ppermute | solution.py:61
  49.7 1.8 %token_grad.7 = (f32[16,5376]{1,0:T(8,128)S(1)}, bf16[32,2688]{1,0:T(8,128)(2,1)S(1)}, f32[16,2688]{1,0:T(8,128)S(1)}, bf16[32,2688]{1,0:T(8,128)(2,1)S(1)}, f32[16,2688]{1,0:T(8,128)S(1)}) custom-call(bf16[64,256]{1,0:T(8,128)(2,1)S(1)} %get-tuple-element.45.refs_0_, bf16[64,256]{1,0:T(8,128)(2,1)S(1)} %get-tuple-element.46.refs_1_, ...), custom_call_target="tpu_custom_call" | custom-call | bytes 344064 | tf_op jit(solution)/shard_map/token_grad/pallas_call | solution.py:65
  52.1 1.1 %collective-permute-start.16 = (bf16[32,2688]{1,0:T(8,128)(2,1)S(1)}, bf16[32,2688]{1,0:T(8,128)(2,1)S(1)}, u32[]{:S(2)}, u32[]{:S(2)}) collective-permute-start(bf16[32,2688]{1,0:T(8,128)(2,1)S(1)} %get-tuple-element.62), channel_id=1, source_target_pairs={{0,2},{1,3},{2,0},{3,1},{4,6},{5,7},{6,4},{7,5},{8,10},{9,11},{10,... | collective-permute-start | bytes 516104 | tf_op jit(solution)/shard_map/token_grad/ppermute | solution.py:61
  53.3 1.0 %collective-permute-start.20 = (bf16[16,2688]{1,0:T(8,128)(2,1)S(1)}, bf16[16,2688]{1,0:T(8,128)(2,1)S(1)}, u32[]{:S(2)}, u32[]{:S(2)}) collective-permute-start(bf16[16,2688]{1,0:T(8,128)(2,1)S(1)} %add_convert_fusion.5), channel_id=1, source_target_pairs={{0,2},{1,3},{2,0},{3,1},{4,6},{5,7},{6,4},{7,5},{8,10},{9,11},{10,... | collective-permute-start | bytes 258056 | tf_op jit(solution)/shard_map/token_grad/ppermute | solution.py:61
  54.5 1.4 %collective-permute-start.21 = (bf16[16,2688]{1,0:T(8,128)(2,1)S(1)}, bf16[16,2688]{1,0:T(8,128)(2,1)S(1)}, u32[]{:S(2)}, u32[]{:S(2)}) collective-permute-start(bf16[16,2688]{1,0:T(8,128)(2,1)S(1)} %add_convert_fusion.4), channel_id=1, source_target_pairs={{0,1},{1,0},{2,3},{3,2},{4,5},{5,4},{6,7},{7,6},{8,9},{9,8},{10,11... | collective-permute-start | bytes 258056 | tf_op jit(solution)/shard_map/token_grad/ppermute | solution.py:61
  56.0 1.1 %collective-permute-start.18 = (bf16[16,2688]{1,0:T(8,128)(2,1)S(1)}, bf16[16,2688]{1,0:T(8,128)(2,1)S(1)}, u32[]{:S(2)}, u32[]{:S(2)}) collective-permute-start(bf16[16,2688]{1,0:T(8,128)(2,1)S(1)} %add_convert_fusion.3), channel_id=1, source_target_pairs={{0,2},{1,3},{2,0},{3,1},{4,6},{5,7},{6,4},{7,5},{8,10},{9,11},{10,... | collective-permute-start | bytes 258056 | tf_op jit(solution)/shard_map/token_grad/ppermute | solution.py:61
  57.5 1.1 %collective-permute-start.19 = (bf16[16,2688]{1,0:T(8,128)(2,1)S(1)}, bf16[16,2688]{1,0:T(8,128)(2,1)S(1)}, u32[]{:S(2)}, u32[]{:S(2)}) collective-permute-start(bf16[16,2688]{1,0:T(8,128)(2,1)S(1)} %add_convert_fusion.2), channel_id=1, source_target_pairs={{0,1},{1,0},{2,3},{3,2},{4,5},{5,4},{6,7},{7,6},{8,9},{9,8},{10,11... | collective-permute-start | bytes 258056 | tf_op jit(solution)/shard_map/token_grad/ppermute | solution.py:61
  58.6 1.1 %collective-permute-done.16.qy = bf16[32,2688]{1,0:T(8,128)(2,1)S(1)} collective-permute-done((bf16[32,2688]{1,0:T(8,128)(2,1)S(1)}, bf16[32,2688]{1,0:T(8,128)(2,1)S(1)}, u32[]{:S(2)}, u32[]{:S(2)}) %collective-permute-start.16) | collective-permute-done | bytes 172064 | tf_op jit(solution)/shard_map/token_grad/ppermute | solution.py:61
  59.6 1.1 %collective-permute-start.15 = (bf16[16,2688]{1,0:T(8,128)(2,1)S(1)}, bf16[16,2688]{1,0:T(8,128)(2,1)S(1)}, u32[]{:S(2)}, u32[]{:S(2)}) collective-permute-start(bf16[16,2688]{1,0:T(8,128)(2,1)S(1)} %add_convert_fusion.1), channel_id=1, source_target_pairs={{0,2},{1,3},{2,0},{3,1},{4,6},{5,7},{6,4},{7,5},{8,10},{9,11},{10,... | collective-permute-start | bytes 258056 | tf_op jit(solution)/shard_map/token_grad/ppermute | solution.py:61
  60.8 1.4 %collective-permute-start.17 = (bf16[16,2688]{1,0:T(8,128)(2,1)S(1)}, bf16[16,2688]{1,0:T(8,128)(2,1)S(1)}, u32[]{:S(2)}, u32[]{:S(2)}) collective-permute-start(bf16[16,2688]{1,0:T(8,128)(2,1)S(1)} %add_convert_fusion), channel_id=1, source_target_pairs={{0,1},{1,0},{2,3},{3,2},{4,5},{5,4},{6,7},{7,6},{8,9},{9,8},{10,11... | collective-permute-start | bytes 258056 | tf_op jit(solution)/shard_map/token_grad/ppermute | solution.py:61
  64.2 1.1 %collective-permute-done.17.qx = bf16[16,2688]{1,0:T(8,128)(2,1)S(1)} collective-permute-done((bf16[16,2688]{1,0:T(8,128)(2,1)S(1)}, bf16[16,2688]{1,0:T(8,128)(2,1)S(1)}, u32[]{:S(2)}, u32[]{:S(2)}) %collective-permute-start.17) | collective-permute-done | bytes 86048 | tf_op jit(solution)/shard_map/token_grad/ppermute | solution.py:61
  (42 shorter events, 6.5 us)
Async XLA Ops:
  2.0 14.8 %collective-permute-start.3 = (bf16[16,16128]{1,0:T(8,128)(2,1)S(1)}, bf16[16,16128]{1,0:T(8,128)(2,1)S(1)}, u32[]{:S(2)}, u32[]{:S(2)}) collective-permute-start(bf16[16,16128]{1,0:T(8,128)(2,1)S(1)} %pad.4.refs_0_.refs_5_.refs_2_), channel_id=1, source_target_pairs={{0,2},{1,3},{2,0},{3,1},{4,6},{5,7},{6,4},{7,5},{8,10},{9,11},{10,... | collective-permute-start | bytes 1548296 | tf_op jit(solution)/shard_map/gather_tokens/ppermute | solution.py:61
  5.0 13.5 %collective-permute-start.2 = (bf16[16,16128]{1,0:T(8,128)(2,1)S(1)}, bf16[16,16128]{1,0:T(8,128)(2,1)S(1)}, u32[]{:S(2)}, u32[]{:S(2)}) collective-permute-start(bf16[16,16128]{1,0:T(8,128)(2,1)S(1)} %pad.4.refs_0_.refs_5_.refs_2_), channel_id=1, source_target_pairs={{0,1},{1,0},{2,3},{3,2},{4,5},{5,4},{6,7},{7,6},{8,9},{9,8},{10,11... | collective-permute-start | bytes 1548296 | tf_op jit(solution)/shard_map/gather_tokens/ppermute | solution.py:61
  7.2 1.2 %collective-permute-start = (f32[1,16,256]{2,1,0:T(8,128)S(1)}, f32[1,16,256]{2,1,0:T(8,128)S(1)}, u32[]{:S(2)}, u32[]{:S(2)}) collective-permute-start(f32[1,16,256]{2,1,0:T(8,128)S(1)} %maximum_bitcast_fusion), channel_id=1, source_target_pairs={{0,4},{4,0},{8,12},{12,8},{16,20},{20,16},{24,28},{28,24},{1,5},{5... | collective-permute-start | bytes 49160 | tf_op jit(solution)/shard_map/gather_tenants/ppermute | solution.py:61
  8.4 11.8 %collective-permute-start.1 = (f32[2,16,256]{2,1,0:T(8,128)S(1)}, f32[2,16,256]{2,1,0:T(8,128)S(1)}, u32[]{:S(2)}, u32[]{:S(2)}) collective-permute-start(f32[2,16,256]{2,1,0:T(8,128)S(1)} %pad_maximum_fusion.2.after_ref), channel_id=1, source_target_pairs={{0,8},{4,12},{8,0},{12,4},{16,24},{20,28},{24,16},{28,20},{1,9},{5... | collective-permute-start | bytes 98312 | tf_op jit(solution)/shard_map/gather_tenants/ppermute | solution.py:61
  16.8 9.2 %collective-permute-start.6 = (bf16[16,8064]{1,0:T(8,128)(2,1)S(1)}, bf16[16,8064]{1,0:T(8,128)(2,1)S(1)}, u32[]{:S(2)}, u32[]{:S(2)}) collective-permute-start(bf16[16,8064]{1,0:T(8,128)(2,1)S(1)} %slice.33), channel_id=1, source_target_pairs={{0,1},{1,0},{2,3},{3,2},{4,5},{5,4},{6,7},{7,6},{8,9},{9,8},{10,11... | collective-permute-start | bytes 774152 | tf_op jit(solution)/shard_map/gather_tokens/ppermute | solution.py:61
  18.6 7.4 %collective-permute-start.5 = (bf16[16,8064]{1,0:T(8,128)(2,1)S(1)}, bf16[16,8064]{1,0:T(8,128)(2,1)S(1)}, u32[]{:S(2)}, u32[]{:S(2)}) collective-permute-start(bf16[16,8064]{1,0:T(8,128)(2,1)S(1)} %slice.32), channel_id=1, source_target_pairs={{0,2},{1,3},{2,0},{3,1},{4,6},{5,7},{6,4},{7,5},{8,10},{9,11},{10,... | collective-permute-start | bytes 774152 | tf_op jit(solution)/shard_map/gather_tokens/ppermute | solution.py:61
  20.2 5.2 %collective-permute-start.4 = (f32[4,16,256]{2,1,0:T(8,128)S(1)}, f32[4,16,256]{2,1,0:T(8,128)S(1)}, u32[]{:S(2)}, u32[]{:S(2)}) collective-permute-start(f32[4,16,256]{2,1,0:T(8,128)S(1)} %pad_maximum_fusion.1), channel_id=1, source_target_pairs={{0,16},{4,20},{8,24},{12,28},{16,0},{20,4},{24,8},{28,12},{1,17},{... | collective-permute-start | bytes 196616 | tf_op jit(solution)/shard_map/gather_tenants/ppermute | solution.py:61
  30.7 1.3 %collective-permute-start.7 = (f32[64,256]{1,0:T(8,128)S(1)}, f32[64,256]{1,0:T(8,128)S(1)}, u32[]{:S(2)}, u32[]{:S(2)}) collective-permute-start(f32[64,256]{1,0:T(8,128)S(1)} %tenant_grad.1), channel_id=1, source_target_pairs={{0,4},{4,0},{8,12},{12,8},{16,20},{20,16},{24,28},{28,24},{1,5},{5... | collective-permute-start | bytes 196616 | tf_op jit(solution)/shard_map/tenant_grad/ppermute | solution.py:61
  32.1 4.0 %collective-permute-start.8 = (bf16[64,256]{1,0:T(8,128)(2,1)S(1)}, bf16[64,256]{1,0:T(8,128)(2,1)S(1)}, u32[]{:S(2)}, u32[]{:S(2)}) collective-permute-start(bf16[64,256]{1,0:T(8,128)(2,1)S(1)} %add_convert_fusion.7), channel_id=1, source_target_pairs={{0,8},{4,12},{8,0},{12,4},{16,24},{20,28},{24,16},{28,20},{1,9},{5... | collective-permute-start | bytes 98312 | tf_op jit(solution)/shard_map/tenant_grad/ppermute | solution.py:61
  36.1 4.9 %collective-permute-start.9 = (bf16[64,256]{1,0:T(8,128)(2,1)S(1)}, bf16[64,256]{1,0:T(8,128)(2,1)S(1)}, u32[]{:S(2)}, u32[]{:S(2)}) collective-permute-start(bf16[64,256]{1,0:T(8,128)(2,1)S(1)} %add_convert_fusion.6.refs_1_), channel_id=1, source_target_pairs={{0,16},{4,20},{8,24},{12,28},{16,0},{20,4},{24,8},{28,12},{1,17},{... | collective-permute-start | bytes 98312 | tf_op jit(solution)/shard_map/token_grad/ppermute | solution.py:61
  43.8 8.4 %collective-permute-start.11 = (bf16[32,2688]{1,0:T(8,128)(2,1)S(1)}, bf16[32,2688]{1,0:T(8,128)(2,1)S(1)}, u32[]{:S(2)}, u32[]{:S(2)}) collective-permute-start(bf16[32,2688]{1,0:T(8,128)(2,1)S(1)} %get-tuple-element.54), channel_id=1, source_target_pairs={{0,1},{1,0},{2,3},{3,2},{4,5},{5,4},{6,7},{7,6},{8,9},{9,8},{10,11... | collective-permute-start | bytes 516104 | tf_op jit(solution)/shard_map/token_grad/ppermute | solution.py:61
  44.3 8.9 %collective-permute-start.12 = (bf16[32,2688]{1,0:T(8,128)(2,1)S(1)}, bf16[32,2688]{1,0:T(8,128)(2,1)S(1)}, u32[]{:S(2)}, u32[]{:S(2)}) collective-permute-start(bf16[32,2688]{1,0:T(8,128)(2,1)S(1)} %get-tuple-element.56), channel_id=1, source_target_pairs={{0,2},{1,3},{2,0},{3,1},{4,6},{5,7},{6,4},{7,5},{8,10},{9,11},{10,... | collective-permute-start | bytes 516104 | tf_op jit(solution)/shard_map/token_grad/ppermute | solution.py:61
  45.4 16.8 %copy-start = (f32[16,16032]{1,0:T(8,128)S(1)}, f32[16,16032]{1,0:T(8,128)}, u32[]{:S(2)}) copy-start(f32[16,16032]{1,0:T(8,128)} %factor_ref.5) | copy-start | bytes 3078148
  45.4 16.8 %copy-start.1 = (f32[16,16032]{1,0:T(8,128)S(1)}, f32[16,16032]{1,0:T(8,128)}, u32[]{:S(2)}) copy-start(f32[16,16032]{1,0:T(8,128)} %accum_ref.5) | copy-start | bytes 3078148
  47.3 7.2 %collective-permute-start.13 = (bf16[32,2688]{1,0:T(8,128)(2,1)S(1)}, bf16[32,2688]{1,0:T(8,128)(2,1)S(1)}, u32[]{:S(2)}, u32[]{:S(2)}) collective-permute-start(bf16[32,2688]{1,0:T(8,128)(2,1)S(1)} %get-tuple-element.58), channel_id=1, source_target_pairs={{0,1},{1,0},{2,3},{3,2},{4,5},{5,4},{6,7},{7,6},{8,9},{9,8},{10,11... | collective-permute-start | bytes 516104 | tf_op jit(solution)/shard_map/token_grad/ppermute | solution.py:61
  48.6 7.3 %collective-permute-start.14 = (bf16[32,2688]{1,0:T(8,128)(2,1)S(1)}, bf16[32,2688]{1,0:T(8,128)(2,1)S(1)}, u32[]{:S(2)}, u32[]{:S(2)}) collective-permute-start(bf16[32,2688]{1,0:T(8,128)(2,1)S(1)} %get-tuple-element.60), channel_id=1, source_target_pairs={{0,2},{1,3},{2,0},{3,1},{4,6},{5,7},{6,4},{7,5},{8,10},{9,11},{10,... | collective-permute-start | bytes 516104 | tf_op jit(solution)/shard_map/token_grad/ppermute | solution.py:61
  51.5 6.0 %collective-permute-start.10 = (bf16[32,2688]{1,0:T(8,128)(2,1)S(1)}, bf16[32,2688]{1,0:T(8,128)(2,1)S(1)}, u32[]{:S(2)}, u32[]{:S(2)}) collective-permute-start(bf16[32,2688]{1,0:T(8,128)(2,1)S(1)} %get-tuple-element.48), channel_id=1, source_target_pairs={{0,1},{1,0},{2,3},{3,2},{4,5},{5,4},{6,7},{7,6},{8,9},{9,8},{10,11... | collective-permute-start | bytes 516104 | tf_op jit(solution)/shard_map/token_grad/ppermute | solution.py:61
  52.1 7.5 %collective-permute-start.16 = (bf16[32,2688]{1,0:T(8,128)(2,1)S(1)}, bf16[32,2688]{1,0:T(8,128)(2,1)S(1)}, u32[]{:S(2)}, u32[]{:S(2)}) collective-permute-start(bf16[32,2688]{1,0:T(8,128)(2,1)S(1)} %get-tuple-element.62), channel_id=1, source_target_pairs={{0,2},{1,3},{2,0},{3,1},{4,6},{5,7},{6,4},{7,5},{8,10},{9,11},{10,... | collective-permute-start | bytes 516104 | tf_op jit(solution)/shard_map/token_grad/ppermute | solution.py:61
  53.3 7.5 %collective-permute-start.20 = (bf16[16,2688]{1,0:T(8,128)(2,1)S(1)}, bf16[16,2688]{1,0:T(8,128)(2,1)S(1)}, u32[]{:S(2)}, u32[]{:S(2)}) collective-permute-start(bf16[16,2688]{1,0:T(8,128)(2,1)S(1)} %add_convert_fusion.5), channel_id=1, source_target_pairs={{0,2},{1,3},{2,0},{3,1},{4,6},{5,7},{6,4},{7,5},{8,10},{9,11},{10,... | collective-permute-start | bytes 258056 | tf_op jit(solution)/shard_map/token_grad/ppermute | solution.py:61
  54.5 7.8 %collective-permute-start.21 = (bf16[16,2688]{1,0:T(8,128)(2,1)S(1)}, bf16[16,2688]{1,0:T(8,128)(2,1)S(1)}, u32[]{:S(2)}, u32[]{:S(2)}) collective-permute-start(bf16[16,2688]{1,0:T(8,128)(2,1)S(1)} %add_convert_fusion.4), channel_id=1, source_target_pairs={{0,1},{1,0},{2,3},{3,2},{4,5},{5,4},{6,7},{7,6},{8,9},{9,8},{10,11... | collective-permute-start | bytes 258056 | tf_op jit(solution)/shard_map/token_grad/ppermute | solution.py:61
  56.0 7.2 %collective-permute-start.18 = (bf16[16,2688]{1,0:T(8,128)(2,1)S(1)}, bf16[16,2688]{1,0:T(8,128)(2,1)S(1)}, u32[]{:S(2)}, u32[]{:S(2)}) collective-permute-start(bf16[16,2688]{1,0:T(8,128)(2,1)S(1)} %add_convert_fusion.3), channel_id=1, source_target_pairs={{0,2},{1,3},{2,0},{3,1},{4,6},{5,7},{6,4},{7,5},{8,10},{9,11},{10,... | collective-permute-start | bytes 258056 | tf_op jit(solution)/shard_map/token_grad/ppermute | solution.py:61
  57.5 5.7 %collective-permute-start.19 = (bf16[16,2688]{1,0:T(8,128)(2,1)S(1)}, bf16[16,2688]{1,0:T(8,128)(2,1)S(1)}, u32[]{:S(2)}, u32[]{:S(2)}) collective-permute-start(bf16[16,2688]{1,0:T(8,128)(2,1)S(1)} %add_convert_fusion.2), channel_id=1, source_target_pairs={{0,1},{1,0},{2,3},{3,2},{4,5},{5,4},{6,7},{7,6},{8,9},{9,8},{10,11... | collective-permute-start | bytes 258056 | tf_op jit(solution)/shard_map/token_grad/ppermute | solution.py:61
  59.6 4.5 %collective-permute-start.15 = (bf16[16,2688]{1,0:T(8,128)(2,1)S(1)}, bf16[16,2688]{1,0:T(8,128)(2,1)S(1)}, u32[]{:S(2)}, u32[]{:S(2)}) collective-permute-start(bf16[16,2688]{1,0:T(8,128)(2,1)S(1)} %add_convert_fusion.1), channel_id=1, source_target_pairs={{0,2},{1,3},{2,0},{3,1},{4,6},{5,7},{6,4},{7,5},{8,10},{9,11},{10,... | collective-permute-start | bytes 258056 | tf_op jit(solution)/shard_map/token_grad/ppermute | solution.py:61
  60.8 4.5 %collective-permute-start.17 = (bf16[16,2688]{1,0:T(8,128)(2,1)S(1)}, bf16[16,2688]{1,0:T(8,128)(2,1)S(1)}, u32[]{:S(2)}, u32[]{:S(2)}) collective-permute-start(bf16[16,2688]{1,0:T(8,128)(2,1)S(1)} %add_convert_fusion), channel_id=1, source_target_pairs={{0,1},{1,0},{2,3},{3,2},{4,5},{5,4},{6,7},{7,6},{8,9},{9,8},{10,11... | collective-permute-start | bytes 258056 | tf_op jit(solution)/shard_map/token_grad/ppermute | solution.py:61

commit v3 on v2

--- a/solution.py
+++ b/solution.py
@@ -8,7 +8,8 @@
 weight_scale = 0.5
 step_rate = 0.3
 LANES = 128
-CHUNK = 5376
+CHUNKS = (5376, 5376)
+GROUP = sum(CHUNKS)
 INNER = 1024
 PASS_COST = 64
 HBM_SIDE_LIMIT = 34 * 2**20
@@ -182,30 +183,27 @@
     )
 
 
-def token_grad(start, size, low, step, blocks, counts):
+def token_grad(start, size, low, step, blocks, counts, after):
     tokens, width = counts.shape
     half = size // 2
     ahead = len(step) if step else 2
 
     def kernel(*refs):
+        refs = refs if after is None else refs[1:]
         blocks_ref, counts_ref = refs[ahead : ahead + 5], refs[ahead + 5]
         mine, sx, kx, sy, ky = refs[ahead + 6 : ahead + 11]
         if step:
-            place_ref, a_ref, b_ref, factor_ref, accum_ref = refs[:ahead]
-            low_ref, half_ref, next_ref, sums_ref, full_ref, total_ref = refs[ahead + 11 :]
+            a_ref, b_ref, factor_ref, accum_ref = refs[:ahead]
+            low_ref, half_ref, next_ref, sums_ref = refs[ahead + 11 :]
             grad = a_ref[...].astype(jnp.float32) + b_ref[...].astype(jnp.float32)
             total = accum_ref[...] + grad * grad
             fresh = factor_ref[...] + step_rate * grad * lax.rsqrt(total)
-            full_ref[...] = fresh
-            total_ref[...] = total
+            next_ref[...] = fresh
+            sums_ref[...] = total
             low_u = fresh.astype(jnp.bfloat16)
             half_u = (low_u.astype(jnp.float32) * 0.5).astype(jnp.bfloat16)
             low_ref[...] = low_u
             half_ref[...] = half_u
-            row = ((place_ref[0] // 2) ^ place_ref[1]) * 16 + (place_ref[0] % 2) * 8
-            mine_rows = pl.ds(pl.multiple_of(row, 8), 8)
-            next_ref[...] = full_ref[mine_rows, :]
-            sums_ref[...] = total_ref[mine_rows, :]
         else:
             low_u, half_u = refs[0][...], refs[1][...]
         middle = start + half
@@ -232,54 +230,71 @@
         jax.ShapeDtypeStruct((32, half), jnp.bfloat16),
         jax.ShapeDtypeStruct((16, half), jnp.float32),
     ]
-    scratch = []
     if step:
         shapes += [jax.ShapeDtypeStruct((64, width), jnp.bfloat16)] * 2
-        shapes += [jax.ShapeDtypeStruct((8, width), jnp.float32)] * 2
-        scratch = [pltpu.VMEM((64, width), jnp.float32)] * 2
+        shapes += [jax.ShapeDtypeStruct((64, width), jnp.float32)] * 2
     front = tuple(step) if step else tuple(low)
     return call(
         kernel,
         tuple(shapes),
-        front + (*blocks, counts),
-        ([scalars] + [whole] * 10) if step else [whole] * 8,
+        (() if after is None else (after,)) + front + (*blocks, counts),
+        [pl.BlockSpec(memory_space=pl.ANY)] * (after is not None) + [whole] * (10 if step else 8),
         moved=PASS_COST * size,
         out_specs=(whole,) * len(shapes),
-        scratch_shapes=scratch,
-    )
-
-
-def update_token(index, size, mine, parts, factor, accum, before):
+    )
+
+
+def update_token(index, group, made, relayed, factor, accum, before, tenant):
     rows, tokens = factor.shape
-    half = size // 2
-    start = index * CHUNK
-
-    def kernel(mine_ref, rx, ry, qy, qx, factor_ref, accum_ref, *rest):
-        next_ref, sums_ref = rest[-2:]
-        for side, (wide, thin) in enumerate(((rx, ry), (qy, qx))):
-            at = side * half
-            valid = min(half, tokens - start - at)
-            here = slice(start + at, start + at + valid)
-            grad = (
-                mine_ref[:, at : at + valid]
-                + wide[:16, :valid].astype(jnp.float32)
-                + thin[:, :valid].astype(jnp.float32)
-            )
-            total = accum_ref[:, here] + grad * grad
-            sums_ref[:, at : at + valid] = total
-            next_ref[:, at : at + valid] = factor_ref[:, here] + step_rate * grad * lax.rsqrt(total)
-
-    block = pl.BlockSpec((rows, CHUNK), lambda i: (0, index))
-    extra = () if before is None else tuple(before)
-    return call(
-        kernel,
-        (jax.ShapeDtypeStruct(factor.shape, jnp.float32),) * 2,
-        (mine, *parts, factor, accum) + extra,
-        [whole] * 7 + [pl.BlockSpec(memory_space=pl.ANY)] * len(extra),
-        moved=16 * rows * size,
+    parts = [part for one in made for part in one]
+
+    def kernel(*refs):
+        chunk_refs, (ry, qx) = refs[: len(parts)], refs[len(parts) : len(parts) + 2]
+        factor_ref, accum_ref = refs[len(parts) + 2 : len(parts) + 4]
+        outs = refs[len(parts) + 4 + len(extra) :]
+        done = 0
+        for i, (start, size) in enumerate(group):
+            mine_ref, rx, qy = chunk_refs[3 * i : 3 * i + 3]
+            half = size // 2
+            for side, (wide, thin) in enumerate(((rx, ry), (qy, qx))):
+                at = side * half
+                valid = min(half, tokens - start - at)
+                here = slice(start + at, start + at + valid)
+                out = slice(start - group[0][0] + at, start - group[0][0] + at + valid)
+                grad = (
+                    mine_ref[:, at : at + valid]
+                    + wide[:16, :valid].astype(jnp.float32)
+                    + thin[:, done : done + valid].astype(jnp.float32)
+                )
+                total = accum_ref[:, here] + grad * grad
+                outs[1][:, out] = total
+                outs[0][:, out] = factor_ref[:, here] + step_rate * grad * lax.rsqrt(total)
+            done += half
+        if tenant is not None:
+            place_ref, next_ref, sums_ref = refs[len(parts) + 4 : len(parts) + 7]
+            row = ((place_ref[0] // 2) ^ place_ref[1]) * 16 + (place_ref[0] % 2) * 8
+            mine_rows = pl.ds(pl.multiple_of(row, 8), 8)
+            outs[2][...] = next_ref[mine_rows, :]
+            outs[3][...] = sums_ref[mine_rows, :]
+
+    block = pl.BlockSpec((rows, GROUP), lambda i: (0, index))
+    shapes, specs = [jax.ShapeDtypeStruct(factor.shape, jnp.float32)] * 2, [block] * 2
+    extra, extra_specs = (), []
+    if before is not None:
+        extra, extra_specs = tuple(before), [pl.BlockSpec(memory_space=pl.ANY)] * 2
+    if tenant is not None:
+        extra, extra_specs = tuple(tenant), [scalars, whole, whole]
+        shapes += [jax.ShapeDtypeStruct((8, tenant[1].shape[1]), jnp.float32)] * 2
+        specs += [whole] * 2
+    return call(
+        kernel,
+        tuple(shapes),
+        (*parts, *relayed, factor, accum) + extra,
+        [whole] * (len(parts) + 4) + extra_specs,
+        moved=16 * rows * GROUP,
         grid=(1,),
-        out_specs=(block, block),
-        input_output_aliases={7: 0, 8: 1} if extra else {},
+        out_specs=tuple(specs),
+        input_output_aliases={len(parts) + 4: 0, len(parts) + 5: 1} if before is not None else {},
     )
 
 
@@ -291,7 +306,7 @@
     tok = lambda a, bit: swap(a, "tok", bit, 8)
 
     padded = -(-tokens // (2 * LANES)) * 2 * LANES
-    chunks = [(i, s, min(CHUNK, padded - s)) for i, s in enumerate(range(0, padded, CHUNK))]
+    groups = [[(0, CHUNKS[0]), (CHUNKS[0], CHUNKS[1])], [(GROUP, padded - GROUP)]]
 
     with jax.named_scope("gather_tokens"):
         own = jnp.pad(v_factor.astype(jnp.bfloat16), ((0, 0), (0, padded - tokens)))
@@ -317,21 +332,26 @@
         grad = grad.astype(jnp.bfloat16)
 
     with jax.named_scope("token_grad"):
-        outs, ahead, low, step = None, None, None, (place, grad, tok(grad, 4), factor, accum)
-        for index, start, size in chunks:
-            made = token_grad(start, size, low, step, blocks, staged)
-            mine, sx, kx, sy, ky = made[:5]
-            if step:
-                low, u_next, u_accum_next, step = made[5:7], made[7], made[8], None
-            rx, qy = ten(sx, 1), ten(sy, 2)
-            if ahead is not None:
-                kx, ky, _, _ = lax.optimization_barrier((kx, ky, *ahead))
-            ahead = (
-                (kx + rx[16:].astype(jnp.float32)).astype(jnp.bfloat16),
-                (ky + qy[16:].astype(jnp.float32)).astype(jnp.bfloat16),
-            )
-            ry, qx = ten(ahead[0], 2), ten(ahead[1], 1)
-            outs = update_token(index, size, mine, (rx, ry, qy, qx), v_factor, v_accum, outs)
+        outs, ahead, after, low, step = None, None, None, None, (grad, tok(grad, 4), factor, accum)
+        for index, group in enumerate(groups):
+            made, add_x, add_y = [], [], []
+            for start, size in group:
+                mine, sx, kx, sy, ky, *news = token_grad(start, size, low, step, blocks, staged, after)
+                after = ky
+                if step:
+                    low, tenant, step = news[:2], (place, *news[2:]), None
+                rx, qy = ten(sx, 1), ten(sy, 2)
+                if ahead is not None:
+                    kx, ky, _, _ = lax.optimization_barrier((kx, ky, *ahead))
+                made.append((mine, rx, qy))
+                add_x.append((kx + rx[16:].astype(jnp.float32)).astype(jnp.bfloat16))
+                add_y.append((ky + qy[16:].astype(jnp.float32)).astype(jnp.bfloat16))
+            ahead = (jnp.concatenate(add_x, axis=1), jnp.concatenate(add_y, axis=1))
+            relayed = (ten(ahead[0], 2), ten(ahead[1], 1))
+            outs = update_token(index, group, made, relayed, v_factor, v_accum, outs, tenant)
+            if tenant is not None:
+                u_next, u_accum_next, tenant = outs[2], outs[3], None
+            outs = outs[:2]
     return (u_next, u_accum_next, *outs)
 
 
@@ -345,7 +365,7 @@
             and rank == 64
             and tenants == 4 * 256
             and tokens % 16 == 0
-            and CHUNK < tokens
+            and GROUP < tokens <= 2 * GROUP
         )
         return jax.shard_map(
             shards if suits else shards_any,

time: 66.5 us -> 64.6 us (0.971)
  starting transfers between devices: 29.5 us -> 26.8 us
  waiting for transfers between devices: 13.3 us -> 15.1 us
  Pallas kernels: 20.4 us -> 19.3 us
    ppermute x22 -> x20, starting transfers between devices: 29.5 us -> 26.8 us  [swap(): return lax.ppermute(a, axis, [(i, i ^ bit) for i in range(size)])]
    ppermute x22 -> x20, waiting for transfers between devices: 13.3 us -> 15.1 us  [swap(): return lax.ppermute(a, axis, [(i, i ^ bit) for i in range(size)])]
    pallas_call x9 -> x8, Pallas kernels: 20.4 us -> 19.3 us  [call(): pl.pallas_call(kernel, out_shape=out_shape, in_specs=in_specs, compiler_p...]
  transfers between devices with their start and end apart: 22 -> 20, of which waited for: 12 -> 11; matrix products, arithmetic and copies ran while one was open for 1% -> 2% of each run, Pallas kernels for 18% -> 18%
where the time goes in v3:
time: 64.6 us; the launch traced here: 64.3 us
  starting transfers between devices  26.8 us (41%)
  Pallas kernels  19.3 us (30%)
  waiting for transfers between devices  15.1 us (23%)
  other arithmetic  2.26 us (3%)
  between operations  0.76 us (1%)
    ppermute x20, starting transfers between devices, swap(): return lax.ppermute(a, axis, [(i, i ^ bit) for i in range(size)])  26.8 us
    pallas_call x8, Pallas kernels, call(): pl.pallas_call(kernel, out_shape=out_shape, in_specs=in_specs, compiler_p...  19.3 us
    ppermute x20, waiting for transfers between devices, swap(): return lax.ppermute(a, axis, [(i, i ^ bit) for i in range(size)])  15.1 us
  transfers between devices with their start and end apart: 20, of which 11 were waited for; matrix products, arithmetic and copies ran while one was open for 2% of the time, Pallas kernels for 18%

profile of v3, /device:TPU:0, one launch (start us, length us, event | category | flops | bytes accessed | tf_op | source)
XLA Modules:
  0.0 64.3 jit_solution(708400094429427526)
XLA Ops:
  0.6 1.3 %convert_element_type.53 = bf16[16,16032]{1,0:T(8,128)(2,1)S(1)} convert(f32[16,16032]{1,0:T(8,128)} %refs_5_.1) | non-fusion elementwise | flops 256512 | bytes 1539072 | tf_op jit(solution)/shard_map/gather_tokens/convert_element_type | solution.py:312
  2.0 3.0 %collective-permute-start.3 = (bf16[16,16128]{1,0:T(8,128)(2,1)S(1)}, bf16[16,16128]{1,0:T(8,128)(2,1)S(1)}, u32[]{:S(2)}, u32[]{:S(2)}) collective-permute-start(bf16[16,16128]{1,0:T(8,128)(2,1)S(1)} %pad.4.refs_0_.refs_4_.refs_3_), channel_id=1, source_target_pairs={{0,2},{1,3},{2,0},{3,1},{4,6},{5,7},{6,4},{7,5},{8,10},{9,11},{10,... | collective-permute-start | bytes 1548296 | tf_op jit(solution)/shard_map/gather_tokens/ppermute | solution.py:62
  5.0 1.5 %collective-permute-start.2 = (bf16[16,16128]{1,0:T(8,128)(2,1)S(1)}, bf16[16,16128]{1,0:T(8,128)(2,1)S(1)}, u32[]{:S(2)}, u32[]{:S(2)}) collective-permute-start(bf16[16,16128]{1,0:T(8,128)(2,1)S(1)} %pad.4.refs_0_.refs_4_.refs_3_), channel_id=1, source_target_pairs={{0,1},{1,0},{2,3},{3,2},{4,5},{5,4},{6,7},{7,6},{8,9},{9,8},{10,11... | collective-permute-start | bytes 1548296 | tf_op jit(solution)/shard_map/gather_tokens/ppermute | solution.py:62
  7.2 1.2 %collective-permute-done = f32[1,16,256]{2,1,0:T(8,128)S(1)} collective-permute-done((f32[1,16,256]{2,1,0:T(8,128)S(1)}, f32[1,16,256]{2,1,0:T(8,128)S(1)}, u32[]{:S(2)}, u32[]{:S(2)}) %collective-permute-start) | collective-permute-done | bytes 16416 | tf_op jit(solution)/shard_map/gather_tenants/ppermute | solution.py:62
  8.4 1.6 %collective-permute-start.1 = (f32[2,16,256]{2,1,0:T(8,128)S(1)}, f32[2,16,256]{2,1,0:T(8,128)S(1)}, u32[]{:S(2)}, u32[]{:S(2)}) collective-permute-start(f32[2,16,256]{2,1,0:T(8,128)S(1)} %pad_maximum_fusion.4.after_ref), channel_id=1, source_target_pairs={{0,8},{4,12},{8,0},{12,4},{16,24},{20,28},{24,16},{28,20},{1,9},{5... | collective-permute-start | bytes 98312 | tf_op jit(solution)/shard_map/gather_tenants/ppermute | solution.py:62
  10.0 5.8 %gather_tenants.2.refs_5_.refs_9_.refs_8_ = s32[16032,256]{1,0:T(8,128)S(1)} custom-call(s32[16032,256]{1,0:T(8,128)} %bitcast.5, f32[2,16,256]{2,1,0:T(8,128)S(1)} %pad_maximum_fusion.4.after_ref), custom_call_target="tpu_custom_call" | custom-call | bytes 32833536 | tf_op jit(solution)/shard_map/gather_tenants/pallas_call | solution.py:66
  15.7 1.0 %collective-permute-done.3.refs_2_.refs_6_.refs_5_ = bf16[16,16128]{1,0:T(8,128)(2,1)S(1)} collective-permute-done((bf16[16,16128]{1,0:T(8,128)(2,1)S(1)}, bf16[16,16128]{1,0:T(8,128)(2,1)S(1)}, u32[]{:S(2)}, u32[]{:S(2)}) %collective-permute-start.3) | collective-permute-done | bytes 516128 | tf_op jit(solution)/shard_map/gather_tokens/ppermute | solution.py:62
  16.8 1.8 %collective-permute-start.6 = (bf16[16,8064]{1,0:T(8,128)(2,1)S(1)}, bf16[16,8064]{1,0:T(8,128)(2,1)S(1)}, u32[]{:S(2)}, u32[]{:S(2)}) collective-permute-start(bf16[16,8064]{1,0:T(8,128)(2,1)S(1)} %slice.33), channel_id=1, source_target_pairs={{0,1},{1,0},{2,3},{3,2},{4,5},{5,4},{6,7},{7,6},{8,9},{9,8},{10,11... | collective-permute-start | bytes 774152 | tf_op jit(solution)/shard_map/gather_tokens/ppermute | solution.py:62
  18.6 1.6 %collective-permute-start.5 = (bf16[16,8064]{1,0:T(8,128)(2,1)S(1)}, bf16[16,8064]{1,0:T(8,128)(2,1)S(1)}, u32[]{:S(2)}, u32[]{:S(2)}) collective-permute-start(bf16[16,8064]{1,0:T(8,128)(2,1)S(1)} %slice.32), channel_id=1, source_target_pairs={{0,2},{1,3},{2,0},{3,1},{4,6},{5,7},{6,4},{7,5},{8,10},{9,11},{10,... | collective-permute-start | bytes 774152 | tf_op jit(solution)/shard_map/gather_tokens/ppermute | solution.py:62
  20.2 2.7 %collective-permute-start.4 = (f32[4,16,256]{2,1,0:T(8,128)S(1)}, f32[4,16,256]{2,1,0:T(8,128)S(1)}, u32[]{:S(2)}, u32[]{:S(2)}) collective-permute-start(f32[4,16,256]{2,1,0:T(8,128)S(1)} %pad_maximum_fusion.3), channel_id=1, source_target_pairs={{0,16},{4,20},{8,24},{12,28},{16,0},{20,4},{24,8},{28,12},{1,17},{... | collective-permute-start | bytes 196616 | tf_op jit(solution)/shard_map/gather_tenants/ppermute | solution.py:62
  22.9 2.5 %collective-permute-done.4 = f32[4,16,256]{2,1,0:T(8,128)S(1)} collective-permute-done((f32[4,16,256]{2,1,0:T(8,128)S(1)}, f32[4,16,256]{2,1,0:T(8,128)S(1)}, u32[]{:S(2)}, u32[]{:S(2)}) %collective-permute-start.4) | collective-permute-done | bytes 65568 | tf_op jit(solution)/shard_map/gather_tenants/ppermute | solution.py:62
  26.0 4.7 %tenant_grad.1 = f32[64,256]{1,0:T(8,128)S(1)} custom-call(bf16[64,256]{1,0:T(8,128)(2,1)S(1)} %get-tuple-element.37.half_ref, bf16[16,16128]{1,0:T(8,128)(2,1)S(1)} %pad.4.refs_0_.refs_4_.refs_3_, bf16[16,16128]{1,0:T(8,128)(2,1)S(1)} %collective-permute-done.2.refs_1_.refs_5_.refs_4_, bf16[16,16128]{1,0:T(8,128)(2,1)S(1)} %collective-permute-done.3.refs_2_.refs_6_.refs_5_, ...), custom_call_target="tpu_custom_call" | custom-call | bytes 1032192 | tf_op jit(solution)/shard_map/tenant_grad/pallas_call | solution.py:66
  30.8 1.2 %collective-permute-done.7 = f32[64,256]{1,0:T(8,128)S(1)} collective-permute-done((f32[64,256]{1,0:T(8,128)S(1)}, f32[64,256]{1,0:T(8,128)S(1)}, u32[]{:S(2)}, u32[]{:S(2)}) %collective-permute-start.7) | collective-permute-done | bytes 65568 | tf_op jit(solution)/shard_map/tenant_grad/ppermute | solution.py:62
  32.1 1.6 %collective-permute-start.8 = (bf16[64,256]{1,0:T(8,128)(2,1)S(1)}, bf16[64,256]{1,0:T(8,128)(2,1)S(1)}, u32[]{:S(2)}, u32[]{:S(2)}) collective-permute-start(bf16[64,256]{1,0:T(8,128)(2,1)S(1)} %add_convert_fusion.7), channel_id=1, source_target_pairs={{0,8},{4,12},{8,0},{12,4},{16,24},{20,28},{24,16},{28,20},{1,9},{5... | collective-permute-start | bytes 98312 | tf_op jit(solution)/shard_map/tenant_grad/ppermute | solution.py:62
  33.7 2.3 %collective-permute-done.8 = bf16[64,256]{1,0:T(8,128)(2,1)S(1)} collective-permute-done((bf16[64,256]{1,0:T(8,128)(2,1)S(1)}, bf16[64,256]{1,0:T(8,128)(2,1)S(1)}, u32[]{:S(2)}, u32[]{:S(2)}) %collective-permute-start.8) | collective-permute-done | bytes 32800 | tf_op jit(solution)/shard_map/tenant_grad/ppermute | solution.py:62
  36.1 2.8 %collective-permute-start.9 = (bf16[64,256]{1,0:T(8,128)(2,1)S(1)}, bf16[64,256]{1,0:T(8,128)(2,1)S(1)}, u32[]{:S(2)}, u32[]{:S(2)}) collective-permute-start(bf16[64,256]{1,0:T(8,128)(2,1)S(1)} %add_convert_fusion.6.refs_0_), channel_id=1, source_target_pairs={{0,16},{4,20},{8,24},{12,28},{16,0},{20,4},{24,8},{28,12},{1,17},{... | collective-permute-start | bytes 98312 | tf_op jit(solution)/shard_map/token_grad/ppermute | solution.py:62
  38.9 2.1 %collective-permute-done.9.refs_1_ = bf16[64,256]{1,0:T(8,128)(2,1)S(1)} collective-permute-done((bf16[64,256]{1,0:T(8,128)(2,1)S(1)}, bf16[64,256]{1,0:T(8,128)(2,1)S(1)}, u32[]{:S(2)}, u32[]{:S(2)}) %collective-permute-start.9) | collective-permute-done | bytes 32800 | tf_op jit(solution)/shard_map/token_grad/ppermute | solution.py:62
  40.9 1.8 %token_grad.5 = (f32[16,5376]{1,0:T(8,128)S(1)}, bf16[32,2688]{1,0:T(8,128)(2,1)S(1)}, f32[16,2688]{1,0:T(8,128)S(1)}, bf16[32,2688]{1,0:T(8,128)(2,1)S(1)}, f32...) custom-call(bf16[64,256]{1,0:T(8,128)(2,1)S(1)} %add_convert_fusion., ...), custom_call_target="tpu_custom_call" | custom-call | bytes 344064 | tf_op jit(solution)/shard_map/token_grad/pallas_call | solution.py:66
  43.4 1.1 %collective-permute-start.11 = (bf16[32,2688]{1,0:T(8,128)(2,1)S(1)}, bf16[32,2688]{1,0:T(8,128)(2,1)S(1)}, u32[]{:S(2)}, u32[]{:S(2)}) collective-permute-start(bf16[32,2688]{1,0:T(8,128)(2,1)S(1)} %get-tuple-element.43), channel_id=1, source_target_pairs={{0,2},{1,3},{2,0},{3,1},{4,6},{5,7},{6,4},{7,5},{8,10},{9,11},{10,... | collective-permute-start | bytes 516104 | tf_op jit(solution)/shard_map/token_grad/ppermute | solution.py:62
  44.5 1.8 %token_grad.6 = (f32[16,5376]{1,0:T(8,128)S(1)}, bf16[32,2688]{1,0:T(8,128)(2,1)S(1)}, f32[16,2688]{1,0:T(8,128)S(1)}, bf16[32,2688]{1,0:T(8,128)(2,1)S(1)}, f32[16,2688]{1,0:T(8,128)S(1)}) custom-call(f32[16,2688]{1,0:T(8,128)S(1)} %get-tuple-element.44.refs_0_, bf16[64,256]{1,0:T(8,128)(2,1)S(1)} %get-tuple-element.45.refs_1_, ...), custom_call_target="tpu_custom_call" | custom-call | bytes 344064 | tf_op jit(solution)/shard_map/token_grad/pallas_call | solution.py:66
  46.3 1.4 %collective-permute-start.12 = (bf16[32,2688]{1,0:T(8,128)(2,1)S(1)}, bf16[32,2688]{1,0:T(8,128)(2,1)S(1)}, u32[]{:S(2)}, u32[]{:S(2)}) collective-permute-start(bf16[32,2688]{1,0:T(8,128)(2,1)S(1)} %get-tuple-element.48), channel_id=1, source_target_pairs={{0,1},{1,0},{2,3},{3,2},{4,5},{5,4},{6,7},{7,6},{8,9},{9,8},{10,11... | collective-permute-start | bytes 516104 | tf_op jit(solution)/shard_map/token_grad/ppermute | solution.py:62
  47.7 1.1 %collective-permute-start.13 = (bf16[32,2688]{1,0:T(8,128)(2,1)S(1)}, bf16[32,2688]{1,0:T(8,128)(2,1)S(1)}, u32[]{:S(2)}, u32[]{:S(2)}) collective-permute-start(bf16[32,2688]{1,0:T(8,128)(2,1)S(1)} %get-tuple-element.49), channel_id=1, source_target_pairs={{0,2},{1,3},{2,0},{3,1},{4,6},{5,7},{6,4},{7,5},{8,10},{9,11},{10,... | collective-permute-start | bytes 516104 | tf_op jit(solution)/shard_map/token_grad/ppermute | solution.py:62
  48.8 1.8 %token_grad.8 = (f32[16,5376]{1,0:T(8,128)S(1)}, bf16[32,2688]{1,0:T(8,128)(2,1)S(1)}, f32[16,2688]{1,0:T(8,128)S(1)}, bf16[32,2688]{1,0:T(8,128)(2,1)S(1)}, f32[16,2688]{1,0:T(8,128)S(1)}) custom-call(f32[16,2688]{1,0:T(8,128)S(1)} %get-tuple-element.52.refs_0_, bf16[64,256]{1,0:T(8,128)(2,1)S(1)} %get-tuple-element.45.refs_1_, ...), custom_call_target="tpu_custom_call" | custom-call | bytes 344064 | tf_op jit(solution)/shard_map/token_grad/pallas_call | solution.py:66
  51.2 1.1 %collective-permute-start.17 = (bf16[32,2688]{1,0:T(8,128)(2,1)S(1)}, bf16[32,2688]{1,0:T(8,128)(2,1)S(1)}, u32[]{:S(2)}, u32[]{:S(2)}) collective-permute-start(bf16[32,2688]{1,0:T(8,128)(2,1)S(1)} %get-tuple-element.59), channel_id=1, source_target_pairs={{0,2},{1,3},{2,0},{3,1},{4,6},{5,7},{6,4},{7,5},{8,10},{9,11},{10,... | collective-permute-start | bytes 516104 | tf_op jit(solution)/shard_map/token_grad/ppermute | solution.py:62
  52.3 1.2 %collective-permute-done.12.refs_4_ = bf16[32,2688]{1,0:T(8,128)(2,1)S(1)} collective-permute-done((bf16[32,2688]{1,0:T(8,128)(2,1)S(1)}, bf16[32,2688]{1,0:T(8,128)(2,1)S(1)}, u32[]{:S(2)}, u32[]{:S(2)}) %collective-permute-start.12) | collective-permute-done | bytes 172064 | tf_op jit(solution)/shard_map/token_grad/ppermute | solution.py:62
  53.5 1.1 %collective-permute-start.14 = (bf16[16,5376]{1,0:T(8,128)(2,1)S(1)}, bf16[16,5376]{1,0:T(8,128)(2,1)S(1)}, u32[]{:S(2)}, u32[]{:S(2)}) collective-permute-start(bf16[16,5376]{1,0:T(8,128)(2,1)S(1)} %pad_maximum_fusion), channel_id=1, source_target_pairs={{0,2},{1,3},{2,0},{3,1},{4,6},{5,7},{6,4},{7,5},{8,10},{9,11},{10,... | collective-permute-start | bytes 516104 | tf_op jit(solution)/shard_map/token_grad/ppermute | solution.py:62
  55.0 0.9 %collective-permute-start.15 = (bf16[16,5376]{1,0:T(8,128)(2,1)S(1)}, bf16[16,5376]{1,0:T(8,128)(2,1)S(1)}, u32[]{:S(2)}, u32[]{:S(2)}) collective-permute-start(bf16[16,5376]{1,0:T(8,128)(2,1)S(1)} %pad_maximum_fusion.1), channel_id=1, source_target_pairs={{0,1},{1,0},{2,3},{3,2},{4,5},{5,4},{6,7},{7,6},{8,9},{9,8},{10,11... | collective-permute-start | bytes 516104 | tf_op jit(solution)/shard_map/token_grad/ppermute | solution.py:62
  55.9 1.8 %collective-permute-done.16.refs_1_ = bf16[32,2688]{1,0:T(8,128)(2,1)S(1)} collective-permute-done((bf16[32,2688]{1,0:T(8,128)(2,1)S(1)}, bf16[32,2688]{1,0:T(8,128)(2,1)S(1)}, u32[]{:S(2)}, u32[]{:S(2)}) %collective-permute-start.16) | collective-permute-done | bytes 172064 | tf_op jit(solution)/shard_map/token_grad/ppermute | solution.py:62
  57.8 0.9 %collective-permute-start.18 = (bf16[16,2688]{1,0:T(8,128)(2,1)S(1)}, bf16[16,2688]{1,0:T(8,128)(2,1)S(1)}, u32[]{:S(2)}, u32[]{:S(2)}) collective-permute-start(bf16[16,2688]{1,0:T(8,128)(2,1)S(1)} %add_convert_fusion.1), channel_id=1, source_target_pairs={{0,2},{1,3},{2,0},{3,1},{4,6},{5,7},{6,4},{7,5},{8,10},{9,11},{10,... | collective-permute-start | bytes 258056 | tf_op jit(solution)/shard_map/token_grad/ppermute | solution.py:62
  58.8 1.3 %collective-permute-start.19 = (bf16[16,2688]{1,0:T(8,128)(2,1)S(1)}, bf16[16,2688]{1,0:T(8,128)(2,1)S(1)}, u32[]{:S(2)}, u32[]{:S(2)}) collective-permute-start(bf16[16,2688]{1,0:T(8,128)(2,1)S(1)} %add_convert_fusion), channel_id=1, source_target_pairs={{0,1},{1,0},{2,3},{3,2},{4,5},{5,4},{6,7},{7,6},{8,9},{9,8},{10,11... | collective-permute-start | bytes 258056 | tf_op jit(solution)/shard_map/token_grad/ppermute | solution.py:62
  60.8 1.8 %token_grad.7 = (f32[16,16032]{1,0:T(8,128)}, f32[16,16032]{1,0:T(8,128)}, f32[8,256]{1,0:T(8,128)}, f32[8,256]{1,0:T(8,128)}) custom-call(f32[16,5376]{1,0:T(8,128)S(1)} %get-tuple-element.41.refs_0_, bf16[32,2688]{1,0:T(8,128)(2,1)S(1)} %collective-permute-done.10.refs_1_, bf16[32,2688]{1,0:T(8,128)(2,1)S(1)} %collective-permute-done.11.refs_2_, ...), custom_call_target="tpu_custom_call" | custom-call | bytes 2752512 | tf_op jit(solution)/shard_map/token_grad/pallas_call | solution.py:66
  63.3 1.0 %token_grad.9 = (f32[16,16032]{1,0:T(8,128)}, f32[16,16032]{1,0:T(8,128)}) custom-call(f32[16,5376]{1,0:T(8,128)S(1)} %get-tuple-element.57.refs_0_, bf16[32,2688]{1,0:T(8,128)(2,1)S(1)} %collective-permute-done.16.refs_1_, bf16[32,2688]{1,0:T(8,128)(2,1)S(1)} %collective-permute-done.17.refs_2_, ...), custom_call_target="tpu_custom_call", output_to_operand_aliasing={{0}: (7, {}), {1}: (8, {})} | custom-call | bytes 2752512 | tf_op jit(solution)/shard_map/token_grad/pallas_call | solution.py:66
  (39 shorter events, 4.7 us)
Async XLA Ops:
  2.0 14.8 %collective-permute-start.3 = (bf16[16,16128]{1,0:T(8,128)(2,1)S(1)}, bf16[16,16128]{1,0:T(8,128)(2,1)S(1)}, u32[]{:S(2)}, u32[]{:S(2)}) collective-permute-start(bf16[16,16128]{1,0:T(8,128)(2,1)S(1)} %pad.4.refs_0_.refs_4_.refs_3_), channel_id=1, source_target_pairs={{0,2},{1,3},{2,0},{3,1},{4,6},{5,7},{6,4},{7,5},{8,10},{9,11},{10,... | collective-permute-start | bytes 1548296 | tf_op jit(solution)/shard_map/gather_tokens/ppermute | solution.py:62
  5.0 13.5 %collective-permute-start.2 = (bf16[16,16128]{1,0:T(8,128)(2,1)S(1)}, bf16[16,16128]{1,0:T(8,128)(2,1)S(1)}, u32[]{:S(2)}, u32[]{:S(2)}) collective-permute-start(bf16[16,16128]{1,0:T(8,128)(2,1)S(1)} %pad.4.refs_0_.refs_4_.refs_3_), channel_id=1, source_target_pairs={{0,1},{1,0},{2,3},{3,2},{4,5},{5,4},{6,7},{7,6},{8,9},{9,8},{10,11... | collective-permute-start | bytes 1548296 | tf_op jit(solution)/shard_map/gather_tokens/ppermute | solution.py:62
  7.2 1.2 %collective-permute-start = (f32[1,16,256]{2,1,0:T(8,128)S(1)}, f32[1,16,256]{2,1,0:T(8,128)S(1)}, u32[]{:S(2)}, u32[]{:S(2)}) collective-permute-start(f32[1,16,256]{2,1,0:T(8,128)S(1)} %maximum_bitcast_fusion), channel_id=1, source_target_pairs={{0,4},{4,0},{8,12},{12,8},{16,20},{20,16},{24,28},{28,24},{1,5},{5... | collective-permute-start | bytes 49160 | tf_op jit(solution)/shard_map/gather_tenants/ppermute | solution.py:62
  8.4 11.8 %collective-permute-start.1 = (f32[2,16,256]{2,1,0:T(8,128)S(1)}, f32[2,16,256]{2,1,0:T(8,128)S(1)}, u32[]{:S(2)}, u32[]{:S(2)}) collective-permute-start(f32[2,16,256]{2,1,0:T(8,128)S(1)} %pad_maximum_fusion.4.after_ref), channel_id=1, source_target_pairs={{0,8},{4,12},{8,0},{12,4},{16,24},{20,28},{24,16},{28,20},{1,9},{5... | collective-permute-start | bytes 98312 | tf_op jit(solution)/shard_map/gather_tenants/ppermute | solution.py:62
  16.8 9.2 %collective-permute-start.6 = (bf16[16,8064]{1,0:T(8,128)(2,1)S(1)}, bf16[16,8064]{1,0:T(8,128)(2,1)S(1)}, u32[]{:S(2)}, u32[]{:S(2)}) collective-permute-start(bf16[16,8064]{1,0:T(8,128)(2,1)S(1)} %slice.33), channel_id=1, source_target_pairs={{0,1},{1,0},{2,3},{3,2},{4,5},{5,4},{6,7},{7,6},{8,9},{9,8},{10,11... | collective-permute-start | bytes 774152 | tf_op jit(solution)/shard_map/gather_tokens/ppermute | solution.py:62
  18.6 7.4 %collective-permute-start.5 = (bf16[16,8064]{1,0:T(8,128)(2,1)S(1)}, bf16[16,8064]{1,0:T(8,128)(2,1)S(1)}, u32[]{:S(2)}, u32[]{:S(2)}) collective-permute-start(bf16[16,8064]{1,0:T(8,128)(2,1)S(1)} %slice.32), channel_id=1, source_target_pairs={{0,2},{1,3},{2,0},{3,1},{4,6},{5,7},{6,4},{7,5},{8,10},{9,11},{10,... | collective-permute-start | bytes 774152 | tf_op jit(solution)/shard_map/gather_tokens/ppermute | solution.py:62
  20.2 5.2 %collective-permute-start.4 = (f32[4,16,256]{2,1,0:T(8,128)S(1)}, f32[4,16,256]{2,1,0:T(8,128)S(1)}, u32[]{:S(2)}, u32[]{:S(2)}) collective-permute-start(f32[4,16,256]{2,1,0:T(8,128)S(1)} %pad_maximum_fusion.3), channel_id=1, source_target_pairs={{0,16},{4,20},{8,24},{12,28},{16,0},{20,4},{24,8},{28,12},{1,17},{... | collective-permute-start | bytes 196616 | tf_op jit(solution)/shard_map/gather_tenants/ppermute | solution.py:62
  30.7 1.3 %collective-permute-start.7 = (f32[64,256]{1,0:T(8,128)S(1)}, f32[64,256]{1,0:T(8,128)S(1)}, u32[]{:S(2)}, u32[]{:S(2)}) collective-permute-start(f32[64,256]{1,0:T(8,128)S(1)} %tenant_grad.1), channel_id=1, source_target_pairs={{0,4},{4,0},{8,12},{12,8},{16,20},{20,16},{24,28},{28,24},{1,5},{5... | collective-permute-start | bytes 196616 | tf_op jit(solution)/shard_map/tenant_grad/ppermute | solution.py:62
  32.1 4.0 %collective-permute-start.8 = (bf16[64,256]{1,0:T(8,128)(2,1)S(1)}, bf16[64,256]{1,0:T(8,128)(2,1)S(1)}, u32[]{:S(2)}, u32[]{:S(2)}) collective-permute-start(bf16[64,256]{1,0:T(8,128)(2,1)S(1)} %add_convert_fusion.7), channel_id=1, source_target_pairs={{0,8},{4,12},{8,0},{12,4},{16,24},{20,28},{24,16},{28,20},{1,9},{5... | collective-permute-start | bytes 98312 | tf_op jit(solution)/shard_map/tenant_grad/ppermute | solution.py:62
  36.1 4.9 %collective-permute-start.9 = (bf16[64,256]{1,0:T(8,128)(2,1)S(1)}, bf16[64,256]{1,0:T(8,128)(2,1)S(1)}, u32[]{:S(2)}, u32[]{:S(2)}) collective-permute-start(bf16[64,256]{1,0:T(8,128)(2,1)S(1)} %add_convert_fusion.6.refs_0_), channel_id=1, source_target_pairs={{0,16},{4,20},{8,24},{12,28},{16,0},{20,4},{24,8},{28,12},{1,17},{... | collective-permute-start | bytes 98312 | tf_op jit(solution)/shard_map/token_grad/ppermute | solution.py:62
  42.8 8.4 %collective-permute-start.10 = (bf16[32,2688]{1,0:T(8,128)(2,1)S(1)}, bf16[32,2688]{1,0:T(8,128)(2,1)S(1)}, u32[]{:S(2)}, u32[]{:S(2)}) collective-permute-start(bf16[32,2688]{1,0:T(8,128)(2,1)S(1)} %get-tuple-element.42), channel_id=1, source_target_pairs={{0,1},{1,0},{2,3},{3,2},{4,5},{5,4},{6,7},{7,6},{8,9},{9,8},{10,11... | collective-permute-start | bytes 516104 | tf_op jit(solution)/shard_map/token_grad/ppermute | solution.py:62
  43.4 11.3 %collective-permute-start.11 = (bf16[32,2688]{1,0:T(8,128)(2,1)S(1)}, bf16[32,2688]{1,0:T(8,128)(2,1)S(1)}, u32[]{:S(2)}, u32[]{:S(2)}) collective-permute-start(bf16[32,2688]{1,0:T(8,128)(2,1)S(1)} %get-tuple-element.43), channel_id=1, source_target_pairs={{0,2},{1,3},{2,0},{3,1},{4,6},{5,7},{6,4},{7,5},{8,10},{9,11},{10,... | collective-permute-start | bytes 516104 | tf_op jit(solution)/shard_map/token_grad/ppermute | solution.py:62
  44.5 16.3 %copy-start = (f32[16,16032]{1,0:T(8,128)S(1)}, f32[16,16032]{1,0:T(8,128)}, u32[]{:S(2)}) copy-start(f32[16,16032]{1,0:T(8,128)} %refs_5_.1) | copy-start | bytes 3078148
  44.5 16.3 %copy-start.1 = (f32[16,16032]{1,0:T(8,128)S(1)}, f32[16,16032]{1,0:T(8,128)}, u32[]{:S(2)}) copy-start(f32[16,16032]{1,0:T(8,128)} %refs_6_.1) | copy-start | bytes 3078148
  46.3 7.2 %collective-permute-start.12 = (bf16[32,2688]{1,0:T(8,128)(2,1)S(1)}, bf16[32,2688]{1,0:T(8,128)(2,1)S(1)}, u32[]{:S(2)}, u32[]{:S(2)}) collective-permute-start(bf16[32,2688]{1,0:T(8,128)(2,1)S(1)} %get-tuple-element.48), channel_id=1, source_target_pairs={{0,1},{1,0},{2,3},{3,2},{4,5},{5,4},{6,7},{7,6},{8,9},{9,8},{10,11... | collective-permute-start | bytes 516104 | tf_op jit(solution)/shard_map/token_grad/ppermute | solution.py:62
  47.7 7.3 %collective-permute-start.13 = (bf16[32,2688]{1,0:T(8,128)(2,1)S(1)}, bf16[32,2688]{1,0:T(8,128)(2,1)S(1)}, u32[]{:S(2)}, u32[]{:S(2)}) collective-permute-start(bf16[32,2688]{1,0:T(8,128)(2,1)S(1)} %get-tuple-element.49), channel_id=1, source_target_pairs={{0,2},{1,3},{2,0},{3,1},{4,6},{5,7},{6,4},{7,5},{8,10},{9,11},{10,... | collective-permute-start | bytes 516104 | tf_op jit(solution)/shard_map/token_grad/ppermute | solution.py:62
  50.6 7.2 %collective-permute-start.16 = (bf16[32,2688]{1,0:T(8,128)(2,1)S(1)}, bf16[32,2688]{1,0:T(8,128)(2,1)S(1)}, u32[]{:S(2)}, u32[]{:S(2)}) collective-permute-start(bf16[32,2688]{1,0:T(8,128)(2,1)S(1)} %get-tuple-element.58), channel_id=1, source_target_pairs={{0,1},{1,0},{2,3},{3,2},{4,5},{5,4},{6,7},{7,6},{8,9},{9,8},{10,11... | collective-permute-start | bytes 516104 | tf_op jit(solution)/shard_map/token_grad/ppermute | solution.py:62
  51.2 7.6 %collective-permute-start.17 = (bf16[32,2688]{1,0:T(8,128)(2,1)S(1)}, bf16[32,2688]{1,0:T(8,128)(2,1)S(1)}, u32[]{:S(2)}, u32[]{:S(2)}) collective-permute-start(bf16[32,2688]{1,0:T(8,128)(2,1)S(1)} %get-tuple-element.59), channel_id=1, source_target_pairs={{0,2},{1,3},{2,0},{3,1},{4,6},{5,7},{6,4},{7,5},{8,10},{9,11},{10,... | collective-permute-start | bytes 516104 | tf_op jit(solution)/shard_map/token_grad/ppermute | solution.py:62
  53.5 7.2 %collective-permute-start.14 = (bf16[16,5376]{1,0:T(8,128)(2,1)S(1)}, bf16[16,5376]{1,0:T(8,128)(2,1)S(1)}, u32[]{:S(2)}, u32[]{:S(2)}) collective-permute-start(bf16[16,5376]{1,0:T(8,128)(2,1)S(1)} %pad_maximum_fusion), channel_id=1, source_target_pairs={{0,2},{1,3},{2,0},{3,1},{4,6},{5,7},{6,4},{7,5},{8,10},{9,11},{10,... | collective-permute-start | bytes 516104 | tf_op jit(solution)/shard_map/token_grad/ppermute | solution.py:62
  55.0 5.7 %collective-permute-start.15 = (bf16[16,5376]{1,0:T(8,128)(2,1)S(1)}, bf16[16,5376]{1,0:T(8,128)(2,1)S(1)}, u32[]{:S(2)}, u32[]{:S(2)}) collective-permute-start(bf16[16,5376]{1,0:T(8,128)(2,1)S(1)} %pad_maximum_fusion.1), channel_id=1, source_target_pairs={{0,1},{1,0},{2,3},{3,2},{4,5},{5,4},{6,7},{7,6},{8,9},{9,8},{10,11... | collective-permute-start | bytes 516104 | tf_op jit(solution)/shard_map/token_grad/ppermute | solution.py:62
  57.8 4.8 %collective-permute-start.18 = (bf16[16,2688]{1,0:T(8,128)(2,1)S(1)}, bf16[16,2688]{1,0:T(8,128)(2,1)S(1)}, u32[]{:S(2)}, u32[]{:S(2)}) collective-permute-start(bf16[16,2688]{1,0:T(8,128)(2,1)S(1)} %add_convert_fusion.1), channel_id=1, source_target_pairs={{0,2},{1,3},{2,0},{3,1},{4,6},{5,7},{6,4},{7,5},{8,10},{9,11},{10,... | collective-permute-start | bytes 258056 | tf_op jit(solution)/shard_map/token_grad/ppermute | solution.py:62
  58.8 4.6 %collective-permute-start.19 = (bf16[16,2688]{1,0:T(8,128)(2,1)S(1)}, bf16[16,2688]{1,0:T(8,128)(2,1)S(1)}, u32[]{:S(2)}, u32[]{:S(2)}) collective-permute-start(bf16[16,2688]{1,0:T(8,128)(2,1)S(1)} %add_convert_fusion), channel_id=1, source_target_pairs={{0,1},{1,0},{2,3},{3,2},{4,5},{5,4},{6,7},{7,6},{8,9},{9,8},{10,11... | collective-permute-start | bytes 258056 | tf_op jit(solution)/shard_map/token_grad/ppermute | solution.py:62

commit v4 on v3

--- a/solution.py
+++ b/solution.py
@@ -75,19 +75,19 @@
     )(*operands)
 
 
-def order_tenant(place, gathered):
-    def kernel(place_ref, all_ref, factor_ref, accum_ref, half_ref):
-        for j in range(4):
-            for h in range(2):
-                source = (2 * (place_ref[1] ^ j) + h) ^ place_ref[0]
-                rows = pl.ds(16 * j + 8 * h, 8)
-                factor_ref[rows, :] = all_ref[source, :8, :]
-                accum_ref[rows, :] = all_ref[source, 8:, :]
-        half_ref[...] = (factor_ref[...].astype(jnp.bfloat16).astype(jnp.float32) * 0.5).astype(
-            jnp.bfloat16
-        )
-
-    width = gathered.shape[2]
+def order_tenant(turn, stack):
+    def kernel(turn_ref, stack_ref, factor_ref, accum_ref, half_ref):
+        for rows, out_ref in ((slice(0, 8), factor_ref), (slice(8, 16), accum_ref)):
+            blocks = [stack_ref[p, rows, :] for p in range(8)]
+            for bit in (1, 2, 4):
+                stays = (turn_ref[...] & bit) == 0
+                blocks = [jnp.where(stays, blocks[p], blocks[p ^ bit]) for p in range(8)]
+            for p in range(8):
+                out_ref[8 * p : 8 * p + 8, :] = blocks[p]
+        low = factor_ref[...].astype(jnp.bfloat16).astype(jnp.float32)
+        half_ref[...] = (low * 0.5).astype(jnp.bfloat16)
+
+    width = stack.shape[2]
     return call(
         kernel,
         (
@@ -95,9 +95,9 @@
             jax.ShapeDtypeStruct((64, width), jnp.float32),
             jax.ShapeDtypeStruct((64, width), jnp.bfloat16),
         ),
-        (place, gathered),
-        [scalars, whole],
-        out_specs=(whole, whole, whole),
+        (turn, stack),
+        [whole] * 2,
+        out_specs=(whole,) * 3,
     )
 
 
@@ -110,28 +110,32 @@
     return found
 
 
-def stage(counts, after):
+def stage(turn, counts, after):
     tokens, width = counts.shape
     step = -(-tokens // 32) * 8
 
-    def kernel(counts_ref, after_ref, out_ref, sems):
+    def kernel(turn_ref, counts_ref, after_ref, out_ref, vector_ref, sems):
         copies = []
         for i, at in enumerate(range(0, tokens, step)):
             rows = pl.ds(at, min(step, tokens - at))
             copies.append(pltpu.make_async_copy(counts_ref.at[rows, :], out_ref.at[rows, :], sems.at[i]))
         for copy in copies:
             copy.start()
+        vector_ref[...] = jnp.broadcast_to(turn_ref[0], vector_ref.shape)
         for copy in copies:
             copy.wait()
 
     return call(
         kernel,
-        jax.ShapeDtypeStruct((tokens, width), jnp.int32),
-        (counts, after),
-        [pl.BlockSpec(memory_space=pltpu.HBM)] * 2,
+        (
+            jax.ShapeDtypeStruct((tokens, width), jnp.int32),
+            jax.ShapeDtypeStruct((8, width), jnp.int32),
+        ),
+        (turn, counts, after),
+        [scalars] + [pl.BlockSpec(memory_space=pltpu.HBM)] * 2,
         moved=8 * tokens * width,
         limit=HBM_SIDE_LIMIT,
-        out_specs=whole,
+        out_specs=(whole, whole),
         scratch_shapes=[pltpu.SemaphoreType.DMA((4,))],
     )
 
@@ -193,9 +197,9 @@
         blocks_ref, counts_ref = refs[ahead : ahead + 5], refs[ahead + 5]
         mine, sx, kx, sy, ky = refs[ahead + 6 : ahead + 11]
         if step:
-            a_ref, b_ref, factor_ref, accum_ref = refs[:ahead]
+            parts_ref, (factor_ref, accum_ref) = refs[:4], refs[4:6]
             low_ref, half_ref, next_ref, sums_ref = refs[ahead + 11 :]
-            grad = a_ref[...].astype(jnp.float32) + b_ref[...].astype(jnp.float32)
+            grad = sum(part[...].astype(jnp.float32) for part in parts_ref)
             total = accum_ref[...] + grad * grad
             fresh = factor_ref[...] + step_rate * grad * lax.rsqrt(total)
             next_ref[...] = fresh
@@ -238,7 +242,7 @@
         kernel,
         tuple(shapes),
         (() if after is None else (after,)) + front + (*blocks, counts),
-        [pl.BlockSpec(memory_space=pl.ANY)] * (after is not None) + [whole] * (10 if step else 8),
+        [pl.BlockSpec(memory_space=pl.ANY)] * (after is not None) + [whole] * (12 if step else 8),
         moved=PASS_COST * size,
         out_specs=(whole,) * len(shapes),
     )
@@ -271,9 +275,8 @@
                 outs[0][:, out] = factor_ref[:, here] + step_rate * grad * lax.rsqrt(total)
             done += half
         if tenant is not None:
-            place_ref, next_ref, sums_ref = refs[len(parts) + 4 : len(parts) + 7]
-            row = ((place_ref[0] // 2) ^ place_ref[1]) * 16 + (place_ref[0] % 2) * 8
-            mine_rows = pl.ds(pl.multiple_of(row, 8), 8)
+            turn_ref, next_ref, sums_ref = refs[len(parts) + 4 : len(parts) + 7]
+            mine_rows = pl.ds(pl.multiple_of(8 * turn_ref[0], 8), 8)
             outs[2][...] = next_ref[mine_rows, :]
             outs[3][...] = sums_ref[mine_rows, :]
 
@@ -301,7 +304,7 @@
 def shards(counts, u_factor, u_accum, v_factor, v_accum):
     tokens = v_factor.shape[1]
     by_token = counts.T
-    place = jnp.stack([lax.axis_index("tok"), lax.axis_index("ten")]).astype(jnp.int32)
+    turn = (lax.axis_index("tok") ^ (2 * lax.axis_index("ten"))).astype(jnp.int32)[None]
     ten = lambda a, bit: swap(a, "ten", bit, 4)
     tok = lambda a, bit: swap(a, "tok", bit, 8)
 
@@ -320,26 +323,24 @@
         for bit in (1, 2, 4):
             stack = jnp.concatenate([stack, tok(stack, bit)], axis=0)
             if bit == 1:
-                staged = stage(by_token, stack)
+                staged, vector = stage(turn, by_token, stack)
             elif bit == 2:
-                stack, staged, _, _ = lax.optimization_barrier((stack, staged, *relayed))
-        factor, accum, half_low = order_tenant(place, stack)
+                stack, vector, _, _ = lax.optimization_barrier((stack, vector, *relayed))
+        factor, accum, half_low = order_tenant(vector, stack)
 
     with jax.named_scope("tenant_grad"):
         grad = tenant_grad(half_low, blocks, staged)
         grad = (grad + tok(grad, 1)).astype(jnp.bfloat16)
-        grad = grad.astype(jnp.float32) + tok(grad, 2).astype(jnp.float32)
-        grad = grad.astype(jnp.bfloat16)
 
     with jax.named_scope("token_grad"):
-        outs, ahead, after, low, step = None, None, None, None, (grad, tok(grad, 4), factor, accum)
+        outs, ahead, after, low, step = None, None, None, None, (grad, tok(grad, 2), tok(grad, 4), tok(grad, 6), factor, accum)
         for index, group in enumerate(groups):
             made, add_x, add_y = [], [], []
             for start, size in group:
                 mine, sx, kx, sy, ky, *news = token_grad(start, size, low, step, blocks, staged, after)
                 after = ky
                 if step:
-                    low, tenant, step = news[:2], (place, *news[2:]), None
+                    low, tenant, step = news[:2], (turn, *news[2:]), None
                 rx, qy = ten(sx, 1), ten(sy, 2)
                 if ahead is not None:
                     kx, ky, _, _ = lax.optimization_barrier((kx, ky, *ahead))

time: 64.6 us -> 64.3 us (level)
  Pallas kernels: 19.3 us -> 18.4 us
    pallas_call x8, Pallas kernels: 19.3 us -> 18.4 us  [call(): pl.pallas_call(kernel, out_shape=out_shape, in_specs=in_specs, compiler_p...]
    ppermute x20 -> x21, starting transfers between devices: 26.8 us -> 27.3 us  [swap(): return lax.ppermute(a, axis, [(i, i ^ bit) for i in range(size)])]
    ppermute x20 -> x21, waiting for transfers between devices: 15.1 us -> 15.3 us  [swap(): return lax.ppermute(a, axis, [(i, i ^ bit) for i in range(size)])]
  transfers between devices with their start and end apart: 20 -> 21, of which waited for: 11 -> 11; matrix products, arithmetic and copies ran while one was open for 2% -> 1% of each run, Pallas kernels for 18% -> 17%
where the time goes in v4:
time: 64.3 us; the launch traced here: 64 us
  starting transfers between devices  27.3 us (42%)
  Pallas kernels  18.4 us (29%)
  waiting for transfers between devices  15.3 us (24%)
  other arithmetic  2.17 us (3%)
  between operations  0.76 us (1%)
    ppermute x21, starting transfers between devices, swap(): return lax.ppermute(a, axis, [(i, i ^ bit) for i in range(size)])  27.3 us
    pallas_call x8, Pallas kernels, call(): pl.pallas_call(kernel, out_shape=out_shape, in_specs=in_specs, compiler_p...  18.4 us
    ppermute x21, waiting for transfers between devices, swap(): return lax.ppermute(a, axis, [(i, i ^ bit) for i in range(size)])  15.3 us
  transfers between devices with their start and end apart: 21, of which 11 were waited for; matrix products, arithmetic and copies ran while one was open for 1% of the time, Pallas kernels for 17%

profile of v4, /device:TPU:0, one launch (start us, length us, event | category | flops | bytes accessed | tf_op | source)
XLA Modules:
  0.0 64.0 jit_solution(14558416578193375683)
XLA Ops:
  0.6 1.3 %convert_element_type.44 = bf16[16,16032]{1,0:T(8,128)(2,1)S(1)} convert(f32[16,16032]{1,0:T(8,128)} %refs_5_.1) | non-fusion elementwise | flops 256512 | bytes 1539072 | tf_op jit(solution)/shard_map/gather_tokens/convert_element_type | solution.py:315
  2.0 3.0 %collective-permute-start.3 = (bf16[16,16128]{1,0:T(8,128)(2,1)S(1)}, bf16[16,16128]{1,0:T(8,128)(2,1)S(1)}, u32[]{:S(2)}, u32[]{:S(2)}) collective-permute-start(bf16[16,16128]{1,0:T(8,128)(2,1)S(1)} %pad.4.refs_0_.refs_6_.refs_3_), channel_id=1, source_target_pairs={{0,2},{1,3},{2,0},{3,1},{4,6},{5,7},{6,4},{7,5},{8,10},{9,11},{10,... | collective-permute-start | bytes 1548296 | tf_op jit(solution)/shard_map/gather_tokens/ppermute | solution.py:62
  5.0 1.5 %collective-permute-start.2 = (bf16[16,16128]{1,0:T(8,128)(2,1)S(1)}, bf16[16,16128]{1,0:T(8,128)(2,1)S(1)}, u32[]{:S(2)}, u32[]{:S(2)}) collective-permute-start(bf16[16,16128]{1,0:T(8,128)(2,1)S(1)} %pad.4.refs_0_.refs_6_.refs_3_), channel_id=1, source_target_pairs={{0,1},{1,0},{2,3},{3,2},{4,5},{5,4},{6,7},{7,6},{8,9},{9,8},{10,11... | collective-permute-start | bytes 1548296 | tf_op jit(solution)/shard_map/gather_tokens/ppermute | solution.py:62
  7.2 1.2 %collective-permute-done = f32[1,16,256]{2,1,0:T(8,128)S(1)} collective-permute-done((f32[1,16,256]{2,1,0:T(8,128)S(1)}, f32[1,16,256]{2,1,0:T(8,128)S(1)}, u32[]{:S(2)}, u32[]{:S(2)}) %collective-permute-start) | collective-permute-done | bytes 16416 | tf_op jit(solution)/shard_map/gather_tenants/ppermute | solution.py:62
  8.4 1.6 %collective-permute-start.1 = (f32[2,16,256]{2,1,0:T(8,128)S(1)}, f32[2,16,256]{2,1,0:T(8,128)S(1)}, u32[]{:S(2)}, u32[]{:S(2)}) collective-permute-start(f32[2,16,256]{2,1,0:T(8,128)S(1)} %pad_maximum_fusion.4.after_ref), channel_id=1, source_target_pairs={{0,8},{4,12},{8,0},{12,4},{16,24},{20,28},{24,16},{28,20},{1,9},{5... | collective-permute-start | bytes 98312 | tf_op jit(solution)/shard_map/gather_tenants/ppermute | solution.py:62
  10.0 5.8 %gather_tenants.2 = (s32[16032,256]{1,0:T(8,128)S(1)}, s32[8,256]{1,0:T(8,128)S(1)}) custom-call(s32[1]{0:T(128)} %bitcast.1.turn_ref.refs_10_, s32[16032,256]{1,0:T(8,128)} %bitcast.4, f32[2,16,256]{2,1,0:T(8,128)S(1)} %pad_maximum_fusion.4.after_ref), custom_call_target="tpu_custom_call" | custom-call | bytes 32833536 | tf_op jit(solution)/shard_map/gather_tenants/pallas_call | solution.py:66
  15.7 1.0 %collective-permute-done.3.refs_2_.refs_8_.refs_5_ = bf16[16,16128]{1,0:T(8,128)(2,1)S(1)} collective-permute-done((bf16[16,16128]{1,0:T(8,128)(2,1)S(1)}, bf16[16,16128]{1,0:T(8,128)(2,1)S(1)}, u32[]{:S(2)}, u32[]{:S(2)}) %collective-permute-start.3) | collective-permute-done | bytes 516128 | tf_op jit(solution)/shard_map/gather_tokens/ppermute | solution.py:62
  16.8 1.8 %collective-permute-start.6 = (bf16[16,8064]{1,0:T(8,128)(2,1)S(1)}, bf16[16,8064]{1,0:T(8,128)(2,1)S(1)}, u32[]{:S(2)}, u32[]{:S(2)}) collective-permute-start(bf16[16,8064]{1,0:T(8,128)(2,1)S(1)} %slice.33), channel_id=1, source_target_pairs={{0,1},{1,0},{2,3},{3,2},{4,5},{5,4},{6,7},{7,6},{8,9},{9,8},{10,11... | collective-permute-start | bytes 774152 | tf_op jit(solution)/shard_map/gather_tokens/ppermute | solution.py:62
  18.6 1.6 %collective-permute-start.5 = (bf16[16,8064]{1,0:T(8,128)(2,1)S(1)}, bf16[16,8064]{1,0:T(8,128)(2,1)S(1)}, u32[]{:S(2)}, u32[]{:S(2)}) collective-permute-start(bf16[16,8064]{1,0:T(8,128)(2,1)S(1)} %slice.32), channel_id=1, source_target_pairs={{0,2},{1,3},{2,0},{3,1},{4,6},{5,7},{6,4},{7,5},{8,10},{9,11},{10,... | collective-permute-start | bytes 774152 | tf_op jit(solution)/shard_map/gather_tokens/ppermute | solution.py:62
  20.2 2.7 %collective-permute-start.4 = (f32[4,16,256]{2,1,0:T(8,128)S(1)}, f32[4,16,256]{2,1,0:T(8,128)S(1)}, u32[]{:S(2)}, u32[]{:S(2)}) collective-permute-start(f32[4,16,256]{2,1,0:T(8,128)S(1)} %pad_maximum_fusion.3), channel_id=1, source_target_pairs={{0,16},{4,20},{8,24},{12,28},{16,0},{20,4},{24,8},{28,12},{1,17},{... | collective-permute-start | bytes 196616 | tf_op jit(solution)/shard_map/gather_tenants/ppermute | solution.py:62
  22.8 2.6 %collective-permute-done.4 = f32[4,16,256]{2,1,0:T(8,128)S(1)} collective-permute-done((f32[4,16,256]{2,1,0:T(8,128)S(1)}, f32[4,16,256]{2,1,0:T(8,128)S(1)}, u32[]{:S(2)}, u32[]{:S(2)}) %collective-permute-start.4) | collective-permute-done | bytes 65568 | tf_op jit(solution)/shard_map/gather_tenants/ppermute | solution.py:62
  25.5 4.9 %tenant_grad.1 = f32[64,256]{1,0:T(8,128)S(1)} custom-call(bf16[64,256]{1,0:T(8,128)(2,1)S(1)} %get-tuple-element.41.half_ref, bf16[16,16128]{1,0:T(8,128)(2,1)S(1)} %pad.4.refs_0_.refs_6_.refs_3_, bf16[16,16128]{1,0:T(8,128)(2,1)S(1)} %collective-permute-done.2.refs_1_.refs_7_.refs_4_, bf16[16,16128]{1,0:T(8,128)(2,1)S(1)} %collective-permute-done.3.refs_2_.refs_8_.refs_5_, ...), custom_call_target="tpu_custom_call" | custom-call | bytes 1032192 | tf_op jit(solution)/shard_map/tenant_grad/pallas_call | solution.py:66
  30.4 1.2 %collective-permute-done.7 = f32[64,256]{1,0:T(8,128)S(1)} collective-permute-done((f32[64,256]{1,0:T(8,128)S(1)}, f32[64,256]{1,0:T(8,128)S(1)}, u32[]{:S(2)}, u32[]{:S(2)}) %collective-permute-start.7) | collective-permute-done | bytes 65568 | tf_op jit(solution)/shard_map/tenant_grad/ppermute | solution.py:62
  31.7 4.3 %collective-permute-start.10 = (bf16[64,256]{1,0:T(8,128)(2,1)S(1)}, bf16[64,256]{1,0:T(8,128)(2,1)S(1)}, u32[]{:S(2)}, u32[]{:S(2)}) collective-permute-start(bf16[64,256]{1,0:T(8,128)(2,1)S(1)} %add_convert_fusion.6.refs_0_), channel_id=1, source_target_pairs={{0,24},{4,28},{8,16},{12,20},{16,8},{20,12},{24,0},{28,4},{1,25},{... | collective-permute-start | bytes 98312 | tf_op jit(solution)/shard_map/token_grad/ppermute | solution.py:62
  36.6 1.3 %collective-permute-done.10.refs_3_ = bf16[64,256]{1,0:T(8,128)(2,1)S(1)} collective-permute-done((bf16[64,256]{1,0:T(8,128)(2,1)S(1)}, bf16[64,256]{1,0:T(8,128)(2,1)S(1)}, u32[]{:S(2)}, u32[]{:S(2)}) %collective-permute-start.10) | collective-permute-done | bytes 32800 | tf_op jit(solution)/shard_map/token_grad/ppermute | solution.py:62
  37.9 2.9 %collective-permute-done.9.refs_2_ = bf16[64,256]{1,0:T(8,128)(2,1)S(1)} collective-permute-done((bf16[64,256]{1,0:T(8,128)(2,1)S(1)}, bf16[64,256]{1,0:T(8,128)(2,1)S(1)}, u32[]{:S(2)}, u32[]{:S(2)}) %collective-permute-start.9) | collective-permute-done | bytes 32800 | tf_op jit(solution)/shard_map/token_grad/ppermute | solution.py:62
  40.7 1.8 %token_grad.5 = (f32[16,5376]{1,0:T(8,128)S(1)}, bf16[32,2688]{1,0:T(8,128)(2,1)S(1)}, f32[16,2688]{1,0:T(8,128)S(1)}, bf16[32,2688]{1,0:T(8,128)(2,1)S(1)}, f32...) custom-call(bf16[64,256]{1,0:T(8,128)(2,1)S(1)} %add_convert_fusion., ...), custom_call_target="tpu_custom_call" | custom-call | bytes 344064 | tf_op jit(solution)/shard_map/token_grad/pallas_call | solution.py:66
  43.2 1.1 %collective-permute-start.12 = (bf16[32,2688]{1,0:T(8,128)(2,1)S(1)}, bf16[32,2688]{1,0:T(8,128)(2,1)S(1)}, u32[]{:S(2)}, u32[]{:S(2)}) collective-permute-start(bf16[32,2688]{1,0:T(8,128)(2,1)S(1)} %get-tuple-element.47), channel_id=1, source_target_pairs={{0,2},{1,3},{2,0},{3,1},{4,6},{5,7},{6,4},{7,5},{8,10},{9,11},{10,... | collective-permute-start | bytes 516104 | tf_op jit(solution)/shard_map/token_grad/ppermute | solution.py:62
  44.3 1.8 %token_grad.6 = (f32[16,5376]{1,0:T(8,128)S(1)}, bf16[32,2688]{1,0:T(8,128)(2,1)S(1)}, f32[16,2688]{1,0:T(8,128)S(1)}, bf16[32,2688]{1,0:T(8,128)(2,1)S(1)}, f32[16,2688]{1,0:T(8,128)S(1)}) custom-call(f32[16,2688]{1,0:T(8,128)S(1)} %get-tuple-element.48.refs_0_, bf16[64,256]{1,0:T(8,128)(2,1)S(1)} %get-tuple-element.49.refs_1_, ...), custom_call_target="tpu_custom_call" | custom-call | bytes 344064 | tf_op jit(solution)/shard_map/token_grad/pallas_call | solution.py:66
  46.1 1.3 %collective-permute-start.13 = (bf16[32,2688]{1,0:T(8,128)(2,1)S(1)}, bf16[32,2688]{1,0:T(8,128)(2,1)S(1)}, u32[]{:S(2)}, u32[]{:S(2)}) collective-permute-start(bf16[32,2688]{1,0:T(8,128)(2,1)S(1)} %get-tuple-element.52), channel_id=1, source_target_pairs={{0,1},{1,0},{2,3},{3,2},{4,5},{5,4},{6,7},{7,6},{8,9},{9,8},{10,11... | collective-permute-start | bytes 516104 | tf_op jit(solution)/shard_map/token_grad/ppermute | solution.py:62
  47.4 1.1 %collective-permute-start.14 = (bf16[32,2688]{1,0:T(8,128)(2,1)S(1)}, bf16[32,2688]{1,0:T(8,128)(2,1)S(1)}, u32[]{:S(2)}, u32[]{:S(2)}) collective-permute-start(bf16[32,2688]{1,0:T(8,128)(2,1)S(1)} %get-tuple-element.53), channel_id=1, source_target_pairs={{0,2},{1,3},{2,0},{3,1},{4,6},{5,7},{6,4},{7,5},{8,10},{9,11},{10,... | collective-permute-start | bytes 516104 | tf_op jit(solution)/shard_map/token_grad/ppermute | solution.py:62
  48.5 1.8 %token_grad.8 = (f32[16,5376]{1,0:T(8,128)S(1)}, bf16[32,2688]{1,0:T(8,128)(2,1)S(1)}, f32[16,2688]{1,0:T(8,128)S(1)}, bf16[32,2688]{1,0:T(8,128)(2,1)S(1)}, f32[16,2688]{1,0:T(8,128)S(1)}) custom-call(f32[16,2688]{1,0:T(8,128)S(1)} %get-tuple-element.56.refs_0_, bf16[64,256]{1,0:T(8,128)(2,1)S(1)} %get-tuple-element.49.refs_1_, ...), custom_call_target="tpu_custom_call" | custom-call | bytes 344064 | tf_op jit(solution)/shard_map/token_grad/pallas_call | solution.py:66
  50.9 1.1 %collective-permute-start.18 = (bf16[32,2688]{1,0:T(8,128)(2,1)S(1)}, bf16[32,2688]{1,0:T(8,128)(2,1)S(1)}, u32[]{:S(2)}, u32[]{:S(2)}) collective-permute-start(bf16[32,2688]{1,0:T(8,128)(2,1)S(1)} %get-tuple-element.63), channel_id=1, source_target_pairs={{0,2},{1,3},{2,0},{3,1},{4,6},{5,7},{6,4},{7,5},{8,10},{9,11},{10,... | collective-permute-start | bytes 516104 | tf_op jit(solution)/shard_map/token_grad/ppermute | solution.py:62
  52.1 0.7 %collective-permute-done.13.refs_4_ = bf16[32,2688]{1,0:T(8,128)(2,1)S(1)} collective-permute-done((bf16[32,2688]{1,0:T(8,128)(2,1)S(1)}, bf16[32,2688]{1,0:T(8,128)(2,1)S(1)}, u32[]{:S(2)}, u32[]{:S(2)}) %collective-permute-start.13) | collective-permute-done | bytes 172064 | tf_op jit(solution)/shard_map/token_grad/ppermute | solution.py:62
  53.5 0.9 %collective-permute-done.14.refs_5_ = bf16[32,2688]{1,0:T(8,128)(2,1)S(1)} collective-permute-done((bf16[32,2688]{1,0:T(8,128)(2,1)S(1)}, bf16[32,2688]{1,0:T(8,128)(2,1)S(1)}, u32[]{:S(2)}, u32[]{:S(2)}) %collective-permute-start.14) | collective-permute-done | bytes 172064 | tf_op jit(solution)/shard_map/token_grad/ppermute | solution.py:62
  54.4 1.2 %collective-permute-start.16 = (bf16[16,5376]{1,0:T(8,128)(2,1)S(1)}, bf16[16,5376]{1,0:T(8,128)(2,1)S(1)}, u32[]{:S(2)}, u32[]{:S(2)}) collective-permute-start(bf16[16,5376]{1,0:T(8,128)(2,1)S(1)} %pad_maximum_fusion.1), channel_id=1, source_target_pairs={{0,1},{1,0},{2,3},{3,2},{4,5},{5,4},{6,7},{7,6},{8,9},{9,8},{10,11... | collective-permute-start | bytes 516104 | tf_op jit(solution)/shard_map/token_grad/ppermute | solution.py:62
  55.6 1.6 %collective-permute-done.17.refs_1_ = bf16[32,2688]{1,0:T(8,128)(2,1)S(1)} collective-permute-done((bf16[32,2688]{1,0:T(8,128)(2,1)S(1)}, bf16[32,2688]{1,0:T(8,128)(2,1)S(1)}, u32[]{:S(2)}, u32[]{:S(2)}) %collective-permute-start.17) | collective-permute-done | bytes 172064 | tf_op jit(solution)/shard_map/token_grad/ppermute | solution.py:62
  57.3 1.2 %collective-permute-start.19 = (bf16[16,2688]{1,0:T(8,128)(2,1)S(1)}, bf16[16,2688]{1,0:T(8,128)(2,1)S(1)}, u32[]{:S(2)}, u32[]{:S(2)}) collective-permute-start(bf16[16,2688]{1,0:T(8,128)(2,1)S(1)} %add_convert_fusion.1), channel_id=1, source_target_pairs={{0,2},{1,3},{2,0},{3,1},{4,6},{5,7},{6,4},{7,5},{8,10},{9,11},{10,... | collective-permute-start | bytes 258056 | tf_op jit(solution)/shard_map/token_grad/ppermute | solution.py:62
  58.5 1.3 %collective-permute-start.20 = (bf16[16,2688]{1,0:T(8,128)(2,1)S(1)}, bf16[16,2688]{1,0:T(8,128)(2,1)S(1)}, u32[]{:S(2)}, u32[]{:S(2)}) collective-permute-start(bf16[16,2688]{1,0:T(8,128)(2,1)S(1)} %add_convert_fusion), channel_id=1, source_target_pairs={{0,1},{1,0},{2,3},{3,2},{4,5},{5,4},{6,7},{7,6},{8,9},{9,8},{10,11... | collective-permute-start | bytes 258056 | tf_op jit(solution)/shard_map/token_grad/ppermute | solution.py:62
  59.8 1.3 %collective-permute-done.15.refs_6_ = bf16[16,5376]{1,0:T(8,128)(2,1)S(1)} collective-permute-done((bf16[16,5376]{1,0:T(8,128)(2,1)S(1)}, bf16[16,5376]{1,0:T(8,128)(2,1)S(1)}, u32[]{:S(2)}, u32[]{:S(2)}) %collective-permute-start.15) | collective-permute-done | bytes 172064 | tf_op jit(solution)/shard_map/token_grad/ppermute | solution.py:62
  61.1 1.3 %token_grad.7 = (f32[16,16032]{1,0:T(8,128)}, f32[16,16032]{1,0:T(8,128)}, f32[8,256]{1,0:T(8,128)}, f32[8,256]{1,0:T(8,128)}) custom-call(f32[16,5376]{1,0:T(8,128)S(1)} %get-tuple-element.45.refs_0_, bf16[32,2688]{1,0:T(8,128)(2,1)S(1)} %collective-permute-done.11.refs_1_, bf16[32,2688]{1,0:T(8,128)(2,1)S(1)} %collective-permute-done.12.refs_2_, ...), custom_call_target="tpu_custom_call" | custom-call | bytes 2752512 | tf_op jit(solution)/shard_map/token_grad/pallas_call | solution.py:66
  63.0 1.0 %token_grad.9 = (f32[16,16032]{1,0:T(8,128)}, f32[16,16032]{1,0:T(8,128)}) custom-call(f32[16,5376]{1,0:T(8,128)S(1)} %get-tuple-element.61.refs_0_, bf16[32,2688]{1,0:T(8,128)(2,1)S(1)} %collective-permute-done.17.refs_1_, bf16[32,2688]{1,0:T(8,128)(2,1)S(1)} %collective-permute-done.18.refs_2_, ...), custom_call_target="tpu_custom_call", output_to_operand_aliasing={{0}: (7, {}), {1}: (8, {})} | custom-call | bytes 2752512 | tf_op jit(solution)/shard_map/token_grad/pallas_call | solution.py:66
  (39 shorter events, 4.1 us)
Async XLA Ops:
  2.0 14.8 %collective-permute-start.3 = (bf16[16,16128]{1,0:T(8,128)(2,1)S(1)}, bf16[16,16128]{1,0:T(8,128)(2,1)S(1)}, u32[]{:S(2)}, u32[]{:S(2)}) collective-permute-start(bf16[16,16128]{1,0:T(8,128)(2,1)S(1)} %pad.4.refs_0_.refs_6_.refs_3_), channel_id=1, source_target_pairs={{0,2},{1,3},{2,0},{3,1},{4,6},{5,7},{6,4},{7,5},{8,10},{9,11},{10,... | collective-permute-start | bytes 1548296 | tf_op jit(solution)/shard_map/gather_tokens/ppermute | solution.py:62
  5.0 13.5 %collective-permute-start.2 = (bf16[16,16128]{1,0:T(8,128)(2,1)S(1)}, bf16[16,16128]{1,0:T(8,128)(2,1)S(1)}, u32[]{:S(2)}, u32[]{:S(2)}) collective-permute-start(bf16[16,16128]{1,0:T(8,128)(2,1)S(1)} %pad.4.refs_0_.refs_6_.refs_3_), channel_id=1, source_target_pairs={{0,1},{1,0},{2,3},{3,2},{4,5},{5,4},{6,7},{7,6},{8,9},{9,8},{10,11... | collective-permute-start | bytes 1548296 | tf_op jit(solution)/shard_map/gather_tokens/ppermute | solution.py:62
  7.2 1.2 %collective-permute-start = (f32[1,16,256]{2,1,0:T(8,128)S(1)}, f32[1,16,256]{2,1,0:T(8,128)S(1)}, u32[]{:S(2)}, u32[]{:S(2)}) collective-permute-start(f32[1,16,256]{2,1,0:T(8,128)S(1)} %maximum_bitcast_fusion), channel_id=1, source_target_pairs={{0,4},{4,0},{8,12},{12,8},{16,20},{20,16},{24,28},{28,24},{1,5},{5... | collective-permute-start | bytes 49160 | tf_op jit(solution)/shard_map/gather_tenants/ppermute | solution.py:62
  8.4 11.8 %collective-permute-start.1 = (f32[2,16,256]{2,1,0:T(8,128)S(1)}, f32[2,16,256]{2,1,0:T(8,128)S(1)}, u32[]{:S(2)}, u32[]{:S(2)}) collective-permute-start(f32[2,16,256]{2,1,0:T(8,128)S(1)} %pad_maximum_fusion.4.after_ref), channel_id=1, source_target_pairs={{0,8},{4,12},{8,0},{12,4},{16,24},{20,28},{24,16},{28,20},{1,9},{5... | collective-permute-start | bytes 98312 | tf_op jit(solution)/shard_map/gather_tenants/ppermute | solution.py:62
  16.8 8.7 %collective-permute-start.6 = (bf16[16,8064]{1,0:T(8,128)(2,1)S(1)}, bf16[16,8064]{1,0:T(8,128)(2,1)S(1)}, u32[]{:S(2)}, u32[]{:S(2)}) collective-permute-start(bf16[16,8064]{1,0:T(8,128)(2,1)S(1)} %slice.33), channel_id=1, source_target_pairs={{0,1},{1,0},{2,3},{3,2},{4,5},{5,4},{6,7},{7,6},{8,9},{9,8},{10,11... | collective-permute-start | bytes 774152 | tf_op jit(solution)/shard_map/gather_tokens/ppermute | solution.py:62
  18.6 6.9 %collective-permute-start.5 = (bf16[16,8064]{1,0:T(8,128)(2,1)S(1)}, bf16[16,8064]{1,0:T(8,128)(2,1)S(1)}, u32[]{:S(2)}, u32[]{:S(2)}) collective-permute-start(bf16[16,8064]{1,0:T(8,128)(2,1)S(1)} %slice.32), channel_id=1, source_target_pairs={{0,2},{1,3},{2,0},{3,1},{4,6},{5,7},{6,4},{7,5},{8,10},{9,11},{10,... | collective-permute-start | bytes 774152 | tf_op jit(solution)/shard_map/gather_tokens/ppermute | solution.py:62
  20.2 5.2 %collective-permute-start.4 = (f32[4,16,256]{2,1,0:T(8,128)S(1)}, f32[4,16,256]{2,1,0:T(8,128)S(1)}, u32[]{:S(2)}, u32[]{:S(2)}) collective-permute-start(f32[4,16,256]{2,1,0:T(8,128)S(1)} %pad_maximum_fusion.3), channel_id=1, source_target_pairs={{0,16},{4,20},{8,24},{12,28},{16,0},{20,4},{24,8},{28,12},{1,17},{... | collective-permute-start | bytes 196616 | tf_op jit(solution)/shard_map/gather_tenants/ppermute | solution.py:62
  30.3 1.3 %collective-permute-start.7 = (f32[64,256]{1,0:T(8,128)S(1)}, f32[64,256]{1,0:T(8,128)S(1)}, u32[]{:S(2)}, u32[]{:S(2)}) collective-permute-start(f32[64,256]{1,0:T(8,128)S(1)} %tenant_grad.1), channel_id=1, source_target_pairs={{0,4},{4,0},{8,12},{12,8},{16,20},{20,16},{24,28},{28,24},{1,5},{5... | collective-permute-start | bytes 196616 | tf_op jit(solution)/shard_map/tenant_grad/ppermute | solution.py:62
  31.7 6.2 %collective-permute-start.10 = (bf16[64,256]{1,0:T(8,128)(2,1)S(1)}, bf16[64,256]{1,0:T(8,128)(2,1)S(1)}, u32[]{:S(2)}, u32[]{:S(2)}) collective-permute-start(bf16[64,256]{1,0:T(8,128)(2,1)S(1)} %add_convert_fusion.6.refs_0_), channel_id=1, source_target_pairs={{0,24},{4,28},{8,16},{12,20},{16,8},{20,12},{24,0},{28,4},{1,25},{... | collective-permute-start | bytes 98312 | tf_op jit(solution)/shard_map/token_grad/ppermute | solution.py:62
  35.9 4.8 %collective-permute-start.9 = (bf16[64,256]{1,0:T(8,128)(2,1)S(1)}, bf16[64,256]{1,0:T(8,128)(2,1)S(1)}, u32[]{:S(2)}, u32[]{:S(2)}) collective-permute-start(bf16[64,256]{1,0:T(8,128)(2,1)S(1)} %add_convert_fusion.6.refs_0_), channel_id=1, source_target_pairs={{0,16},{4,20},{8,24},{12,28},{16,0},{20,4},{24,8},{28,12},{1,17},{... | collective-permute-start | bytes 98312 | tf_op jit(solution)/shard_map/token_grad/ppermute | solution.py:62
  35.9 4.8 %collective-permute-start.8 = (bf16[64,256]{1,0:T(8,128)(2,1)S(1)}, bf16[64,256]{1,0:T(8,128)(2,1)S(1)}, u32[]{:S(2)}, u32[]{:S(2)}) collective-permute-start(bf16[64,256]{1,0:T(8,128)(2,1)S(1)} %add_convert_fusion.6.refs_0_), channel_id=1, source_target_pairs={{0,8},{4,12},{8,0},{12,4},{16,24},{20,28},{24,16},{28,20},{1,9},{5... | collective-permute-start | bytes 98312 | tf_op jit(solution)/shard_map/token_grad/ppermute | solution.py:62
  42.6 8.4 %collective-permute-start.11 = (bf16[32,2688]{1,0:T(8,128)(2,1)S(1)}, bf16[32,2688]{1,0:T(8,128)(2,1)S(1)}, u32[]{:S(2)}, u32[]{:S(2)}) collective-permute-start(bf16[32,2688]{1,0:T(8,128)(2,1)S(1)} %get-tuple-element.46), channel_id=1, source_target_pairs={{0,1},{1,0},{2,3},{3,2},{4,5},{5,4},{6,7},{7,6},{8,9},{9,8},{10,11... | collective-permute-start | bytes 516104 | tf_op jit(solution)/shard_map/token_grad/ppermute | solution.py:62
  43.2 10.3 %collective-permute-start.12 = (bf16[32,2688]{1,0:T(8,128)(2,1)S(1)}, bf16[32,2688]{1,0:T(8,128)(2,1)S(1)}, u32[]{:S(2)}, u32[]{:S(2)}) collective-permute-start(bf16[32,2688]{1,0:T(8,128)(2,1)S(1)} %get-tuple-element.47), channel_id=1, source_target_pairs={{0,2},{1,3},{2,0},{3,1},{4,6},{5,7},{6,4},{7,5},{8,10},{9,11},{10,... | collective-permute-start | bytes 516104 | tf_op jit(solution)/shard_map/token_grad/ppermute | solution.py:62
  44.3 16.8 %copy-start = (f32[16,16032]{1,0:T(8,128)S(1)}, f32[16,16032]{1,0:T(8,128)}, u32[]{:S(2)}) copy-start(f32[16,16032]{1,0:T(8,128)} %refs_5_.1) | copy-start | bytes 3078148
  44.3 16.8 %copy-start.1 = (f32[16,16032]{1,0:T(8,128)S(1)}, f32[16,16032]{1,0:T(8,128)}, u32[]{:S(2)}) copy-start(f32[16,16032]{1,0:T(8,128)} %refs_6_.1) | copy-start | bytes 3078148
  46.1 6.7 %collective-permute-start.13 = (bf16[32,2688]{1,0:T(8,128)(2,1)S(1)}, bf16[32,2688]{1,0:T(8,128)(2,1)S(1)}, u32[]{:S(2)}, u32[]{:S(2)}) collective-permute-start(bf16[32,2688]{1,0:T(8,128)(2,1)S(1)} %get-tuple-element.52), channel_id=1, source_target_pairs={{0,1},{1,0},{2,3},{3,2},{4,5},{5,4},{6,7},{7,6},{8,9},{9,8},{10,11... | collective-permute-start | bytes 516104 | tf_op jit(solution)/shard_map/token_grad/ppermute | solution.py:62
  47.4 6.9 %collective-permute-start.14 = (bf16[32,2688]{1,0:T(8,128)(2,1)S(1)}, bf16[32,2688]{1,0:T(8,128)(2,1)S(1)}, u32[]{:S(2)}, u32[]{:S(2)}) collective-permute-start(bf16[32,2688]{1,0:T(8,128)(2,1)S(1)} %get-tuple-element.53), channel_id=1, source_target_pairs={{0,2},{1,3},{2,0},{3,1},{4,6},{5,7},{6,4},{7,5},{8,10},{9,11},{10,... | collective-permute-start | bytes 516104 | tf_op jit(solution)/shard_map/token_grad/ppermute | solution.py:62
  50.3 6.9 %collective-permute-start.17 = (bf16[32,2688]{1,0:T(8,128)(2,1)S(1)}, bf16[32,2688]{1,0:T(8,128)(2,1)S(1)}, u32[]{:S(2)}, u32[]{:S(2)}) collective-permute-start(bf16[32,2688]{1,0:T(8,128)(2,1)S(1)} %get-tuple-element.62), channel_id=1, source_target_pairs={{0,1},{1,0},{2,3},{3,2},{4,5},{5,4},{6,7},{7,6},{8,9},{9,8},{10,11... | collective-permute-start | bytes 516104 | tf_op jit(solution)/shard_map/token_grad/ppermute | solution.py:62
  50.9 7.5 %collective-permute-start.18 = (bf16[32,2688]{1,0:T(8,128)(2,1)S(1)}, bf16[32,2688]{1,0:T(8,128)(2,1)S(1)}, u32[]{:S(2)}, u32[]{:S(2)}) collective-permute-start(bf16[32,2688]{1,0:T(8,128)(2,1)S(1)} %get-tuple-element.63), channel_id=1, source_target_pairs={{0,2},{1,3},{2,0},{3,1},{4,6},{5,7},{6,4},{7,5},{8,10},{9,11},{10,... | collective-permute-start | bytes 516104 | tf_op jit(solution)/shard_map/token_grad/ppermute | solution.py:62
  52.9 8.3 %collective-permute-start.15 = (bf16[16,5376]{1,0:T(8,128)(2,1)S(1)}, bf16[16,5376]{1,0:T(8,128)(2,1)S(1)}, u32[]{:S(2)}, u32[]{:S(2)}) collective-permute-start(bf16[16,5376]{1,0:T(8,128)(2,1)S(1)} %pad_maximum_fusion), channel_id=1, source_target_pairs={{0,2},{1,3},{2,0},{3,1},{4,6},{5,7},{6,4},{7,5},{8,10},{9,11},{10,... | collective-permute-start | bytes 516104 | tf_op jit(solution)/shard_map/token_grad/ppermute | solution.py:62
  54.4 6.7 %collective-permute-start.16 = (bf16[16,5376]{1,0:T(8,128)(2,1)S(1)}, bf16[16,5376]{1,0:T(8,128)(2,1)S(1)}, u32[]{:S(2)}, u32[]{:S(2)}) collective-permute-start(bf16[16,5376]{1,0:T(8,128)(2,1)S(1)} %pad_maximum_fusion.1), channel_id=1, source_target_pairs={{0,1},{1,0},{2,3},{3,2},{4,5},{5,4},{6,7},{7,6},{8,9},{9,8},{10,11... | collective-permute-start | bytes 516104 | tf_op jit(solution)/shard_map/token_grad/ppermute | solution.py:62
  57.3 5.1 %collective-permute-start.19 = (bf16[16,2688]{1,0:T(8,128)(2,1)S(1)}, bf16[16,2688]{1,0:T(8,128)(2,1)S(1)}, u32[]{:S(2)}, u32[]{:S(2)}) collective-permute-start(bf16[16,2688]{1,0:T(8,128)(2,1)S(1)} %add_convert_fusion.1), channel_id=1, source_target_pairs={{0,2},{1,3},{2,0},{3,1},{4,6},{5,7},{6,4},{7,5},{8,10},{9,11},{10,... | collective-permute-start | bytes 258056 | tf_op jit(solution)/shard_map/token_grad/ppermute | solution.py:62
  58.5 4.6 %collective-permute-start.20 = (bf16[16,2688]{1,0:T(8,128)(2,1)S(1)}, bf16[16,2688]{1,0:T(8,128)(2,1)S(1)}, u32[]{:S(2)}, u32[]{:S(2)}) collective-permute-start(bf16[16,2688]{1,0:T(8,128)(2,1)S(1)} %add_convert_fusion), channel_id=1, source_target_pairs={{0,1},{1,0},{2,3},{3,2},{4,5},{5,4},{6,7},{7,6},{8,9},{9,8},{10,11... | collective-permute-start | bytes 258056 | tf_op jit(solution)/shard_map/token_grad/ppermute | solution.py:62

commit v5 on v4

--- a/solution.py
+++ b/solution.py
@@ -11,6 +11,7 @@
 CHUNKS = (5376, 5376)
 GROUP = sum(CHUNKS)
 INNER = 1024
+CUT = 8192
 PASS_COST = 64
 HBM_SIDE_LIMIT = 34 * 2**20
 VMEM_LIMIT = 12 * 2**20
@@ -78,7 +79,7 @@
 def order_tenant(turn, stack):
     def kernel(turn_ref, stack_ref, factor_ref, accum_ref, half_ref):
         for rows, out_ref in ((slice(0, 8), factor_ref), (slice(8, 16), accum_ref)):
-            blocks = [stack_ref[p, rows, :] for p in range(8)]
+            blocks = [stack_ref[(p >> 1) | ((p & 1) << 2), rows, :] for p in range(8)]
             for bit in (1, 2, 4):
                 stays = (turn_ref[...] & bit) == 0
                 blocks = [jnp.where(stays, blocks[p], blocks[p ^ bit]) for p in range(8)]
@@ -157,37 +158,45 @@
     return resid
 
 
-def gathered(blocks, at, length):
-    own, x, y, d0, d1 = blocks
-    middle = d0.shape[1]
-    diag = d0[:, at : at + length] if at < middle else d1[:, at - middle : at - middle + length]
-    return jnp.concatenate([r[:, at : at + length] for r in (own, x, y)] + [diag], axis=0)
-
-
-def tenant_grad(half_low, blocks, counts):
+def gathered(blocks, bounds, at, length):
+    own, x, y, *diags = blocks
+    which = max(i for i, bound in enumerate(bounds) if bound <= at)
+    lo = at - bounds[which]
+    return jnp.concatenate(
+        [r[:, at : at + length] for r in (own, x, y)] + [diags[which][:, lo : lo + length]], axis=0
+    )
+
+
+def tenant_grad(span, half_low, blocks, bounds, counts, total):
     tokens, width = counts.shape
-    padded = blocks[0].shape[1]
-
-    def kernel(half_ref, *refs):
-        blocks_ref, counts_ref, out_ref = refs[:5], refs[5], refs[6]
-        grad = jnp.zeros(out_ref.shape, jnp.float32)
-        for at, length, valid in pieces(0, padded, [padded // 2], tokens):
-            v = gathered(blocks_ref, at, length)
+    start, stop = span
+    parts = [i for i, bound in enumerate(bounds) if start <= bound < stop]
+    extra = () if total is None else (total,)
+
+    def kernel(half_ref, own, x, y, *refs):
+        diags = [None] * len(bounds)
+        for i, ref in zip(parts, refs):
+            diags[i] = ref
+        counts_ref, out_ref = refs[len(parts)], refs[-1]
+        grad = refs[len(parts) + 1][...] if extra else jnp.zeros(out_ref.shape, jnp.float32)
+        for at, length, valid in pieces(start, stop - start, bounds, tokens):
+            v = gathered((own, x, y, *diags), bounds, at, length)
             resid = fresh_residual(half_ref[...], v, lifted(counts_ref[at : at + valid, :]))
             grad += jnp.dot(v, resid, preferred_element_type=jnp.float32)
         out_ref[...] = grad
 
+    operands = (half_low, *blocks[:3], *[blocks[3 + i] for i in parts], counts) + extra
     return call(
         kernel,
         jax.ShapeDtypeStruct((64, width), jnp.float32),
-        (half_low, *blocks, counts),
-        [whole] * 7,
-        moved=PASS_COST * padded,
+        operands,
+        [whole] * len(operands),
+        moved=PASS_COST * (stop - start),
         out_specs=whole,
     )
 
 
-def token_grad(start, size, low, step, blocks, counts, after):
+def token_grad(start, size, low, step, blocks, bounds, counts, after):
     tokens, width = counts.shape
     half = size // 2
     ahead = len(step) if step else 2
@@ -211,8 +220,8 @@
         else:
             low_u, half_u = refs[0][...], refs[1][...]
         middle = start + half
-        for at, length, valid in pieces(start, size, [middle, blocks[0].shape[1] // 2], tokens):
-            v = gathered(blocks_ref, at, length)
+        for at, length, valid in pieces(start, size, [middle, *bounds], tokens):
+            v = gathered(blocks_ref, bounds, at, length)
             resid = fresh_residual(half_u, v, lifted(counts_ref[at : at + valid, :]))
             grad = lax.dot_general(
                 low_u, resid, (((1,), (1,)), ((), ())), preferred_element_type=jnp.float32
@@ -314,22 +323,23 @@
     with jax.named_scope("gather_tokens"):
         own = jnp.pad(v_factor.astype(jnp.bfloat16), ((0, 0), (0, padded - tokens)))
         x, y = ten(own, 1), ten(own, 2)
-        d0, d1 = x[:, : padded // 2], y[:, padded // 2 :]
-        relayed = (d0, d1)
-        blocks = (own, x, y, ten(d0, 2), ten(d1, 1))
+        bounds = (0, padded // 2)
+        relayed = (x[:, : bounds[1]], y[:, bounds[1] :])
 
     with jax.named_scope("gather_tenants"):
         stack = jnp.concatenate([u_factor, u_accum], axis=0)[None]
-        for bit in (1, 2, 4):
+        for bit in (2, 4, 1):
             stack = jnp.concatenate([stack, tok(stack, bit)], axis=0)
-            if bit == 1:
-                staged, vector = stage(turn, by_token, stack)
-            elif bit == 2:
-                stack, vector, _, _ = lax.optimization_barrier((stack, vector, *relayed))
+            if bit == 2:
+                staged, vector = stage(turn, by_token, stack[:1])
+                stack, vector = lax.optimization_barrier((stack, vector))
         factor, accum, half_low = order_tenant(vector, stack)
 
     with jax.named_scope("tenant_grad"):
-        grad = tenant_grad(half_low, blocks, staged)
+        blocks = (own, x, y, ten(relayed[0], 2), ten(relayed[1], 1))
+        spans = [(0, bounds[1]), (bounds[1], padded)]
+        grad = tenant_grad(spans[1], half_low, blocks, bounds, staged, None)
+        grad = tenant_grad(spans[1 - 1], half_low, blocks, bounds, staged, grad)
         grad = (grad + tok(grad, 1)).astype(jnp.bfloat16)
 
     with jax.named_scope("token_grad"):
@@ -337,7 +347,7 @@
         for index, group in enumerate(groups):
             made, add_x, add_y = [], [], []
             for start, size in group:
-                mine, sx, kx, sy, ky, *news = token_grad(start, size, low, step, blocks, staged, after)
+                mine, sx, kx, sy, ky, *news = token_grad(start, size, low, step, blocks, bounds, staged, after)
                 after = ky
                 if step:
                     low, tenant, step = news[:2], (turn, *news[2:]), None

time: 64.3 us -> 63.6 us (0.989)
  waiting for transfers between devices: 15.3 us -> 14.3 us
    ppermute x21, waiting for transfers between devices: 15.3 us -> 14.3 us  [swap(): return lax.ppermute(a, axis, [(i, i ^ bit) for i in range(size)])]
    pallas_call x8 -> x9, Pallas kernels: 18.4 us -> 18.8 us  [call(): pl.pallas_call(kernel, out_shape=out_shape, in_specs=in_specs, compiler_p...]
  transfers between devices with their start and end apart: 21 -> 21, of which waited for: 11 -> 10; matrix products, arithmetic and copies ran while one was open for 1% -> 1% of each run, Pallas kernels for 17% -> 21%
where the time goes in v5:
time: 63.6 us; the launch traced here: 63.3 us
  starting transfers between devices  27.1 us (43%)
  Pallas kernels  18.8 us (30%)
  waiting for transfers between devices  14.3 us (22%)
  other arithmetic  2.18 us (3%)
  between operations  0.81 us (1%)
    ppermute x21, starting transfers between devices, swap(): return lax.ppermute(a, axis, [(i, i ^ bit) for i in range(size)])  27.1 us
    pallas_call x9, Pallas kernels, call(): pl.pallas_call(kernel, out_shape=out_shape, in_specs=in_specs, compiler_p...  18.8 us
    ppermute x21, waiting for transfers between devices, swap(): return lax.ppermute(a, axis, [(i, i ^ bit) for i in range(size)])  14.3 us
    convert_element_type x1, other arithmetic, shards(): own = jnp.pad(v_factor.astype(jnp.bfloat16), ((0, 0), (0, padded - tokens)))  1.27 us
  transfers between devices with their start and end apart: 21, of which 10 were waited for; matrix products, arithmetic and copies ran while one was open for 1% of the time, Pallas kernels for 21%

profile of v5, /device:TPU:0, one launch (start us, length us, event | category | flops | bytes accessed | tf_op | source)
XLA Modules:
  0.0 63.3 jit_solution(16292102289951864431)
XLA Ops:
  0.6 1.3 %convert_element_type.44 = bf16[16,16032]{1,0:T(8,128)(2,1)S(1)} convert(f32[16,16032]{1,0:T(8,128)} %refs_5_.1) | non-fusion elementwise | flops 256512 | bytes 1539072 | tf_op jit(solution)/shard_map/gather_tokens/convert_element_type | solution.py:324
  2.0 3.0 %collective-permute-start.4 = (bf16[16,16128]{1,0:T(8,128)(2,1)S(1)}, bf16[16,16128]{1,0:T(8,128)(2,1)S(1)}, u32[]{:S(2)}, u32[]{:S(2)}) collective-permute-start(bf16[16,16128]{1,0:T(8,128)(2,1)S(1)} %pad.4.own.refs_6_.refs_3_), channel_id=1, source_target_pairs={{0,2},{1,3},{2,0},{3,1},{4,6},{5,7},{6,4},{7,5},{8,10},{9,11},{10,... | collective-permute-start | bytes 1548296 | tf_op jit(solution)/shard_map/gather_tokens/ppermute | solution.py:63
  5.0 1.5 %collective-permute-start.3 = (bf16[16,16128]{1,0:T(8,128)(2,1)S(1)}, bf16[16,16128]{1,0:T(8,128)(2,1)S(1)}, u32[]{:S(2)}, u32[]{:S(2)}) collective-permute-start(bf16[16,16128]{1,0:T(8,128)(2,1)S(1)} %pad.4.own.refs_6_.refs_3_), channel_id=1, source_target_pairs={{0,1},{1,0},{2,3},{3,2},{4,5},{5,4},{6,7},{7,6},{8,9},{9,8},{10,11... | collective-permute-start | bytes 1548296 | tf_op jit(solution)/shard_map/gather_tokens/ppermute | solution.py:63
  7.2 1.6 %collective-permute-start = (f32[1,16,256]{2,1,0:T(8,128)S(1)}, f32[1,16,256]{2,1,0:T(8,128)S(1)}, u32[]{:S(2)}, u32[]{:S(2)}) collective-permute-start(f32[1,16,256]{2,1,0:T(8,128)S(1)} %maximum_bitcast_fusion.after_ref), channel_id=1, source_target_pairs={{0,8},{4,12},{8,0},{12,4},{16,24},{20,28},{24,16},{28,20},{1,9},{5... | collective-permute-start | bytes 49160 | tf_op jit(solution)/shard_map/gather_tenants/ppermute | solution.py:63
  8.8 5.8 %gather_tenants.2 = (s32[16032,256]{1,0:T(8,128)S(1)}, s32[8,256]{1,0:T(8,128)S(1)}) custom-call(s32[1]{0:T(128)} %bitcast.1.turn_ref.refs_10_, s32[16032,256]{1,0:T(8,128)} %bitcast.4, f32[1,16,256]{2,1,0:T(8,128)S(1)} %maximum_bitcast_fusion.after_ref), custom_call_target="tpu_custom_call" | custom-call | bytes 32833536 | tf_op jit(solution)/shard_map/gather_tenants/pallas_call | solution.py:67
  14.6 2.7 %collective-permute-start.1 = (f32[2,16,256]{2,1,0:T(8,128)S(1)}, f32[2,16,256]{2,1,0:T(8,128)S(1)}, u32[]{:S(2)}, u32[]{:S(2)}) collective-permute-start(f32[2,16,256]{2,1,0:T(8,128)S(1)} %pad_maximum_fusion.4), channel_id=1, source_target_pairs={{0,16},{4,20},{8,24},{12,28},{16,0},{20,4},{24,8},{28,12},{1,17},{... | collective-permute-start | bytes 98312 | tf_op jit(solution)/shard_map/gather_tenants/ppermute | solution.py:63
  17.3 1.3 %collective-permute-start.6 = (bf16[16,8064]{1,0:T(8,128)(2,1)S(1)}, bf16[16,8064]{1,0:T(8,128)(2,1)S(1)}, u32[]{:S(2)}, u32[]{:S(2)}) collective-permute-start(bf16[16,8064]{1,0:T(8,128)(2,1)S(1)} %slice.33), channel_id=1, source_target_pairs={{0,1},{1,0},{2,3},{3,2},{4,5},{5,4},{6,7},{7,6},{8,9},{9,8},{10,11... | collective-permute-start | bytes 774152 | tf_op jit(solution)/shard_map/tenant_grad/ppermute | solution.py:63
  18.6 1.6 %collective-permute-start.5 = (bf16[16,8064]{1,0:T(8,128)(2,1)S(1)}, bf16[16,8064]{1,0:T(8,128)(2,1)S(1)}, u32[]{:S(2)}, u32[]{:S(2)}) collective-permute-start(bf16[16,8064]{1,0:T(8,128)(2,1)S(1)} %slice.32), channel_id=1, source_target_pairs={{0,2},{1,3},{2,0},{3,1},{4,6},{5,7},{6,4},{7,5},{8,10},{9,11},{10,... | collective-permute-start | bytes 774152 | tf_op jit(solution)/shard_map/tenant_grad/ppermute | solution.py:63
  20.2 1.2 %collective-permute-done.2 = f32[4,16,256]{2,1,0:T(8,128)S(1)} collective-permute-done((f32[4,16,256]{2,1,0:T(8,128)S(1)}, f32[4,16,256]{2,1,0:T(8,128)S(1)}, u32[]{:S(2)}, u32[]{:S(2)}) %collective-permute-start.2) | collective-permute-done | bytes 65568 | tf_op jit(solution)/shard_map/gather_tenants/ppermute | solution.py:63
  21.5 2.7 %collective-permute-done.6.refs_0_.refs_10_.refs_7_ = bf16[16,8064]{1,0:T(8,128)(2,1)S(1)} collective-permute-done((bf16[16,8064]{1,0:T(8,128)(2,1)S(1)}, bf16[16,8064]{1,0:T(8,128)(2,1)S(1)}, u32[]{:S(2)}, u32[]{:S(2)}) %collective-permute-start.6) | collective-permute-done | bytes 258080 | tf_op jit(solution)/shard_map/tenant_grad/ppermute | solution.py:63
  24.2 2.6 %tenant_grad.2.refs_2_ = f32[64,256]{1,0:T(8,128)S(1)} custom-call(bf16[64,256]{1,0:T(8,128)(2,1)S(1)} %get-tuple-element.41.half_ref, bf16[16,16128]{1,0:T(8,128)(2,1)S(1)} %pad.4.own.refs_6_.refs_3_, bf16[16,16128]{1,0:T(8,128)(2,1)S(1)} %collective-permute-done.3.x.refs_7_.refs_4_, bf16[16,16128]{1,0:T(8,128)(2,1)S(1)} %collective-permute-done.4.y.refs_8_.refs_5_, ...), custom_call_target="tpu_custom_call" | custom-call | bytes 516096 | tf_op jit(solution)/shard_map/tenant_grad/pallas_call | solution.py:67
  26.8 2.7 %tenant_grad.3 = f32[64,256]{1,0:T(8,128)S(1)} custom-call(bf16[64,256]{1,0:T(8,128)(2,1)S(1)} %get-tuple-element.41.half_ref, bf16[16,16128]{1,0:T(8,128)(2,1)S(1)} %pad.4.own.refs_6_.refs_3_, bf16[16,16128]{1,0:T(8,128)(2,1)S(1)} %collective-permute-done.3.x.refs_7_.refs_4_, bf16[16,16128]{1,0:T(8,128)(2,1)S(1)} %collective-permute-done.4.y.refs_8_.refs_5_, ...), custom_call_target="tpu_custom_call" | custom-call | bytes 516096 | tf_op jit(solution)/shard_map/tenant_grad/pallas_call | solution.py:67
  29.6 1.2 %collective-permute-done.7 = f32[64,256]{1,0:T(8,128)S(1)} collective-permute-done((f32[64,256]{1,0:T(8,128)S(1)}, f32[64,256]{1,0:T(8,128)S(1)}, u32[]{:S(2)}, u32[]{:S(2)}) %collective-permute-start.7) | collective-permute-done | bytes 65568 | tf_op jit(solution)/shard_map/tenant_grad/ppermute | solution.py:63
  30.9 3.6 %collective-permute-start.10 = (bf16[64,256]{1,0:T(8,128)(2,1)S(1)}, bf16[64,256]{1,0:T(8,128)(2,1)S(1)}, u32[]{:S(2)}, u32[]{:S(2)}) collective-permute-start(bf16[64,256]{1,0:T(8,128)(2,1)S(1)} %add_convert_fusion.6.refs_0_), channel_id=1, source_target_pairs={{0,24},{4,28},{8,16},{12,20},{16,8},{20,12},{24,0},{28,4},{1,25},{... | collective-permute-start | bytes 98312 | tf_op jit(solution)/shard_map/token_grad/ppermute | solution.py:63
  34.5 0.9 %collective-permute-start.8 = (bf16[64,256]{1,0:T(8,128)(2,1)S(1)}, bf16[64,256]{1,0:T(8,128)(2,1)S(1)}, u32[]{:S(2)}, u32[]{:S(2)}) collective-permute-start(bf16[64,256]{1,0:T(8,128)(2,1)S(1)} %add_convert_fusion.6.refs_0_), channel_id=1, source_target_pairs={{0,8},{4,12},{8,0},{12,4},{16,24},{20,28},{24,16},{28,20},{1,9},{5... | collective-permute-start | bytes 98312 | tf_op jit(solution)/shard_map/token_grad/ppermute | solution.py:63
  35.4 1.3 %collective-permute-done.10.refs_3_ = bf16[64,256]{1,0:T(8,128)(2,1)S(1)} collective-permute-done((bf16[64,256]{1,0:T(8,128)(2,1)S(1)}, bf16[64,256]{1,0:T(8,128)(2,1)S(1)}, u32[]{:S(2)}, u32[]{:S(2)}) %collective-permute-start.10) | collective-permute-done | bytes 32800 | tf_op jit(solution)/shard_map/token_grad/ppermute | solution.py:63
  36.7 2.6 %collective-permute-done.9.refs_2_ = bf16[64,256]{1,0:T(8,128)(2,1)S(1)} collective-permute-done((bf16[64,256]{1,0:T(8,128)(2,1)S(1)}, bf16[64,256]{1,0:T(8,128)(2,1)S(1)}, u32[]{:S(2)}, u32[]{:S(2)}) %collective-permute-start.9) | collective-permute-done | bytes 32800 | tf_op jit(solution)/shard_map/token_grad/ppermute | solution.py:63
  39.3 1.8 %token_grad.5 = (f32[16,5376]{1,0:T(8,128)S(1)}, bf16[32,2688]{1,0:T(8,128)(2,1)S(1)}, f32[16,2688]{1,0:T(8,128)S(1)}, bf16[32,2688]{1,0:T(8,128)(2,1)S(1)}, f32...) custom-call(bf16[64,256]{1,0:T(8,128)(2,1)S(1)} %add_convert_fusion., ...), custom_call_target="tpu_custom_call" | custom-call | bytes 344064 | tf_op jit(solution)/shard_map/token_grad/pallas_call | solution.py:67
  41.1 1.5 %collective-permute-start.11 = (bf16[32,2688]{1,0:T(8,128)(2,1)S(1)}, bf16[32,2688]{1,0:T(8,128)(2,1)S(1)}, u32[]{:S(2)}, u32[]{:S(2)}) collective-permute-start(bf16[32,2688]{1,0:T(8,128)(2,1)S(1)} %get-tuple-element.46), channel_id=1, source_target_pairs={{0,1},{1,0},{2,3},{3,2},{4,5},{5,4},{6,7},{7,6},{8,9},{9,8},{10,11... | collective-permute-start | bytes 516104 | tf_op jit(solution)/shard_map/token_grad/ppermute | solution.py:63
  42.7 1.5 %collective-permute-start.12 = (bf16[32,2688]{1,0:T(8,128)(2,1)S(1)}, bf16[32,2688]{1,0:T(8,128)(2,1)S(1)}, u32[]{:S(2)}, u32[]{:S(2)}) collective-permute-start(bf16[32,2688]{1,0:T(8,128)(2,1)S(1)} %get-tuple-element.47), channel_id=1, source_target_pairs={{0,2},{1,3},{2,0},{3,1},{4,6},{5,7},{6,4},{7,5},{8,10},{9,11},{10,... | collective-permute-start | bytes 516104 | tf_op jit(solution)/shard_map/token_grad/ppermute | solution.py:63
  44.2 1.8 %token_grad.6 = (f32[16,5376]{1,0:T(8,128)S(1)}, bf16[32,2688]{1,0:T(8,128)(2,1)S(1)}, f32[16,2688]{1,0:T(8,128)S(1)}, bf16[32,2688]{1,0:T(8,128)(2,1)S(1)}, f32[16,2688]{1,0:T(8,128)S(1)}) custom-call(f32[16,2688]{1,0:T(8,128)S(1)} %get-tuple-element.48.refs_0_, bf16[64,256]{1,0:T(8,128)(2,1)S(1)} %get-tuple-element.49.refs_1_, ...), custom_call_target="tpu_custom_call" | custom-call | bytes 344064 | tf_op jit(solution)/shard_map/token_grad/pallas_call | solution.py:67
  47.1 1.8 %token_grad.8 = (f32[16,5376]{1,0:T(8,128)S(1)}, bf16[32,2688]{1,0:T(8,128)(2,1)S(1)}, f32[16,2688]{1,0:T(8,128)S(1)}, bf16[32,2688]{1,0:T(8,128)(2,1)S(1)}, f32[16,2688]{1,0:T(8,128)S(1)}) custom-call(f32[16,2688]{1,0:T(8,128)S(1)} %get-tuple-element.56.refs_0_, bf16[64,256]{1,0:T(8,128)(2,1)S(1)} %get-tuple-element.49.refs_1_, ...), custom_call_target="tpu_custom_call" | custom-call | bytes 344064 | tf_op jit(solution)/shard_map/token_grad/pallas_call | solution.py:67
  48.9 1.6 %collective-permute-start.17 = (bf16[32,2688]{1,0:T(8,128)(2,1)S(1)}, bf16[32,2688]{1,0:T(8,128)(2,1)S(1)}, u32[]{:S(2)}, u32[]{:S(2)}) collective-permute-start(bf16[32,2688]{1,0:T(8,128)(2,1)S(1)} %get-tuple-element.62), channel_id=1, source_target_pairs={{0,1},{1,0},{2,3},{3,2},{4,5},{5,4},{6,7},{7,6},{8,9},{9,8},{10,11... | collective-permute-start | bytes 516104 | tf_op jit(solution)/shard_map/token_grad/ppermute | solution.py:63
  50.5 1.5 %collective-permute-start.18 = (bf16[32,2688]{1,0:T(8,128)(2,1)S(1)}, bf16[32,2688]{1,0:T(8,128)(2,1)S(1)}, u32[]{:S(2)}, u32[]{:S(2)}) collective-permute-start(bf16[32,2688]{1,0:T(8,128)(2,1)S(1)} %get-tuple-element.63), channel_id=1, source_target_pairs={{0,2},{1,3},{2,0},{3,1},{4,6},{5,7},{6,4},{7,5},{8,10},{9,11},{10,... | collective-permute-start | bytes 516104 | tf_op jit(solution)/shard_map/token_grad/ppermute | solution.py:63
  52.0 1.3 %collective-permute-done.13.refs_4_ = bf16[32,2688]{1,0:T(8,128)(2,1)S(1)} collective-permute-done((bf16[32,2688]{1,0:T(8,128)(2,1)S(1)}, bf16[32,2688]{1,0:T(8,128)(2,1)S(1)}, u32[]{:S(2)}, u32[]{:S(2)}) %collective-permute-start.13) | collective-permute-done | bytes 172064 | tf_op jit(solution)/shard_map/token_grad/ppermute | solution.py:63
  53.5 1.8 %collective-permute-start.16 = (bf16[16,5376]{1,0:T(8,128)(2,1)S(1)}, bf16[16,5376]{1,0:T(8,128)(2,1)S(1)}, u32[]{:S(2)}, u32[]{:S(2)}) collective-permute-start(bf16[16,5376]{1,0:T(8,128)(2,1)S(1)} %pad_maximum_fusion.1), channel_id=1, source_target_pairs={{0,1},{1,0},{2,3},{3,2},{4,5},{5,4},{6,7},{7,6},{8,9},{9,8},{10,11... | collective-permute-start | bytes 516104 | tf_op jit(solution)/shard_map/token_grad/ppermute | solution.py:63
  55.3 1.6 %collective-permute-done.17.refs_1_ = bf16[32,2688]{1,0:T(8,128)(2,1)S(1)} collective-permute-done((bf16[32,2688]{1,0:T(8,128)(2,1)S(1)}, bf16[32,2688]{1,0:T(8,128)(2,1)S(1)}, u32[]{:S(2)}, u32[]{:S(2)}) %collective-permute-start.17) | collective-permute-done | bytes 172064 | tf_op jit(solution)/shard_map/token_grad/ppermute | solution.py:63
  57.8 1.3 %collective-permute-start.20 = (bf16[16,2688]{1,0:T(8,128)(2,1)S(1)}, bf16[16,2688]{1,0:T(8,128)(2,1)S(1)}, u32[]{:S(2)}, u32[]{:S(2)}) collective-permute-start(bf16[16,2688]{1,0:T(8,128)(2,1)S(1)} %add_convert_fusion), channel_id=1, source_target_pairs={{0,1},{1,0},{2,3},{3,2},{4,5},{5,4},{6,7},{7,6},{8,9},{9,8},{10,11... | collective-permute-start | bytes 258056 | tf_op jit(solution)/shard_map/token_grad/ppermute | solution.py:63
  59.1 1.2 %collective-permute-done.15.refs_6_ = bf16[16,5376]{1,0:T(8,128)(2,1)S(1)} collective-permute-done((bf16[16,5376]{1,0:T(8,128)(2,1)S(1)}, bf16[16,5376]{1,0:T(8,128)(2,1)S(1)}, u32[]{:S(2)}, u32[]{:S(2)}) %collective-permute-start.15) | collective-permute-done | bytes 172064 | tf_op jit(solution)/shard_map/token_grad/ppermute | solution.py:63
  60.3 1.3 %token_grad.7 = (f32[16,16032]{1,0:T(8,128)}, f32[16,16032]{1,0:T(8,128)}, f32[8,256]{1,0:T(8,128)}, f32[8,256]{1,0:T(8,128)}) custom-call(f32[16,5376]{1,0:T(8,128)S(1)} %get-tuple-element.45.refs_0_, bf16[32,2688]{1,0:T(8,128)(2,1)S(1)} %collective-permute-done.11.refs_1_, bf16[32,2688]{1,0:T(8,128)(2,1)S(1)} %collective-permute-done.12.refs_2_, ...), custom_call_target="tpu_custom_call" | custom-call | bytes 2752512 | tf_op jit(solution)/shard_map/token_grad/pallas_call | solution.py:67
  61.6 0.8 %collective-permute-done.20.refs_4_ = bf16[16,2688]{1,0:T(8,128)(2,1)S(1)} collective-permute-done((bf16[16,2688]{1,0:T(8,128)(2,1)S(1)}, bf16[16,2688]{1,0:T(8,128)(2,1)S(1)}, u32[]{:S(2)}, u32[]{:S(2)}) %collective-permute-start.20) | collective-permute-done | bytes 86048 | tf_op jit(solution)/shard_map/token_grad/ppermute | solution.py:63
  62.3 1.0 %token_grad.9 = (f32[16,16032]{1,0:T(8,128)}, f32[16,16032]{1,0:T(8,128)}) custom-call(f32[16,5376]{1,0:T(8,128)S(1)} %get-tuple-element.61.refs_0_, bf16[32,2688]{1,0:T(8,128)(2,1)S(1)} %collective-permute-done.17.refs_1_, bf16[32,2688]{1,0:T(8,128)(2,1)S(1)} %collective-permute-done.18.refs_2_, ...), custom_call_target="tpu_custom_call", output_to_operand_aliasing={{0}: (7, {}), {1}: (8, {})} | custom-call | bytes 2752512 | tf_op jit(solution)/shard_map/token_grad/pallas_call | solution.py:67
  (40 shorter events, 3.1 us)
Async XLA Ops:
  2.0 15.3 %collective-permute-start.4 = (bf16[16,16128]{1,0:T(8,128)(2,1)S(1)}, bf16[16,16128]{1,0:T(8,128)(2,1)S(1)}, u32[]{:S(2)}, u32[]{:S(2)}) collective-permute-start(bf16[16,16128]{1,0:T(8,128)(2,1)S(1)} %pad.4.own.refs_6_.refs_3_), channel_id=1, source_target_pairs={{0,2},{1,3},{2,0},{3,1},{4,6},{5,7},{6,4},{7,5},{8,10},{9,11},{10,... | collective-permute-start | bytes 1548296 | tf_op jit(solution)/shard_map/gather_tokens/ppermute | solution.py:63
  5.0 13.5 %collective-permute-start.3 = (bf16[16,16128]{1,0:T(8,128)(2,1)S(1)}, bf16[16,16128]{1,0:T(8,128)(2,1)S(1)}, u32[]{:S(2)}, u32[]{:S(2)}) collective-permute-start(bf16[16,16128]{1,0:T(8,128)(2,1)S(1)} %pad.4.own.refs_6_.refs_3_), channel_id=1, source_target_pairs={{0,1},{1,0},{2,3},{3,2},{4,5},{5,4},{6,7},{7,6},{8,9},{9,8},{10,11... | collective-permute-start | bytes 1548296 | tf_op jit(solution)/shard_map/gather_tokens/ppermute | solution.py:63
  7.2 7.4 %collective-permute-start = (f32[1,16,256]{2,1,0:T(8,128)S(1)}, f32[1,16,256]{2,1,0:T(8,128)S(1)}, u32[]{:S(2)}, u32[]{:S(2)}) collective-permute-start(f32[1,16,256]{2,1,0:T(8,128)S(1)} %maximum_bitcast_fusion.after_ref), channel_id=1, source_target_pairs={{0,8},{4,12},{8,0},{12,4},{16,24},{20,28},{24,16},{28,20},{1,9},{5... | collective-permute-start | bytes 49160 | tf_op jit(solution)/shard_map/gather_tenants/ppermute | solution.py:63
  14.6 5.6 %collective-permute-start.1 = (f32[2,16,256]{2,1,0:T(8,128)S(1)}, f32[2,16,256]{2,1,0:T(8,128)S(1)}, u32[]{:S(2)}, u32[]{:S(2)}) collective-permute-start(f32[2,16,256]{2,1,0:T(8,128)S(1)} %pad_maximum_fusion.4), channel_id=1, source_target_pairs={{0,16},{4,20},{8,24},{12,28},{16,0},{20,4},{24,8},{28,12},{1,17},{... | collective-permute-start | bytes 98312 | tf_op jit(solution)/shard_map/gather_tenants/ppermute | solution.py:63
  17.3 7.0 %collective-permute-start.6 = (bf16[16,8064]{1,0:T(8,128)(2,1)S(1)}, bf16[16,8064]{1,0:T(8,128)(2,1)S(1)}, u32[]{:S(2)}, u32[]{:S(2)}) collective-permute-start(bf16[16,8064]{1,0:T(8,128)(2,1)S(1)} %slice.33), channel_id=1, source_target_pairs={{0,1},{1,0},{2,3},{3,2},{4,5},{5,4},{6,7},{7,6},{8,9},{9,8},{10,11... | collective-permute-start | bytes 774152 | tf_op jit(solution)/shard_map/tenant_grad/ppermute | solution.py:63
  18.6 8.3 %collective-permute-start.5 = (bf16[16,8064]{1,0:T(8,128)(2,1)S(1)}, bf16[16,8064]{1,0:T(8,128)(2,1)S(1)}, u32[]{:S(2)}, u32[]{:S(2)}) collective-permute-start(bf16[16,8064]{1,0:T(8,128)(2,1)S(1)} %slice.32), channel_id=1, source_target_pairs={{0,2},{1,3},{2,0},{3,1},{4,6},{5,7},{6,4},{7,5},{8,10},{9,11},{10,... | collective-permute-start | bytes 774152 | tf_op jit(solution)/shard_map/tenant_grad/ppermute | solution.py:63
  20.2 1.3 %collective-permute-start.2 = (f32[4,16,256]{2,1,0:T(8,128)S(1)}, f32[4,16,256]{2,1,0:T(8,128)S(1)}, u32[]{:S(2)}, u32[]{:S(2)}) collective-permute-start(f32[4,16,256]{2,1,0:T(8,128)S(1)} %pad_maximum_fusion.3), channel_id=1, source_target_pairs={{0,4},{4,0},{8,12},{12,8},{16,20},{20,16},{24,28},{28,24},{1,5},{5... | collective-permute-start | bytes 196616 | tf_op jit(solution)/shard_map/gather_tenants/ppermute | solution.py:63
  29.6 1.3 %collective-permute-start.7 = (f32[64,256]{1,0:T(8,128)S(1)}, f32[64,256]{1,0:T(8,128)S(1)}, u32[]{:S(2)}, u32[]{:S(2)}) collective-permute-start(f32[64,256]{1,0:T(8,128)S(1)} %tenant_grad.3), channel_id=1, source_target_pairs={{0,4},{4,0},{8,12},{12,8},{16,20},{20,16},{24,28},{28,24},{1,5},{5... | collective-permute-start | bytes 196616 | tf_op jit(solution)/shard_map/tenant_grad/ppermute | solution.py:63
  30.9 5.8 %collective-permute-start.10 = (bf16[64,256]{1,0:T(8,128)(2,1)S(1)}, bf16[64,256]{1,0:T(8,128)(2,1)S(1)}, u32[]{:S(2)}, u32[]{:S(2)}) collective-permute-start(bf16[64,256]{1,0:T(8,128)(2,1)S(1)} %add_convert_fusion.6.refs_0_), channel_id=1, source_target_pairs={{0,24},{4,28},{8,16},{12,20},{16,8},{20,12},{24,0},{28,4},{1,25},{... | collective-permute-start | bytes 98312 | tf_op jit(solution)/shard_map/token_grad/ppermute | solution.py:63
  34.5 4.8 %collective-permute-start.9 = (bf16[64,256]{1,0:T(8,128)(2,1)S(1)}, bf16[64,256]{1,0:T(8,128)(2,1)S(1)}, u32[]{:S(2)}, u32[]{:S(2)}) collective-permute-start(bf16[64,256]{1,0:T(8,128)(2,1)S(1)} %add_convert_fusion.6.refs_0_), channel_id=1, source_target_pairs={{0,16},{4,20},{8,24},{12,28},{16,0},{20,4},{24,8},{28,12},{1,17},{... | collective-permute-start | bytes 98312 | tf_op jit(solution)/shard_map/token_grad/ppermute | solution.py:63
  34.5 4.8 %collective-permute-start.8 = (bf16[64,256]{1,0:T(8,128)(2,1)S(1)}, bf16[64,256]{1,0:T(8,128)(2,1)S(1)}, u32[]{:S(2)}, u32[]{:S(2)}) collective-permute-start(bf16[64,256]{1,0:T(8,128)(2,1)S(1)} %add_convert_fusion.6.refs_0_), channel_id=1, source_target_pairs={{0,8},{4,12},{8,0},{12,4},{16,24},{20,28},{24,16},{28,20},{1,9},{5... | collective-permute-start | bytes 98312 | tf_op jit(solution)/shard_map/token_grad/ppermute | solution.py:63
  41.1 9.3 %collective-permute-start.11 = (bf16[32,2688]{1,0:T(8,128)(2,1)S(1)}, bf16[32,2688]{1,0:T(8,128)(2,1)S(1)}, u32[]{:S(2)}, u32[]{:S(2)}) collective-permute-start(bf16[32,2688]{1,0:T(8,128)(2,1)S(1)} %get-tuple-element.46), channel_id=1, source_target_pairs={{0,1},{1,0},{2,3},{3,2},{4,5},{5,4},{6,7},{7,6},{8,9},{9,8},{10,11... | collective-permute-start | bytes 516104 | tf_op jit(solution)/shard_map/token_grad/ppermute | solution.py:63
  42.7 10.8 %collective-permute-start.12 = (bf16[32,2688]{1,0:T(8,128)(2,1)S(1)}, bf16[32,2688]{1,0:T(8,128)(2,1)S(1)}, u32[]{:S(2)}, u32[]{:S(2)}) collective-permute-start(bf16[32,2688]{1,0:T(8,128)(2,1)S(1)} %get-tuple-element.47), channel_id=1, source_target_pairs={{0,2},{1,3},{2,0},{3,1},{4,6},{5,7},{6,4},{7,5},{8,10},{9,11},{10,... | collective-permute-start | bytes 516104 | tf_op jit(solution)/shard_map/token_grad/ppermute | solution.py:63
  44.2 16.1 %copy-start = (f32[16,16032]{1,0:T(8,128)S(1)}, f32[16,16032]{1,0:T(8,128)}, u32[]{:S(2)}) copy-start(f32[16,16032]{1,0:T(8,128)} %refs_5_.1) | copy-start | bytes 3078148
  44.2 16.1 %copy-start.1 = (f32[16,16032]{1,0:T(8,128)S(1)}, f32[16,16032]{1,0:T(8,128)}, u32[]{:S(2)}) copy-start(f32[16,16032]{1,0:T(8,128)} %refs_6_.1) | copy-start | bytes 3078148
  46.0 7.3 %collective-permute-start.13 = (bf16[32,2688]{1,0:T(8,128)(2,1)S(1)}, bf16[32,2688]{1,0:T(8,128)(2,1)S(1)}, u32[]{:S(2)}, u32[]{:S(2)}) collective-permute-start(bf16[32,2688]{1,0:T(8,128)(2,1)S(1)} %get-tuple-element.52), channel_id=1, source_target_pairs={{0,1},{1,0},{2,3},{3,2},{4,5},{5,4},{6,7},{7,6},{8,9},{9,8},{10,11... | collective-permute-start | bytes 516104 | tf_op jit(solution)/shard_map/token_grad/ppermute | solution.py:63
  46.6 6.9 %collective-permute-start.14 = (bf16[32,2688]{1,0:T(8,128)(2,1)S(1)}, bf16[32,2688]{1,0:T(8,128)(2,1)S(1)}, u32[]{:S(2)}, u32[]{:S(2)}) collective-permute-start(bf16[32,2688]{1,0:T(8,128)(2,1)S(1)} %get-tuple-element.53), channel_id=1, source_target_pairs={{0,2},{1,3},{2,0},{3,1},{4,6},{5,7},{6,4},{7,5},{8,10},{9,11},{10,... | collective-permute-start | bytes 516104 | tf_op jit(solution)/shard_map/token_grad/ppermute | solution.py:63
  48.9 8.1 %collective-permute-start.17 = (bf16[32,2688]{1,0:T(8,128)(2,1)S(1)}, bf16[32,2688]{1,0:T(8,128)(2,1)S(1)}, u32[]{:S(2)}, u32[]{:S(2)}) collective-permute-start(bf16[32,2688]{1,0:T(8,128)(2,1)S(1)} %get-tuple-element.62), channel_id=1, source_target_pairs={{0,1},{1,0},{2,3},{3,2},{4,5},{5,4},{6,7},{7,6},{8,9},{9,8},{10,11... | collective-permute-start | bytes 516104 | tf_op jit(solution)/shard_map/token_grad/ppermute | solution.py:63
  50.5 7.3 %collective-permute-start.18 = (bf16[32,2688]{1,0:T(8,128)(2,1)S(1)}, bf16[32,2688]{1,0:T(8,128)(2,1)S(1)}, u32[]{:S(2)}, u32[]{:S(2)}) collective-permute-start(bf16[32,2688]{1,0:T(8,128)(2,1)S(1)} %get-tuple-element.63), channel_id=1, source_target_pairs={{0,2},{1,3},{2,0},{3,1},{4,6},{5,7},{6,4},{7,5},{8,10},{9,11},{10,... | collective-permute-start | bytes 516104 | tf_op jit(solution)/shard_map/token_grad/ppermute | solution.py:63
  53.3 6.9 %collective-permute-start.15 = (bf16[16,5376]{1,0:T(8,128)(2,1)S(1)}, bf16[16,5376]{1,0:T(8,128)(2,1)S(1)}, u32[]{:S(2)}, u32[]{:S(2)}) collective-permute-start(bf16[16,5376]{1,0:T(8,128)(2,1)S(1)} %pad_maximum_fusion), channel_id=1, source_target_pairs={{0,2},{1,3},{2,0},{3,1},{4,6},{5,7},{6,4},{7,5},{8,10},{9,11},{10,... | collective-permute-start | bytes 516104 | tf_op jit(solution)/shard_map/token_grad/ppermute | solution.py:63
  53.5 6.8 %collective-permute-start.16 = (bf16[16,5376]{1,0:T(8,128)(2,1)S(1)}, bf16[16,5376]{1,0:T(8,128)(2,1)S(1)}, u32[]{:S(2)}, u32[]{:S(2)}) collective-permute-start(bf16[16,5376]{1,0:T(8,128)(2,1)S(1)} %pad_maximum_fusion.1), channel_id=1, source_target_pairs={{0,1},{1,0},{2,3},{3,2},{4,5},{5,4},{6,7},{7,6},{8,9},{9,8},{10,11... | collective-permute-start | bytes 516104 | tf_op jit(solution)/shard_map/token_grad/ppermute | solution.py:63
  57.0 4.6 %collective-permute-start.19 = (bf16[16,2688]{1,0:T(8,128)(2,1)S(1)}, bf16[16,2688]{1,0:T(8,128)(2,1)S(1)}, u32[]{:S(2)}, u32[]{:S(2)}) collective-permute-start(bf16[16,2688]{1,0:T(8,128)(2,1)S(1)} %add_convert_fusion.1), channel_id=1, source_target_pairs={{0,2},{1,3},{2,0},{3,1},{4,6},{5,7},{6,4},{7,5},{8,10},{9,11},{10,... | collective-permute-start | bytes 258056 | tf_op jit(solution)/shard_map/token_grad/ppermute | solution.py:63
  57.8 4.6 %collective-permute-start.20 = (bf16[16,2688]{1,0:T(8,128)(2,1)S(1)}, bf16[16,2688]{1,0:T(8,128)(2,1)S(1)}, u32[]{:S(2)}, u32[]{:S(2)}) collective-permute-start(bf16[16,2688]{1,0:T(8,128)(2,1)S(1)} %add_convert_fusion), channel_id=1, source_target_pairs={{0,1},{1,0},{2,3},{3,2},{4,5},{5,4},{6,7},{7,6},{8,9},{9,8},{10,11... | collective-permute-start | bytes 258056 | tf_op jit(solution)/shard_map/token_grad/ppermute | solution.py:63

commit v6 on v5

--- a/solution.py
+++ b/solution.py
@@ -323,7 +323,7 @@
     with jax.named_scope("gather_tokens"):
         own = jnp.pad(v_factor.astype(jnp.bfloat16), ((0, 0), (0, padded - tokens)))
         x, y = ten(own, 1), ten(own, 2)
-        bounds = (0, padded // 2)
+        bounds = (0, 8576)
         relayed = (x[:, : bounds[1]], y[:, bounds[1] :])
 
     with jax.named_scope("gather_tenants"):

time: 63.6 us -> 63.4 us (level)
  no operation moved by 1% of the time
where the time goes in v6:
time: 63.4 us; the launch traced here: 63.1 us
  starting transfers between devices  27.1 us (43%)
  Pallas kernels  19 us (30%)
  waiting for transfers between devices  14 us (22%)
  other arithmetic  2.17 us (3%)
  between operations  0.82 us (1%)
    ppermute x21, starting transfers between devices, swap(): return lax.ppermute(a, axis, [(i, i ^ bit) for i in range(size)])  27.1 us
    pallas_call x9, Pallas kernels, call(): pl.pallas_call(kernel, out_shape=out_shape, in_specs=in_specs, compiler_p...  19 us
    ppermute x21, waiting for transfers between devices, swap(): return lax.ppermute(a, axis, [(i, i ^ bit) for i in range(size)])  14 us
    convert_element_type x1, other arithmetic, shards(): own = jnp.pad(v_factor.astype(jnp.bfloat16), ((0, 0), (0, padded - tokens)))  1.27 us
  transfers between devices with their start and end apart: 21, of which 10 were waited for; matrix products, arithmetic and copies ran while one was open for 1% of the time, Pallas kernels for 21%

profile of v6, /device:TPU:0, one launch (start us, length us, event | category | flops | bytes accessed | tf_op | source)
XLA Modules:
  0.0 63.1 jit_solution(14835013650870783220)
XLA Ops:
  0.6 1.3 %convert_element_type.44 = bf16[16,16032]{1,0:T(8,128)(2,1)S(1)} convert(f32[16,16032]{1,0:T(8,128)} %refs_5_.1) | non-fusion elementwise | flops 256512 | bytes 1539072 | tf_op jit(solution)/shard_map/gather_tokens/convert_element_type | solution.py:324
  2.0 3.0 %collective-permute-start.4 = (bf16[16,16128]{1,0:T(8,128)(2,1)S(1)}, bf16[16,16128]{1,0:T(8,128)(2,1)S(1)}, u32[]{:S(2)}, u32[]{:S(2)}) collective-permute-start(bf16[16,16128]{1,0:T(8,128)(2,1)S(1)} %pad.4.own.refs_6_.refs_3_), channel_id=1, source_target_pairs={{0,2},{1,3},{2,0},{3,1},{4,6},{5,7},{6,4},{7,5},{8,10},{9,11},{10,... | collective-permute-start | bytes 1548296 | tf_op jit(solution)/shard_map/gather_tokens/ppermute | solution.py:63
  5.0 1.5 %collective-permute-start.3 = (bf16[16,16128]{1,0:T(8,128)(2,1)S(1)}, bf16[16,16128]{1,0:T(8,128)(2,1)S(1)}, u32[]{:S(2)}, u32[]{:S(2)}) collective-permute-start(bf16[16,16128]{1,0:T(8,128)(2,1)S(1)} %pad.4.own.refs_6_.refs_3_), channel_id=1, source_target_pairs={{0,1},{1,0},{2,3},{3,2},{4,5},{5,4},{6,7},{7,6},{8,9},{9,8},{10,11... | collective-permute-start | bytes 1548296 | tf_op jit(solution)/shard_map/gather_tokens/ppermute | solution.py:63
  7.2 1.6 %collective-permute-start = (f32[1,16,256]{2,1,0:T(8,128)S(1)}, f32[1,16,256]{2,1,0:T(8,128)S(1)}, u32[]{:S(2)}, u32[]{:S(2)}) collective-permute-start(f32[1,16,256]{2,1,0:T(8,128)S(1)} %maximum_bitcast_fusion.after_ref), channel_id=1, source_target_pairs={{0,8},{4,12},{8,0},{12,4},{16,24},{20,28},{24,16},{28,20},{1,9},{5... | collective-permute-start | bytes 49160 | tf_op jit(solution)/shard_map/gather_tenants/ppermute | solution.py:63
  8.8 5.8 %gather_tenants.2 = (s32[16032,256]{1,0:T(8,128)S(1)}, s32[8,256]{1,0:T(8,128)S(1)}) custom-call(s32[1]{0:T(128)} %bitcast.1.turn_ref.refs_10_, s32[16032,256]{1,0:T(8,128)} %bitcast.4, f32[1,16,256]{2,1,0:T(8,128)S(1)} %maximum_bitcast_fusion.after_ref), custom_call_target="tpu_custom_call" | custom-call | bytes 32833536 | tf_op jit(solution)/shard_map/gather_tenants/pallas_call | solution.py:67
  14.6 2.7 %collective-permute-start.1 = (f32[2,16,256]{2,1,0:T(8,128)S(1)}, f32[2,16,256]{2,1,0:T(8,128)S(1)}, u32[]{:S(2)}, u32[]{:S(2)}) collective-permute-start(f32[2,16,256]{2,1,0:T(8,128)S(1)} %pad_maximum_fusion.4), channel_id=1, source_target_pairs={{0,16},{4,20},{8,24},{12,28},{16,0},{20,4},{24,8},{28,12},{1,17},{... | collective-permute-start | bytes 98312 | tf_op jit(solution)/shard_map/gather_tenants/ppermute | solution.py:63
  17.3 1.3 %collective-permute-start.6 = (bf16[16,7552]{1,0:T(8,128)(2,1)S(1)}, bf16[16,7552]{1,0:T(8,128)(2,1)S(1)}, u32[]{:S(2)}, u32[]{:S(2)}) collective-permute-start(bf16[16,7552]{1,0:T(8,128)(2,1)S(1)} %slice.33), channel_id=1, source_target_pairs={{0,1},{1,0},{2,3},{3,2},{4,5},{5,4},{6,7},{7,6},{8,9},{9,8},{10,11... | collective-permute-start | bytes 725000 | tf_op jit(solution)/shard_map/tenant_grad/ppermute | solution.py:63
  18.6 1.6 %collective-permute-start.5 = (bf16[16,8576]{1,0:T(8,128)(2,1)S(1)}, bf16[16,8576]{1,0:T(8,128)(2,1)S(1)}, u32[]{:S(2)}, u32[]{:S(2)}) collective-permute-start(bf16[16,8576]{1,0:T(8,128)(2,1)S(1)} %slice.32), channel_id=1, source_target_pairs={{0,2},{1,3},{2,0},{3,1},{4,6},{5,7},{6,4},{7,5},{8,10},{9,11},{10,... | collective-permute-start | bytes 823304 | tf_op jit(solution)/shard_map/tenant_grad/ppermute | solution.py:63
  20.2 1.2 %collective-permute-done.2 = f32[4,16,256]{2,1,0:T(8,128)S(1)} collective-permute-done((f32[4,16,256]{2,1,0:T(8,128)S(1)}, f32[4,16,256]{2,1,0:T(8,128)S(1)}, u32[]{:S(2)}, u32[]{:S(2)}) %collective-permute-start.2) | collective-permute-done | bytes 65568 | tf_op jit(solution)/shard_map/gather_tenants/ppermute | solution.py:63
  21.5 2.3 %collective-permute-done.6.refs_0_.refs_10_.refs_7_ = bf16[16,7552]{1,0:T(8,128)(2,1)S(1)} collective-permute-done((bf16[16,7552]{1,0:T(8,128)(2,1)S(1)}, bf16[16,7552]{1,0:T(8,128)(2,1)S(1)}, u32[]{:S(2)}, u32[]{:S(2)}) %collective-permute-start.6) | collective-permute-done | bytes 241696 | tf_op jit(solution)/shard_map/tenant_grad/ppermute | solution.py:63
  23.9 2.5 %tenant_grad.2.refs_2_ = f32[64,256]{1,0:T(8,128)S(1)} custom-call(bf16[64,256]{1,0:T(8,128)(2,1)S(1)} %get-tuple-element.41.half_ref, bf16[16,16128]{1,0:T(8,128)(2,1)S(1)} %pad.4.own.refs_6_.refs_3_, bf16[16,16128]{1,0:T(8,128)(2,1)S(1)} %collective-permute-done.3.x.refs_7_.refs_4_, bf16[16,16128]{1,0:T(8,128)(2,1)S(1)} %collective-permute-done.4.y.refs_8_.refs_5_, ...), custom_call_target="tpu_custom_call" | custom-call | bytes 483328 | tf_op jit(solution)/shard_map/tenant_grad/pallas_call | solution.py:67
  26.4 2.9 %tenant_grad.3 = f32[64,256]{1,0:T(8,128)S(1)} custom-call(bf16[64,256]{1,0:T(8,128)(2,1)S(1)} %get-tuple-element.41.half_ref, bf16[16,16128]{1,0:T(8,128)(2,1)S(1)} %pad.4.own.refs_6_.refs_3_, bf16[16,16128]{1,0:T(8,128)(2,1)S(1)} %collective-permute-done.3.x.refs_7_.refs_4_, bf16[16,16128]{1,0:T(8,128)(2,1)S(1)} %collective-permute-done.4.y.refs_8_.refs_5_, ...), custom_call_target="tpu_custom_call" | custom-call | bytes 548864 | tf_op jit(solution)/shard_map/tenant_grad/pallas_call | solution.py:67
  29.4 1.2 %collective-permute-done.7 = f32[64,256]{1,0:T(8,128)S(1)} collective-permute-done((f32[64,256]{1,0:T(8,128)S(1)}, f32[64,256]{1,0:T(8,128)S(1)}, u32[]{:S(2)}, u32[]{:S(2)}) %collective-permute-start.7) | collective-permute-done | bytes 65568 | tf_op jit(solution)/shard_map/tenant_grad/ppermute | solution.py:63
  30.7 3.6 %collective-permute-start.10 = (bf16[64,256]{1,0:T(8,128)(2,1)S(1)}, bf16[64,256]{1,0:T(8,128)(2,1)S(1)}, u32[]{:S(2)}, u32[]{:S(2)}) collective-permute-start(bf16[64,256]{1,0:T(8,128)(2,1)S(1)} %add_convert_fusion.6.refs_0_), channel_id=1, source_target_pairs={{0,24},{4,28},{8,16},{12,20},{16,8},{20,12},{24,0},{28,4},{1,25},{... | collective-permute-start | bytes 98312 | tf_op jit(solution)/shard_map/token_grad/ppermute | solution.py:63
  34.2 0.9 %collective-permute-start.8 = (bf16[64,256]{1,0:T(8,128)(2,1)S(1)}, bf16[64,256]{1,0:T(8,128)(2,1)S(1)}, u32[]{:S(2)}, u32[]{:S(2)}) collective-permute-start(bf16[64,256]{1,0:T(8,128)(2,1)S(1)} %add_convert_fusion.6.refs_0_), channel_id=1, source_target_pairs={{0,8},{4,12},{8,0},{12,4},{16,24},{20,28},{24,16},{28,20},{1,9},{5... | collective-permute-start | bytes 98312 | tf_op jit(solution)/shard_map/token_grad/ppermute | solution.py:63
  35.1 1.3 %collective-permute-done.10.refs_3_ = bf16[64,256]{1,0:T(8,128)(2,1)S(1)} collective-permute-done((bf16[64,256]{1,0:T(8,128)(2,1)S(1)}, bf16[64,256]{1,0:T(8,128)(2,1)S(1)}, u32[]{:S(2)}, u32[]{:S(2)}) %collective-permute-start.10) | collective-permute-done | bytes 32800 | tf_op jit(solution)/shard_map/token_grad/ppermute | solution.py:63
  36.4 2.6 %collective-permute-done.9.refs_2_ = bf16[64,256]{1,0:T(8,128)(2,1)S(1)} collective-permute-done((bf16[64,256]{1,0:T(8,128)(2,1)S(1)}, bf16[64,256]{1,0:T(8,128)(2,1)S(1)}, u32[]{:S(2)}, u32[]{:S(2)}) %collective-permute-start.9) | collective-permute-done | bytes 32800 | tf_op jit(solution)/shard_map/token_grad/ppermute | solution.py:63
  39.0 1.8 %token_grad.5 = (f32[16,5376]{1,0:T(8,128)S(1)}, bf16[32,2688]{1,0:T(8,128)(2,1)S(1)}, f32[16,2688]{1,0:T(8,128)S(1)}, bf16[32,2688]{1,0:T(8,128)(2,1)S(1)}, f32...) custom-call(bf16[64,256]{1,0:T(8,128)(2,1)S(1)} %add_convert_fusion., ...), custom_call_target="tpu_custom_call" | custom-call | bytes 344064 | tf_op jit(solution)/shard_map/token_grad/pallas_call | solution.py:67
  40.9 1.6 %collective-permute-start.11 = (bf16[32,2688]{1,0:T(8,128)(2,1)S(1)}, bf16[32,2688]{1,0:T(8,128)(2,1)S(1)}, u32[]{:S(2)}, u32[]{:S(2)}) collective-permute-start(bf16[32,2688]{1,0:T(8,128)(2,1)S(1)} %get-tuple-element.46), channel_id=1, source_target_pairs={{0,1},{1,0},{2,3},{3,2},{4,5},{5,4},{6,7},{7,6},{8,9},{9,8},{10,11... | collective-permute-start | bytes 516104 | tf_op jit(solution)/shard_map/token_grad/ppermute | solution.py:63
  42.4 1.5 %collective-permute-start.12 = (bf16[32,2688]{1,0:T(8,128)(2,1)S(1)}, bf16[32,2688]{1,0:T(8,128)(2,1)S(1)}, u32[]{:S(2)}, u32[]{:S(2)}) collective-permute-start(bf16[32,2688]{1,0:T(8,128)(2,1)S(1)} %get-tuple-element.47), channel_id=1, source_target_pairs={{0,2},{1,3},{2,0},{3,1},{4,6},{5,7},{6,4},{7,5},{8,10},{9,11},{10,... | collective-permute-start | bytes 516104 | tf_op jit(solution)/shard_map/token_grad/ppermute | solution.py:63
  44.0 1.8 %token_grad.6 = (f32[16,5376]{1,0:T(8,128)S(1)}, bf16[32,2688]{1,0:T(8,128)(2,1)S(1)}, f32[16,2688]{1,0:T(8,128)S(1)}, bf16[32,2688]{1,0:T(8,128)(2,1)S(1)}, f32[16,2688]{1,0:T(8,128)S(1)}) custom-call(f32[16,2688]{1,0:T(8,128)S(1)} %get-tuple-element.48.refs_0_, bf16[64,256]{1,0:T(8,128)(2,1)S(1)} %get-tuple-element.49.refs_1_, ...), custom_call_target="tpu_custom_call" | custom-call | bytes 344064 | tf_op jit(solution)/shard_map/token_grad/pallas_call | solution.py:67
  46.9 1.8 %token_grad.8 = (f32[16,5376]{1,0:T(8,128)S(1)}, bf16[32,2688]{1,0:T(8,128)(2,1)S(1)}, f32[16,2688]{1,0:T(8,128)S(1)}, bf16[32,2688]{1,0:T(8,128)(2,1)S(1)}, f32[16,2688]{1,0:T(8,128)S(1)}) custom-call(f32[16,2688]{1,0:T(8,128)S(1)} %get-tuple-element.56.refs_0_, bf16[64,256]{1,0:T(8,128)(2,1)S(1)} %get-tuple-element.49.refs_1_, ...), custom_call_target="tpu_custom_call" | custom-call | bytes 344064 | tf_op jit(solution)/shard_map/token_grad/pallas_call | solution.py:67
  48.7 1.6 %collective-permute-start.17 = (bf16[32,2688]{1,0:T(8,128)(2,1)S(1)}, bf16[32,2688]{1,0:T(8,128)(2,1)S(1)}, u32[]{:S(2)}, u32[]{:S(2)}) collective-permute-start(bf16[32,2688]{1,0:T(8,128)(2,1)S(1)} %get-tuple-element.62), channel_id=1, source_target_pairs={{0,1},{1,0},{2,3},{3,2},{4,5},{5,4},{6,7},{7,6},{8,9},{9,8},{10,11... | collective-permute-start | bytes 516104 | tf_op jit(solution)/shard_map/token_grad/ppermute | solution.py:63
  50.2 1.5 %collective-permute-start.18 = (bf16[32,2688]{1,0:T(8,128)(2,1)S(1)}, bf16[32,2688]{1,0:T(8,128)(2,1)S(1)}, u32[]{:S(2)}, u32[]{:S(2)}) collective-permute-start(bf16[32,2688]{1,0:T(8,128)(2,1)S(1)} %get-tuple-element.63), channel_id=1, source_target_pairs={{0,2},{1,3},{2,0},{3,1},{4,6},{5,7},{6,4},{7,5},{8,10},{9,11},{10,... | collective-permute-start | bytes 516104 | tf_op jit(solution)/shard_map/token_grad/ppermute | solution.py:63
  51.8 1.3 %collective-permute-done.13.refs_4_ = bf16[32,2688]{1,0:T(8,128)(2,1)S(1)} collective-permute-done((bf16[32,2688]{1,0:T(8,128)(2,1)S(1)}, bf16[32,2688]{1,0:T(8,128)(2,1)S(1)}, u32[]{:S(2)}, u32[]{:S(2)}) %collective-permute-start.13) | collective-permute-done | bytes 172064 | tf_op jit(solution)/shard_map/token_grad/ppermute | solution.py:63
  53.3 1.8 %collective-permute-start.16 = (bf16[16,5376]{1,0:T(8,128)(2,1)S(1)}, bf16[16,5376]{1,0:T(8,128)(2,1)S(1)}, u32[]{:S(2)}, u32[]{:S(2)}) collective-permute-start(bf16[16,5376]{1,0:T(8,128)(2,1)S(1)} %pad_maximum_fusion.1), channel_id=1, source_target_pairs={{0,1},{1,0},{2,3},{3,2},{4,5},{5,4},{6,7},{7,6},{8,9},{9,8},{10,11... | collective-permute-start | bytes 516104 | tf_op jit(solution)/shard_map/token_grad/ppermute | solution.py:63
  55.1 1.6 %collective-permute-done.17.refs_1_ = bf16[32,2688]{1,0:T(8,128)(2,1)S(1)} collective-permute-done((bf16[32,2688]{1,0:T(8,128)(2,1)S(1)}, bf16[32,2688]{1,0:T(8,128)(2,1)S(1)}, u32[]{:S(2)}, u32[]{:S(2)}) %collective-permute-start.17) | collective-permute-done | bytes 172064 | tf_op jit(solution)/shard_map/token_grad/ppermute | solution.py:63
  57.6 1.3 %collective-permute-start.20 = (bf16[16,2688]{1,0:T(8,128)(2,1)S(1)}, bf16[16,2688]{1,0:T(8,128)(2,1)S(1)}, u32[]{:S(2)}, u32[]{:S(2)}) collective-permute-start(bf16[16,2688]{1,0:T(8,128)(2,1)S(1)} %add_convert_fusion), channel_id=1, source_target_pairs={{0,1},{1,0},{2,3},{3,2},{4,5},{5,4},{6,7},{7,6},{8,9},{9,8},{10,11... | collective-permute-start | bytes 258056 | tf_op jit(solution)/shard_map/token_grad/ppermute | solution.py:63
  58.8 1.2 %collective-permute-done.15.refs_6_ = bf16[16,5376]{1,0:T(8,128)(2,1)S(1)} collective-permute-done((bf16[16,5376]{1,0:T(8,128)(2,1)S(1)}, bf16[16,5376]{1,0:T(8,128)(2,1)S(1)}, u32[]{:S(2)}, u32[]{:S(2)}) %collective-permute-start.15) | collective-permute-done | bytes 172064 | tf_op jit(solution)/shard_map/token_grad/ppermute | solution.py:63
  60.1 1.3 %token_grad.7 = (f32[16,16032]{1,0:T(8,128)}, f32[16,16032]{1,0:T(8,128)}, f32[8,256]{1,0:T(8,128)}, f32[8,256]{1,0:T(8,128)}) custom-call(f32[16,5376]{1,0:T(8,128)S(1)} %get-tuple-element.45.refs_0_, bf16[32,2688]{1,0:T(8,128)(2,1)S(1)} %collective-permute-done.11.refs_1_, bf16[32,2688]{1,0:T(8,128)(2,1)S(1)} %collective-permute-done.12.refs_2_, ...), custom_call_target="tpu_custom_call" | custom-call | bytes 2752512 | tf_op jit(solution)/shard_map/token_grad/pallas_call | solution.py:67
  61.4 0.8 %collective-permute-done.20.refs_4_ = bf16[16,2688]{1,0:T(8,128)(2,1)S(1)} collective-permute-done((bf16[16,2688]{1,0:T(8,128)(2,1)S(1)}, bf16[16,2688]{1,0:T(8,128)(2,1)S(1)}, u32[]{:S(2)}, u32[]{:S(2)}) %collective-permute-start.20) | collective-permute-done | bytes 86048 | tf_op jit(solution)/shard_map/token_grad/ppermute | solution.py:63
  62.1 1.0 %token_grad.9 = (f32[16,16032]{1,0:T(8,128)}, f32[16,16032]{1,0:T(8,128)}) custom-call(f32[16,5376]{1,0:T(8,128)S(1)} %get-tuple-element.61.refs_0_, bf16[32,2688]{1,0:T(8,128)(2,1)S(1)} %collective-permute-done.17.refs_1_, bf16[32,2688]{1,0:T(8,128)(2,1)S(1)} %collective-permute-done.18.refs_2_, ...), custom_call_target="tpu_custom_call", output_to_operand_aliasing={{0}: (7, {}), {1}: (8, {})} | custom-call | bytes 2752512 | tf_op jit(solution)/shard_map/token_grad/pallas_call | solution.py:67
  (40 shorter events, 3.1 us)
Async XLA Ops:
  2.0 15.3 %collective-permute-start.4 = (bf16[16,16128]{1,0:T(8,128)(2,1)S(1)}, bf16[16,16128]{1,0:T(8,128)(2,1)S(1)}, u32[]{:S(2)}, u32[]{:S(2)}) collective-permute-start(bf16[16,16128]{1,0:T(8,128)(2,1)S(1)} %pad.4.own.refs_6_.refs_3_), channel_id=1, source_target_pairs={{0,2},{1,3},{2,0},{3,1},{4,6},{5,7},{6,4},{7,5},{8,10},{9,11},{10,... | collective-permute-start | bytes 1548296 | tf_op jit(solution)/shard_map/gather_tokens/ppermute | solution.py:63
  5.0 13.5 %collective-permute-start.3 = (bf16[16,16128]{1,0:T(8,128)(2,1)S(1)}, bf16[16,16128]{1,0:T(8,128)(2,1)S(1)}, u32[]{:S(2)}, u32[]{:S(2)}) collective-permute-start(bf16[16,16128]{1,0:T(8,128)(2,1)S(1)} %pad.4.own.refs_6_.refs_3_), channel_id=1, source_target_pairs={{0,1},{1,0},{2,3},{3,2},{4,5},{5,4},{6,7},{7,6},{8,9},{9,8},{10,11... | collective-permute-start | bytes 1548296 | tf_op jit(solution)/shard_map/gather_tokens/ppermute | solution.py:63
  7.2 7.4 %collective-permute-start = (f32[1,16,256]{2,1,0:T(8,128)S(1)}, f32[1,16,256]{2,1,0:T(8,128)S(1)}, u32[]{:S(2)}, u32[]{:S(2)}) collective-permute-start(f32[1,16,256]{2,1,0:T(8,128)S(1)} %maximum_bitcast_fusion.after_ref), channel_id=1, source_target_pairs={{0,8},{4,12},{8,0},{12,4},{16,24},{20,28},{24,16},{28,20},{1,9},{5... | collective-permute-start | bytes 49160 | tf_op jit(solution)/shard_map/gather_tenants/ppermute | solution.py:63
  14.6 5.6 %collective-permute-start.1 = (f32[2,16,256]{2,1,0:T(8,128)S(1)}, f32[2,16,256]{2,1,0:T(8,128)S(1)}, u32[]{:S(2)}, u32[]{:S(2)}) collective-permute-start(f32[2,16,256]{2,1,0:T(8,128)S(1)} %pad_maximum_fusion.4), channel_id=1, source_target_pairs={{0,16},{4,20},{8,24},{12,28},{16,0},{20,4},{24,8},{28,12},{1,17},{... | collective-permute-start | bytes 98312 | tf_op jit(solution)/shard_map/gather_tenants/ppermute | solution.py:63
  17.3 6.6 %collective-permute-start.6 = (bf16[16,7552]{1,0:T(8,128)(2,1)S(1)}, bf16[16,7552]{1,0:T(8,128)(2,1)S(1)}, u32[]{:S(2)}, u32[]{:S(2)}) collective-permute-start(bf16[16,7552]{1,0:T(8,128)(2,1)S(1)} %slice.33), channel_id=1, source_target_pairs={{0,1},{1,0},{2,3},{3,2},{4,5},{5,4},{6,7},{7,6},{8,9},{9,8},{10,11... | collective-permute-start | bytes 725000 | tf_op jit(solution)/shard_map/tenant_grad/ppermute | solution.py:63
  18.6 7.9 %collective-permute-start.5 = (bf16[16,8576]{1,0:T(8,128)(2,1)S(1)}, bf16[16,8576]{1,0:T(8,128)(2,1)S(1)}, u32[]{:S(2)}, u32[]{:S(2)}) collective-permute-start(bf16[16,8576]{1,0:T(8,128)(2,1)S(1)} %slice.32), channel_id=1, source_target_pairs={{0,2},{1,3},{2,0},{3,1},{4,6},{5,7},{6,4},{7,5},{8,10},{9,11},{10,... | collective-permute-start | bytes 823304 | tf_op jit(solution)/shard_map/tenant_grad/ppermute | solution.py:63
  20.2 1.3 %collective-permute-start.2 = (f32[4,16,256]{2,1,0:T(8,128)S(1)}, f32[4,16,256]{2,1,0:T(8,128)S(1)}, u32[]{:S(2)}, u32[]{:S(2)}) collective-permute-start(f32[4,16,256]{2,1,0:T(8,128)S(1)} %pad_maximum_fusion.3), channel_id=1, source_target_pairs={{0,4},{4,0},{8,12},{12,8},{16,20},{20,16},{24,28},{28,24},{1,5},{5... | collective-permute-start | bytes 196616 | tf_op jit(solution)/shard_map/gather_tenants/ppermute | solution.py:63
  29.3 1.3 %collective-permute-start.7 = (f32[64,256]{1,0:T(8,128)S(1)}, f32[64,256]{1,0:T(8,128)S(1)}, u32[]{:S(2)}, u32[]{:S(2)}) collective-permute-start(f32[64,256]{1,0:T(8,128)S(1)} %tenant_grad.3), channel_id=1, source_target_pairs={{0,4},{4,0},{8,12},{12,8},{16,20},{20,16},{24,28},{28,24},{1,5},{5... | collective-permute-start | bytes 196616 | tf_op jit(solution)/shard_map/tenant_grad/ppermute | solution.py:63
  30.7 5.8 %collective-permute-start.10 = (bf16[64,256]{1,0:T(8,128)(2,1)S(1)}, bf16[64,256]{1,0:T(8,128)(2,1)S(1)}, u32[]{:S(2)}, u32[]{:S(2)}) collective-permute-start(bf16[64,256]{1,0:T(8,128)(2,1)S(1)} %add_convert_fusion.6.refs_0_), channel_id=1, source_target_pairs={{0,24},{4,28},{8,16},{12,20},{16,8},{20,12},{24,0},{28,4},{1,25},{... | collective-permute-start | bytes 98312 | tf_op jit(solution)/shard_map/token_grad/ppermute | solution.py:63
  34.2 4.8 %collective-permute-start.9 = (bf16[64,256]{1,0:T(8,128)(2,1)S(1)}, bf16[64,256]{1,0:T(8,128)(2,1)S(1)}, u32[]{:S(2)}, u32[]{:S(2)}) collective-permute-start(bf16[64,256]{1,0:T(8,128)(2,1)S(1)} %add_convert_fusion.6.refs_0_), channel_id=1, source_target_pairs={{0,16},{4,20},{8,24},{12,28},{16,0},{20,4},{24,8},{28,12},{1,17},{... | collective-permute-start | bytes 98312 | tf_op jit(solution)/shard_map/token_grad/ppermute | solution.py:63
  34.2 4.8 %collective-permute-start.8 = (bf16[64,256]{1,0:T(8,128)(2,1)S(1)}, bf16[64,256]{1,0:T(8,128)(2,1)S(1)}, u32[]{:S(2)}, u32[]{:S(2)}) collective-permute-start(bf16[64,256]{1,0:T(8,128)(2,1)S(1)} %add_convert_fusion.6.refs_0_), channel_id=1, source_target_pairs={{0,8},{4,12},{8,0},{12,4},{16,24},{20,28},{24,16},{28,20},{1,9},{5... | collective-permute-start | bytes 98312 | tf_op jit(solution)/shard_map/token_grad/ppermute | solution.py:63
  40.9 9.4 %collective-permute-start.11 = (bf16[32,2688]{1,0:T(8,128)(2,1)S(1)}, bf16[32,2688]{1,0:T(8,128)(2,1)S(1)}, u32[]{:S(2)}, u32[]{:S(2)}) collective-permute-start(bf16[32,2688]{1,0:T(8,128)(2,1)S(1)} %get-tuple-element.46), channel_id=1, source_target_pairs={{0,1},{1,0},{2,3},{3,2},{4,5},{5,4},{6,7},{7,6},{8,9},{9,8},{10,11... | collective-permute-start | bytes 516104 | tf_op jit(solution)/shard_map/token_grad/ppermute | solution.py:63
  42.4 10.8 %collective-permute-start.12 = (bf16[32,2688]{1,0:T(8,128)(2,1)S(1)}, bf16[32,2688]{1,0:T(8,128)(2,1)S(1)}, u32[]{:S(2)}, u32[]{:S(2)}) collective-permute-start(bf16[32,2688]{1,0:T(8,128)(2,1)S(1)} %get-tuple-element.47), channel_id=1, source_target_pairs={{0,2},{1,3},{2,0},{3,1},{4,6},{5,7},{6,4},{7,5},{8,10},{9,11},{10,... | collective-permute-start | bytes 516104 | tf_op jit(solution)/shard_map/token_grad/ppermute | solution.py:63
  44.0 16.1 %copy-start = (f32[16,16032]{1,0:T(8,128)S(1)}, f32[16,16032]{1,0:T(8,128)}, u32[]{:S(2)}) copy-start(f32[16,16032]{1,0:T(8,128)} %refs_5_.1) | copy-start | bytes 3078148
  44.0 16.1 %copy-start.1 = (f32[16,16032]{1,0:T(8,128)S(1)}, f32[16,16032]{1,0:T(8,128)}, u32[]{:S(2)}) copy-start(f32[16,16032]{1,0:T(8,128)} %refs_6_.1) | copy-start | bytes 3078148
  45.8 7.3 %collective-permute-start.13 = (bf16[32,2688]{1,0:T(8,128)(2,1)S(1)}, bf16[32,2688]{1,0:T(8,128)(2,1)S(1)}, u32[]{:S(2)}, u32[]{:S(2)}) collective-permute-start(bf16[32,2688]{1,0:T(8,128)(2,1)S(1)} %get-tuple-element.52), channel_id=1, source_target_pairs={{0,1},{1,0},{2,3},{3,2},{4,5},{5,4},{6,7},{7,6},{8,9},{9,8},{10,11... | collective-permute-start | bytes 516104 | tf_op jit(solution)/shard_map/token_grad/ppermute | solution.py:63
  46.4 6.9 %collective-permute-start.14 = (bf16[32,2688]{1,0:T(8,128)(2,1)S(1)}, bf16[32,2688]{1,0:T(8,128)(2,1)S(1)}, u32[]{:S(2)}, u32[]{:S(2)}) collective-permute-start(bf16[32,2688]{1,0:T(8,128)(2,1)S(1)} %get-tuple-element.53), channel_id=1, source_target_pairs={{0,2},{1,3},{2,0},{3,1},{4,6},{5,7},{6,4},{7,5},{8,10},{9,11},{10,... | collective-permute-start | bytes 516104 | tf_op jit(solution)/shard_map/token_grad/ppermute | solution.py:63
  48.7 8.1 %collective-permute-start.17 = (bf16[32,2688]{1,0:T(8,128)(2,1)S(1)}, bf16[32,2688]{1,0:T(8,128)(2,1)S(1)}, u32[]{:S(2)}, u32[]{:S(2)}) collective-permute-start(bf16[32,2688]{1,0:T(8,128)(2,1)S(1)} %get-tuple-element.62), channel_id=1, source_target_pairs={{0,1},{1,0},{2,3},{3,2},{4,5},{5,4},{6,7},{7,6},{8,9},{9,8},{10,11... | collective-permute-start | bytes 516104 | tf_op jit(solution)/shard_map/token_grad/ppermute | solution.py:63
  50.2 7.3 %collective-permute-start.18 = (bf16[32,2688]{1,0:T(8,128)(2,1)S(1)}, bf16[32,2688]{1,0:T(8,128)(2,1)S(1)}, u32[]{:S(2)}, u32[]{:S(2)}) collective-permute-start(bf16[32,2688]{1,0:T(8,128)(2,1)S(1)} %get-tuple-element.63), channel_id=1, source_target_pairs={{0,2},{1,3},{2,0},{3,1},{4,6},{5,7},{6,4},{7,5},{8,10},{9,11},{10,... | collective-permute-start | bytes 516104 | tf_op jit(solution)/shard_map/token_grad/ppermute | solution.py:63
  53.1 6.9 %collective-permute-start.15 = (bf16[16,5376]{1,0:T(8,128)(2,1)S(1)}, bf16[16,5376]{1,0:T(8,128)(2,1)S(1)}, u32[]{:S(2)}, u32[]{:S(2)}) collective-permute-start(bf16[16,5376]{1,0:T(8,128)(2,1)S(1)} %pad_maximum_fusion), channel_id=1, source_target_pairs={{0,2},{1,3},{2,0},{3,1},{4,6},{5,7},{6,4},{7,5},{8,10},{9,11},{10,... | collective-permute-start | bytes 516104 | tf_op jit(solution)/shard_map/token_grad/ppermute | solution.py:63
  53.3 6.8 %collective-permute-start.16 = (bf16[16,5376]{1,0:T(8,128)(2,1)S(1)}, bf16[16,5376]{1,0:T(8,128)(2,1)S(1)}, u32[]{:S(2)}, u32[]{:S(2)}) collective-permute-start(bf16[16,5376]{1,0:T(8,128)(2,1)S(1)} %pad_maximum_fusion.1), channel_id=1, source_target_pairs={{0,1},{1,0},{2,3},{3,2},{4,5},{5,4},{6,7},{7,6},{8,9},{9,8},{10,11... | collective-permute-start | bytes 516104 | tf_op jit(solution)/shard_map/token_grad/ppermute | solution.py:63
  56.8 4.6 %collective-permute-start.19 = (bf16[16,2688]{1,0:T(8,128)(2,1)S(1)}, bf16[16,2688]{1,0:T(8,128)(2,1)S(1)}, u32[]{:S(2)}, u32[]{:S(2)}) collective-permute-start(bf16[16,2688]{1,0:T(8,128)(2,1)S(1)} %add_convert_fusion.1), channel_id=1, source_target_pairs={{0,2},{1,3},{2,0},{3,1},{4,6},{5,7},{6,4},{7,5},{8,10},{9,11},{10,... | collective-permute-start | bytes 258056 | tf_op jit(solution)/shard_map/token_grad/ppermute | solution.py:63
  57.6 4.6 %collective-permute-start.20 = (bf16[16,2688]{1,0:T(8,128)(2,1)S(1)}, bf16[16,2688]{1,0:T(8,128)(2,1)S(1)}, u32[]{:S(2)}, u32[]{:S(2)}) collective-permute-start(bf16[16,2688]{1,0:T(8,128)(2,1)S(1)} %add_convert_fusion), channel_id=1, source_target_pairs={{0,1},{1,0},{2,3},{3,2},{4,5},{5,4},{6,7},{7,6},{8,9},{9,8},{10,11... | collective-permute-start | bytes 258056 | tf_op jit(solution)/shard_map/token_grad/ppermute | solution.py:63
